TPU v7x, 32 devices: a whole 2x2x4 slice. The times are simulated.
32 devices in a mesh: row: 8 (over z, y), col: 4 (over x, core).
Axes of the slice: x: 2, y: 2, z: 4, core: 2. Of those that a mesh axis runs over, the one named last changes fastest.
Arguments:
- center: bfloat16 [512, 8192], P('col', 'row'), may hold values from -6 to 6
- radius: bfloat16 [512, 8192], P('col', 'row'), may hold values from 0.049804688 to 1
- grad_center: bfloat16 [512, 8192], P('row', 'col'), may hold values from -6 to 6
- grad_radius: bfloat16 [512, 8192], P('row', 'col'), may hold values from -6 to 6
- weight: bfloat16 [8192, 8192], P('row', 'col'), may hold values from -0.0625 to 0.0625
- active: int32 [512, 8192], P('col', 'row'), may hold values 0 or 1
Outputs:
- center_in: float32 [512, 8192], P('col', 'row')
- radius_in: float32 [512, 8192], P('col', 'row')
- weight_grad: float32 [8192, 8192], P('row', 'col')
All inputs are finite; a program needn't handle non-finite values. No bound on the sum of `active` on one device may be relied on, other than what follows from the above.
Results may differ from a plain program's by a relative error of at most 0.0003.
Values may be sent and summed in bfloat16 or wider, within the bound.
No kernel may reach another device: no remote copies, remote signals or barrier semaphores. Data moves between devices by JAX's collectives and lax.ppermute only.
A program may use at most 64 MiB of HBM per device.

v0:
```python
import jax
import jax.numpy as jnp
from jax import lax
from jax.sharding import PartitionSpec as P


def on_device(center, radius, grad_center, grad_radius, weight, active):
    magnitude = jnp.abs(weight)
    stacked = jnp.stack((grad_center, grad_radius))
    inputs = lax.all_gather(jnp.stack((center, radius)), "col", axis=1, tiled=True)
    contract_out = (((1,), (1,)), ((), ()))
    contract_tok = (((0,), (0,)), ((), ()))
    total_tokens = inputs.shape[1]
    panels = lax.all_gather(stacked, "row", axis=1, tiled=True)
    through_center = lax.dot_general(
        panels[0], weight, contract_out, preferred_element_type=jnp.float32
    )
    through_radius = lax.dot_general(
        panels[1], magnitude, contract_out, preferred_element_type=jnp.float32
    )
    partial_terms = jnp.stack((through_center, through_radius))
    center_acc = lax.dot_general(
        inputs[0], panels[0], contract_tok, preferred_element_type=jnp.float32
    )
    radius_acc = lax.dot_general(
        inputs[1], panels[1], contract_tok, preferred_element_type=jnp.float32
    )
    center_acc, radius_acc = (center_acc, radius_acc)
    summed = lax.psum_scatter(partial_terms, "col", scatter_dimension=1, tiled=True)
    gating = active.astype(jnp.float32)
    center_in = gating * summed[0]
    radius_in = gating * summed[1]
    scale_factor = jnp.float32(1.0) / jnp.sqrt(jnp.float32(total_tokens))
    weight_grad = (center_acc + jnp.sign(weight).astype(jnp.float32) * radius_acc) * scale_factor
    return (center_in, radius_in, weight_grad)


def solution(mesh):
    in_specs = (
        P("col", "row"),
        P("col", "row"),
        P("row", "col"),
        P("row", "col"),
        P("row", "col"),
        P("col", "row"),
    )
    out_specs = (P("col", "row"), P("col", "row"), P("row", "col"))
    return jax.shard_map(
        on_device, mesh=mesh, in_specs=in_specs, out_specs=out_specs, check_vma=False
    )
```

profile of v0, /device:TPU:0, one launch (start us, length us, event | category | flops | bytes accessed | tf_op | source)
XLA Modules:
  0.0 165.8 jit_solution(12259911058662007890)
XLA Ops:
  7.2 0.0 all-gather.3.cloned.1.call-start
  7.2 1.9 %pad_maximum_fusion.1 = bf16[2,64,2048]{2,1,0:T(8,128)(2,1)} fusion(bf16[1,64,2048]{2,1,0:T(8,128)(2,1)} %bitcast.35, bf16[1,64,2048]{2,1,0:T(8,128)(2,1)} %bitcast.36), kind=kLoop, calls=%fused_computation.16 | loop fusion | flops 262144 | bytes 1048576 | tf_op jit(solution)/shard_map/stack | solution.py:9
  9.1 0.0 all-gather.3.cloned.1.call-update
  9.1 0.0 all-gather.5.cloned.1.call-start
  9.2 1.9 %pad_maximum_fusion.2 = bf16[2,128,1024]{2,1,0:T(8,128)(2,1)} fusion(bf16[1,128,1024]{2,1,0:T(8,128)(2,1)} %bitcast.37, bf16[1,128,1024]{2,1,0:T(8,128)(2,1)} %bitcast.38), kind=kLoop, calls=%fused_computation.17 | loop fusion | flops 262144 | bytes 1048576 | tf_op jit(solution)/shard_map/stack | solution.py:10
  11.0 0.0 all-gather.5.cloned.1.call-update
  11.1 0.0 reduce-scatter.2.cloned.1.call-start
  11.1 75.8 %all-gather.3.cloned.1.call-done = bf16[2,512,2048]{2,1,0:T(8,128)(2,1)} async-done(((bf16[2,64,2048]{2,1,0:T(8,128)(2,1)}), bf16[2,512,2048]{2,1,0:T(8,128)(2,1)}) %all-gather.3.cloned.1.call-update) | async-done | bytes 4194320 | tf_op jit(solution)/shard_map/all_gather | solution.py:14
  86.9 0.0 copy-start
  86.9 0.0 copy-start.3
  86.9 5.3 %fusion.5 = f32[1,512,1024]{2,1,0:T(8,128)S(1)} fusion(bf16[1024,2048]{1,0:T(8,128)(2,1)} %param.10, bf16[2,512,2048]{2,1,0:T(8,128)(2,1)} %all-gather.3.cloned.1.call-done), kind=kOutput, calls=%fused_computation.9 | convolution fusion | flops 2149580800 | bytes 8388608 | tf_op jit(solution)/shard_map/dot_general | solution.py:18
  92.2 0.0 copy-done
  92.2 0.0 copy-done.3
  92.2 2.4 %fusion.4 = f32[1,512,1024]{2,1,0:T(8,128)S(1)} fusion(bf16[1024,2048]{1,0:T(8,128)(2,1)S(1)} %copy-done, bf16[2,512,2048]{2,1,0:T(8,128)(2,1)S(1)} %copy-done.3), kind=kOutput, calls=%fused_computation.8 | convolution fusion | flops 2147483648 | bytes 8388608 | tf_op jit(solution)/shard_map/dot_general | solution.py:15
  94.6 2.6 %pad_maximum_fusion = f32[2,512,1024]{2,1,0:T(8,128)} fusion(f32[1,512,1024]{2,1,0:T(8,128)S(1)} %fusion.5, f32[1,512,1024]{2,1,0:T(8,128)S(1)} %fusion.4), kind=kLoop, calls=%fused_computation.1 | loop fusion | flops 1048576 | bytes 8388608 | tf_op jit(solution)/shard_map/stack | solution.py:21
  97.2 0.0 reduce-scatter.2.cloned.1.call-update
  97.2 12.7 %all-gather.5.cloned.1.call-done = bf16[2,512,1024]{2,1,0:T(8,128)(2,1)} async-done(((bf16[2,128,1024]{2,1,0:T(8,128)(2,1)}), bf16[2,512,1024]{2,1,0:T(8,128)(2,1)}) %all-gather.5.cloned.1.call-update) | async-done | bytes 2097168 | tf_op jit(solution)/shard_map/all_gather | solution.py:10
  109.9 0.0 copy-start.1
  109.9 0.0 copy-start.2
  109.9 0.0 copy-start.4
  109.9 4.5 %fusion.2 = f32[1024,2048]{1,0:T(8,128)S(1)} fusion(bf16[2,512,2048]{2,1,0:T(8,128)(2,1)} %all-gather.3.cloned.1.call-done, bf16[2,512,1024]{2,1,0:T(8,128)(2,1)} %all-gather.5.cloned.1.call-done), kind=kOutput, calls=%fused_computation.6 | convolution fusion | flops 2147483648 | bytes 11534336 | tf_op jit(solution)/shard_map/dot_general | solution.py:22
  114.4 0.0 copy-done.1
  114.4 0.0 copy-done.2
  114.4 0.5 copy-done.4
  114.9 0.0 copy-start.5
  114.9 8.7 %add_multiply_fusion = f32[1024,2048]{1,0:T(8,128)} fusion(f32[1024,2048]{1,0:T(8,128)S(1)} %fusion.2, bf16[1024,2048]{1,0:T(8,128)(2,1)S(1)} %copy-done.1, bf16[2,512,2048]{2,1,0:T(8,128)(2,1)S(1)} %copy-done.4, bf16[2,512,1024]{2,1,0:T(8,128)(2,1)S(1)} %copy-done.2), kind=kOutput, calls=%fused_computation | convolution fusion | flops 2157969408 | bytes 24117248 | tf_op jit(solution)/shard_map/dot_general | solution.py:25
  123.6 33.4 %reduce-scatter.2.cloned.1.call-done = f32[2,128,1024]{2,1,0:T(8,128)} async-done(((f32[2,512,1024]{2,1,0:T(8,128)}), f32[2,128,1024]{2,1,0:T(8,128)}) %reduce-scatter.2.cloned.1.call-update) | async-done | bytes 1048592 | tf_op jit(solution)/shard_map/reduce_scatter | solution.py:29
  157.0 0.0 copy-done.5
  157.0 2.3 %fusion.8 = (f32[128,1024]{1,0:T(8,128)}, f32[128,1024]{1,0:T(8,128)}) fusion(f32[2,128,1024]{2,1,0:T(8,128)} %reduce-scatter.2.cloned.1.call-done, s32[128,1024]{1,0:T(8,128)S(1)} %copy-done.5), kind=kLoop, calls=%fused_computation.13 | loop fusion | flops 393216 | bytes 2621440 | tf_op jit(solution)/shard_map/mul | solution.py:32
Async XLA Ops:
  7.2 79.7 %all-gather.3.cloned.1.call-start = ((), (), s32[]{:S(2)}) async-start(), calls=%async_computation.1 | async-start | bytes 4718592 | tf_op jit(solution)/shard_map/all_gather | solution.py:14
  9.1 100.8 %all-gather.5.cloned.1.call-start = ((), (), s32[]{:S(2)}) async-start(), calls=%async_computation.3 | async-start | bytes 2621440 | tf_op jit(solution)/shard_map/all_gather | solution.py:10
  11.1 145.9 %reduce-scatter.2.cloned.1.call-start = ((), (), s32[]{:S(2)}) async-start(), calls=%async_computation.2 | async-start | bytes 5242880 | tf_op jit(solution)/shard_map/reduce_scatter | solution.py:29
  86.9 5.3 %copy-start = (bf16[1024,2048]{1,0:T(8,128)(2,1)S(1)}, bf16[1024,2048]{1,0:T(8,128)(2,1)}, u32[]{:S(2)}) copy-start(bf16[1024,2048]{1,0:T(8,128)(2,1)} %param.10) | copy-start | bytes 12582916
  86.9 5.4 %copy-start.3 = (bf16[2,512,2048]{2,1,0:T(8,128)(2,1)S(1)}, bf16[2,512,2048]{2,1,0:T(8,128)(2,1)}, u32[]{:S(2)}) copy-start(bf16[2,512,2048]{2,1,0:T(8,128)(2,1)} %all-gather.3.cloned.1.call-done) | copy-start | bytes 12582916
  109.9 4.5 %copy-start.1 = (bf16[1024,2048]{1,0:T(8,128)(2,1)S(1)}, bf16[1024,2048]{1,0:T(8,128)(2,1)}, u32[]{:S(2)}) copy-start(bf16[1024,2048]{1,0:T(8,128)(2,1)} %param.10) | copy-start | bytes 12582916
  109.9 4.5 %copy-start.2 = (bf16[2,512,1024]{2,1,0:T(8,128)(2,1)S(1)}, bf16[2,512,1024]{2,1,0:T(8,128)(2,1)}, u32[]{:S(2)}) copy-start(bf16[2,512,1024]{2,1,0:T(8,128)(2,1)} %all-gather.5.cloned.1.call-done) | copy-start | bytes 6291460
  109.9 5.0 %copy-start.4 = (bf16[2,512,2048]{2,1,0:T(8,128)(2,1)S(1)}, bf16[2,512,2048]{2,1,0:T(8,128)(2,1)}, u32[]{:S(2)}) copy-start(bf16[2,512,2048]{2,1,0:T(8,128)(2,1)} %all-gather.3.cloned.1.call-done) | copy-start | bytes 12582916
  114.9 42.1 %copy-start.5 = (s32[128,1024]{1,0:T(8,128)S(1)}, s32[128,1024]{1,0:T(8,128)}, u32[]{:S(2)}) copy-start(s32[128,1024]{1,0:T(8,128)} %param.11) | copy-start | bytes 1572868
Sparse Core Ops, SparseCore 0:
  10.8 76.0 all-gather.2
  89.0 20.8 all-gather.4
  112.4 44.4 reduce-scatter.1
where the time goes:
time: 166 us
  waiting for transfers between devices  122 us (73%)
  matrix products  20.9 us (13%)
  between operations  13.8 us (8%)
  other arithmetic  8.6 us (5%)
    all_gather x1, waiting for transfers between devices, on_device(): panels = lax.all_gather(stacked, 'row', axis=1, tiled=True)  75.8 us
    reduce_scatter x1, waiting for transfers between devices, on_device(): lax.psum_scatter(partial_terms, 'col', scatter_dimension=1, tiled=True)  33.4 us
    all_gather x1, waiting for transfers between devices, on_device(): lax.all_gather(jnp.stack((center, radius)), 'col', axis=1, tiled=True)  12.7 us
    dot_general x1, matrix products, on_device(): lax.dot_general(inputs[1], panels[1], contract_tok, preferred_element_typ...  8.69 us
    dot_general x1, matrix products, on_device(): lax.dot_general(panels[1], magnitude, contract_out, preferred_element_typ...  5.33 us
    dot_general x1, matrix products, on_device(): lax.dot_general(inputs[0], panels[0], contract_tok, preferred_element_typ...  4.47 us
  transfers between devices with their start and end apart: 3, of which 3 were waited for; matrix products, arithmetic and copies ran while one was open for 15% of the time, Pallas kernels for 0%

commit v1 on v0

v1 whole, which is shorter than its diff:
```python
import functools

import jax
import jax.numpy as jnp
import numpy as np
from jax import lax
from jax.experimental import pallas as pl
from jax.experimental.pallas import tpu as pltpu
from jax.sharding import PartitionSpec as P

VMEM_LIMIT = 24 * 1024 * 1024
VMEM_ALL = 60 * 1024 * 1024
VMEM_MOST = 48 * 1024 * 1024
HERE = pl.BlockSpec(memory_space=pltpu.VMEM)
LANES = 128
LEVELS = np.float32(32000)
TINY = np.float32(2.0**-100)
ANYWHERE = pl.BlockSpec(memory_space=pl.ANY)
BY_LAST = (((1,), (1,)), ((), ()))
BY_TOKEN = (((1,), (0,)), ((), ()))


def ring_of(rows):
    if rows % 2:
        return list(range(rows))
    return list(range(0, rows, 2)) + list(range(rows - 1, 0, -2))


def on_ring(row, rows):
    return row if rows % 2 else lax.select(lax.rem(row, 2) == 0, lax.div(row, 2), rows - 1 - lax.div(row, 2))


def off_ring(place, rows):
    return place if rows % 2 else lax.select(place < rows // 2, 2 * place, 2 * (rows - place) - 1)


def col_split(cols):
    return (cols // 2, 2) if cols % 2 == 0 else (cols, 1)


def place(rows, cols, owned, shifts, slots, half, held, order):
    chips, cores = col_split(cols)
    here, col = on_ring(lax.axis_index("row"), rows), lax.axis_index("col")
    x, core = lax.div(col, cores), lax.rem(col, cores)
    share = owned // held
    for shift, slot in zip(shifts, slots):
        first = half * held if slot.shape[0] > held else 0
        source = off_ring(lax.rem(here + (rows - shift) % rows, rows), rows)
        owner = lax.div(source, share)
        away = lax.rem(lax.rem(owner, cores) + cores - core, cores)
        near = away * chips + lax.rem(lax.div(owner, cores) + chips - x, chips)
        start = pl.multiple_of((near * share + lax.rem(source, share)) * held, held)
        order[pl.ds(start, held), :] = slot[first : first + held, :]


def input_kernel(rows, cols, shifts, absolute, *refs):
    count, pieces = len(shifts), cols
    slots, weight, outs, order = refs[:count], refs[count], refs[count + 1 : -1], refs[-1]
    inner = weight.shape[0]
    tile = min(256, inner)
    step = order.shape[0] // pieces
    place(rows, cols, step, shifts, slots, int(absolute), order.shape[0] // rows, order)
    for i in range(inner // tile):
        span = slice(i * tile, (i + 1) * tile)
        block = weight[span, :]
        if absolute:
            block = jnp.abs(block)
        terms = lax.dot_general(order[...], block, BY_LAST, preferred_element_type=jnp.float32)
        for n in range(pieces):
            outs[n][:, span] = terms[n * step : (n + 1) * step, :]


def input_terms(rows, cols, shifts, slots, weight, absolute):
    inner, width = weight.shape
    tokens = slots[0].shape[0] // 2 * rows
    found = pl.pallas_call(
        functools.partial(input_kernel, rows, cols, shifts, absolute),
        in_specs=[HERE] * (len(slots) + 1),
        out_specs=[HERE] * (cols + 1),
        out_shape=[jax.ShapeDtypeStruct((tokens // cols, inner), jnp.float32)] * cols
        + [jax.ShapeDtypeStruct((tokens, width), jnp.bfloat16)],
        compiler_params=pltpu.CompilerParams(vmem_limit_bytes=VMEM_LIMIT),
        cost_estimate=pl.CostEstimate(
            flops=2 * tokens * inner * width,
            bytes_accessed=2 * (tokens + inner) * width + 4 * tokens * inner,
            transcendentals=0,
        ),
    )(*slots, weight)
    return found[:cols], found[cols]


def load_kernel(source, target, sem):
    copy = pltpu.make_async_copy(source, target, sem)
    copy.start()
    copy.wait()


def loaded(value):
    return pl.pallas_call(
        load_kernel,
        in_specs=[ANYWHERE],
        out_specs=HERE,
        out_shape=jax.ShapeDtypeStruct(value.shape, value.dtype),
        scratch_shapes=[pltpu.SemaphoreType.DMA],
        compiler_params=pltpu.CompilerParams(vmem_limit_bytes=VMEM_MOST),
        cost_estimate=pl.CostEstimate(flops=0, bytes_accessed=4 * value.size, transcendentals=0),
    )(value)


def sum_kernel(count, *refs):
    parts, out = refs[:count], refs[count]
    total = parts[0][...]
    for part in parts[1:]:
        total = total + part[...]
    rows, width = total.shape
    most = jnp.max(jnp.abs(total), axis=1, keepdims=True)
    exponent = jnp.ceil(jnp.log2(jnp.maximum(most, TINY)) + 1e-3)
    coded = jnp.round(total * (LEVELS / jnp.exp2(exponent)))
    out[:, :width] = coded.astype(jnp.int16)
    out[:, width:] = jnp.broadcast_to(exponent, (rows, LANES)).astype(jnp.int16)


def coded_sum(*parts):
    rows, width = parts[0].shape
    return pl.pallas_call(
        functools.partial(sum_kernel, len(parts)),
        in_specs=[HERE] * len(parts),
        out_specs=HERE,
        out_shape=jax.ShapeDtypeStruct((rows, width + LANES), jnp.int16),
        compiler_params=pltpu.CompilerParams(vmem_limit_bytes=VMEM_LIMIT),
        cost_estimate=pl.CostEstimate(
            flops=4 * rows * width, bytes_accessed=10 * rows * width, transcendentals=rows
        ),
    )(*parts)


def gate_kernel(near, far, *refs):
    active, out = refs[-2:]
    width = out.shape[1]
    total = refs[0][...]
    for part in refs[1:near]:
        total = total + part[...]
    for part in refs[near : near + far]:
        exponent = part[:, width : width + 1].astype(jnp.float32)
        total = total + part[:, :width].astype(jnp.float32) * (jnp.exp2(exponent) / LEVELS)
    out[...] = active[...].astype(jnp.float32) * total


def gated(near, far, active):
    rows, width = active.shape
    return pl.pallas_call(
        functools.partial(gate_kernel, len(near), len(far)),
        in_specs=[HERE] * (len(near) + len(far) + 1),
        out_specs=HERE,
        out_shape=jax.ShapeDtypeStruct((rows, width), jnp.float32),
        compiler_params=pltpu.CompilerParams(vmem_limit_bytes=VMEM_LIMIT),
        cost_estimate=pl.CostEstimate(
            flops=8 * rows * width, bytes_accessed=20 * rows * width, transcendentals=rows
        ),
    )(*near, *far, active)


def pack_kernel(first, second, out, both, sems):
    rows = first.shape[0]
    spans = [pl.ds(0, rows), pl.ds(rows, rows)]
    copies = [
        pltpu.make_async_copy(source, both.at[span, :], sem)
        for source, span, sem in zip((first, second), spans, (sems.at[0], sems.at[1]))
    ]
    onward = [
        pltpu.make_async_copy(both.at[span, :], out.at[span, :], sem)
        for span, sem in zip(spans, (sems.at[2], sems.at[3]))
    ]
    for copy in copies:
        copy.start()
    for copy, then in zip(copies, onward):
        copy.wait()
        then.start()
    for then in onward:
        then.wait()


def packed(first, second):
    rows, width = first.shape
    return pl.pallas_call(
        pack_kernel,
        in_specs=[ANYWHERE] * 2,
        out_specs=ANYWHERE,
        out_shape=jax.ShapeDtypeStruct((2 * rows, width), first.dtype),
        scratch_shapes=[pltpu.VMEM((2 * rows, width), first.dtype), pltpu.SemaphoreType.DMA((4,))],
        compiler_params=pltpu.CompilerParams(vmem_limit_bytes=VMEM_ALL),
        cost_estimate=pl.CostEstimate(flops=0, bytes_accessed=8 * rows * width, transcendentals=0),
    )(first, second)


def turn_kernel(pieces, *refs):
    held, turned = refs[:-2], refs[-2:]
    rows = held[0].shape[0] // pieces
    tokens = 0
    for ref in held:
        for n in range(0, pieces, 2):
            for half, out in enumerate(turned):
                out[:, tokens : tokens + rows] = ref[(n + half) * rows : (n + half + 1) * rows, :].T
            tokens += rows


def turned(held, pieces):
    rows, inner = held[0].shape
    tokens = rows // 2 * len(held)
    return pl.pallas_call(
        functools.partial(turn_kernel, pieces),
        in_specs=[HERE] * len(held),
        out_specs=[HERE] * 2,
        out_shape=[jax.ShapeDtypeStruct((inner, tokens), jnp.bfloat16)] * 2,
        compiler_params=pltpu.CompilerParams(vmem_limit_bytes=VMEM_LIMIT),
        cost_estimate=pl.CostEstimate(
            flops=2 * tokens * inner, bytes_accessed=8 * tokens * inner, transcendentals=0
        ),
    )(*held)


def center_kernel(center, grads, out):
    tile = min(256, out.shape[0])

    @pl.loop(0, out.shape[0] // tile)
    def _(i):
        span = pl.ds(pl.multiple_of(i * tile, tile), tile)
        out[span, :] = lax.dot_general(
            center[span, :], grads[...], BY_TOKEN, preferred_element_type=jnp.float32
        )


def center_terms(center, grads):
    inner, tokens = center.shape
    width = grads.shape[1]
    return pl.pallas_call(
        center_kernel,
        in_specs=[HERE] * 2,
        out_specs=HERE,
        out_shape=jax.ShapeDtypeStruct((inner, width), jnp.float32),
        compiler_params=pltpu.CompilerParams(vmem_limit_bytes=VMEM_LIMIT),
        cost_estimate=pl.CostEstimate(
            flops=2 * tokens * inner * width,
            bytes_accessed=2 * tokens * (inner + width) + 4 * inner * width,
            transcendentals=0,
        ),
    )(center, grads)


def weight_kernel(scale, center, radius, grads, weight, out, parts, sems):
    tile = parts.shape[1]
    copies = []
    for n in range(out.shape[0] // tile):
        span = slice(n * tile, (n + 1) * tile)
        part, sem = parts.at[n % 2], sems.at[n % 2]
        if n >= 2:
            copies[n - 2].wait()
        through_radius = lax.dot_general(
            radius[span, :], grads[...], BY_TOKEN, preferred_element_type=jnp.float32
        )
        w = weight[span, :].astype(jnp.float32)
        signed = jnp.where(w > 0, through_radius, jnp.where(w < 0, -through_radius, 0.0))
        part[...] = (center[span, :] + signed) * scale
        copies.append(pltpu.make_async_copy(part, out.at[pl.ds(n * tile, tile), :], sem))
        copies[n].start()
    for copy in copies[-2:]:
        copy.wait()


def weight_terms(center, radius, grads, weight):
    inner, width = weight.shape
    tokens = grads.shape[0]
    tile = min(256, inner)
    scale = np.float32(1.0) / np.sqrt(np.float32(tokens))
    return pl.pallas_call(
        functools.partial(weight_kernel, scale),
        in_specs=[HERE] * 4,
        out_specs=ANYWHERE,
        out_shape=jax.ShapeDtypeStruct((inner, width), jnp.float32),
        scratch_shapes=[
            pltpu.VMEM((2, tile, width), jnp.float32),
            pltpu.SemaphoreType.DMA((2,)),
        ],
        compiler_params=pltpu.CompilerParams(vmem_limit_bytes=VMEM_LIMIT),
        cost_estimate=pl.CostEstimate(
            flops=2 * tokens * inner * width,
            bytes_accessed=2 * tokens * (inner + width) + 10 * inner * width,
            transcendentals=0,
        ),
    )(center, radius, grads, weight)


def on_device(rows, cols, center, radius, grad_center, grad_radius, weight, active):
    chips, cores = col_split(cols)
    ring = ring_of(rows)
    clockwise = [(ring[i], ring[(i + 1) % rows]) for i in range(rows)]
    counter = [(b, a) for a, b in clockwise]

    def swap_cores(value, j):
        perm = [(i, i - i % cores + (i % cores + j) % cores) for i in range(cols)]
        return lax.ppermute(value, "col", perm)

    def hop_chips(value, k):
        return lax.ppermute(value, "col", [(i, (i + k * cores) % cols) for i in range(cols)])

    def scattered(terms):
        parts = [[terms[k]] for k in range(chips)]
        for j in range(1, cores):
            for k in reversed(range(chips)):
                parts[k].append(swap_cores(terms[j * chips + k], j))
        return parts[0], [hop_chips(coded_sum(*parts[k]), k) for k in range(1, chips)]

    grads, both = packed(grad_center, grad_radius), packed(center, radius)
    held = [both] + [hop_chips(both, -k) for k in range(1, chips)]
    slots = {0: grads}
    for step in range(1, (rows + 1) // 2):
        slots[step] = lax.ppermute(slots[step - 1], "row", clockwise)
        slots[-step] = lax.ppermute(slots[1 - step], "row", counter)
        if step == 2:
            slots[step], weight = lax.optimization_barrier((slots[step], loaded(weight)))
    for j in range(1, cores):
        held += [swap_cores(value, -j) for value in held[:chips]]
    turned_c, turned_r = turned(held, 2)
    slots_c, slots_r = dict(slots), dict(slots)
    if rows % 2 == 0:
        step, count = rows // 2, grad_center.shape[0]
        slots_c[step] = lax.ppermute(slots[step - 1][:count], "row", clockwise)
        slots_r[-step] = lax.ppermute(slots[1 - step][count:], "row", counter)
    slots_c[0], turned_c, turned_r = lax.optimization_barrier((slots_c[0], turned_c, turned_r))

    terms_c, order_c = input_terms(
        rows, cols, tuple(slots_c), list(slots_c.values()), weight, False
    )
    near_c, far_c = scattered(terms_c)
    terms_r, order_r = input_terms(rows, cols, tuple(slots_r), list(slots_r.values()), weight, True)
    near_r, far_r = scattered(terms_r)
    through_center = center_terms(turned_c, order_c)
    weight_grad = weight_terms(through_center, turned_r, order_r, weight)
    return gated(near_c, far_c, active), gated(near_r, far_r, active), weight_grad


def solution(mesh):
    spec_in, spec_out, spec_weight = P("col", "row"), P("row", "col"), P("row", "col")
    return jax.shard_map(
        functools.partial(on_device, mesh.shape["row"], mesh.shape["col"]),
        mesh=mesh,
        in_specs=(spec_in, spec_in, spec_out, spec_out, spec_weight, spec_in),
        out_specs=(spec_in, spec_in, spec_weight),
        check_vma=False,
    )
```

time: 166 us -> 73.1 us (0.44)
  waiting for transfers between devices: 122 us -> 34.9 us
  Pallas kernels: 0 us -> 22.4 us
  matrix products: 20.9 us -> 0 us
  starting transfers between devices: 0.12 us -> 14.8 us
  between operations: 13.8 us -> 0.79 us
  other arithmetic: 8.6 us -> 0 us
    all_gather x2 -> x0, waiting for transfers between devices: 88.5 us -> none  [the longest x1 75.8 us: on_device(): panels = lax.all_gather(stacked, 'row', axis=1, tiled=True)]
    ppermute x0 -> x17, waiting for transfers between devices: none -> 34.9 us  [the longest x3 27 us: on_device(): slots[-step] = lax.ppermute(slots[1 - step], 'row', counter)]
    reduce_scatter x1 -> x0, waiting for transfers between devices: 33.4 us -> none  [on_device(): lax.psum_scatter(partial_terms, 'col', scatter_dimension=1, tiled=True)]
    pallas_call x0 -> x12, Pallas kernels: none -> 22.4 us  [the longest x1 5.87 us: weight_terms(): pl.pallas_call(functools.partial(weight_kernel, scale), in_specs=[HERE] *...]
    dot_general x4 -> x0, matrix products: 20.9 us -> none  [the longest x1 8.69 us: on_device(): lax.dot_general(inputs[1], panels[1], contract_tok, preferred_element_typ...]
    ppermute x0 -> x17, starting transfers between devices: none -> 14.8 us  [the longest x3 6.07 us: on_device(): slots[-step] = lax.ppermute(slots[1 - step], 'row', counter)]
    another operation x3 -> x0, other arithmetic: 6.31 us -> none  [the longest x1 2.56 us: on_device(): partial_terms = jnp.stack((through_center, through_radius))]
    mul x1 -> x0, other arithmetic: 2.29 us -> none  [on_device(): radius_in = gating * summed[1]]
  transfers between devices with their start and end apart: 3 -> 17, of which waited for: 3 -> 7; matrix products, arithmetic and copies ran while one was open for 15% -> 0% of each run, Pallas kernels for 0% -> 27%
where the time goes in v1:
time: 73.1 us; the launch traced here: 72.9 us
  waiting for transfers between devices  34.9 us (48%)
  Pallas kernels  22.4 us (31%)
  starting transfers between devices  14.8 us (20%)
  between operations  0.79 us (1%)
    ppermute x3, waiting for transfers between devices, on_device(): slots[-step] = lax.ppermute(slots[1 - step], 'row', counter)  27 us
    ppermute x3, starting transfers between devices, on_device(): slots[-step] = lax.ppermute(slots[1 - step], 'row', counter)  6.07 us
    pallas_call x1, Pallas kernels, weight_terms(): pl.pallas_call(functools.partial(weight_kernel, scale), in_specs=[HERE] *...  5.87 us
    pallas_call x2, Pallas kernels, input_terms(): pl.pallas_call(functools.partial(input_kernel, rows, cols, shifts, absolu...  5 us
    ppermute x3, starting transfers between devices, hop_chips(): lax.ppermute(value, 'col', [(i, (i + k * cores) % cols) for i in range(co...  4.38 us
    pallas_call x2, Pallas kernels, packed(): pl.pallas_call(pack_kernel, in_specs=[ANYWHERE] * 2, out_specs=ANYWHERE,...  3.54 us
    ppermute x3, waiting for transfers between devices, hop_chips(): lax.ppermute(value, 'col', [(i, (i + k * cores) % cols) for i in range(co...  3.12 us
    pallas_call x1, Pallas kernels, center_terms(): pl.pallas_call(center_kernel, in_specs=[HERE] * 2, out_specs=HERE, out_sh...  2.84 us
  transfers between devices with their start and end apart: 17, of which 7 were waited for; matrix products, arithmetic and copies ran while one was open for 0% of the time, Pallas kernels for 27%

profile of v1, /device:TPU:0, one launch (start us, length us, event | category | flops | bytes accessed | tf_op | source)
XLA Modules:
  0.0 72.9 jit_solution(11723002503134622234)
XLA Ops:
  0.6 1.8 %shard_map.85.refs_0_ = bf16[128,2048]{1,0:T(8,128)(2,1)} custom-call(bf16[64,2048]{1,0:T(8,128)(2,1)} %first.2, bf16[64,2048]{1,0:T(8,128)(2,1)} %second.2), custom_call_target="tpu_custom_call" | custom-call | bytes 1048576 | tf_op jit(solution)/shard_map/pallas_call | solution.py:185
  2.4 3.0 %collective-permute-start.4 = (bf16[128,2048]{1,0:T(8,128)(2,1)}, bf16[128,2048]{1,0:T(8,128)(2,1)S(1)}, u32[]{:S(2)}, u32[]{:S(2)}) collective-permute-start(bf16[128,2048]{1,0:T(8,128)(2,1)} %shard_map.85.refs_0_), channel_id=1, source_target_pairs={{8,0},{16,8},{24,16},{28,24},{20,28},{12,20},{4,12},{0,4},{9,1},{1... | collective-permute-start | bytes 1572872 | tf_op jit(solution)/shard_map/ppermute | solution.py:318
  5.4 0.1 collective-permute-start.3
  5.6 12.1 %collective-permute-done.4.refs_2_ = bf16[128,2048]{1,0:T(8,128)(2,1)S(1)} collective-permute-done((bf16[128,2048]{1,0:T(8,128)(2,1)}, bf16[128,2048]{1,0:T(8,128)(2,1)S(1)}, u32[]{:S(2)}, u32[]{:S(2)}) %collective-permute-start.4) | collective-permute-done | bytes 524320 | tf_op jit(solution)/shard_map/ppermute | solution.py:318
  17.6 1.7 %collective-permute-start.6 = (bf16[128,2048]{1,0:T(8,128)(2,1)S(1)}, bf16[128,2048]{1,0:T(8,128)(2,1)S(1)}, u32[]{:S(2)}, u32[]{:S(2)}) collective-permute-start(bf16[128,2048]{1,0:T(8,128)(2,1)S(1)} %collective-permute-done.4.refs_2_), channel_id=1, source_target_pairs={{8,0},{16,8},{24,16},{28,24},{20,28},{12,20},{4,12},{0,4},{9,1},{1... | collective-permute-start | bytes 1572872 | tf_op jit(solution)/shard_map/ppermute | solution.py:318
  19.3 0.3 collective-permute-start.5
  19.7 1.8 %shard_map.86.refs_0_ = bf16[256,1024]{1,0:T(8,128)(2,1)} custom-call(bf16[128,1024]{1,0:T(8,128)(2,1)} %first.3, bf16[128,1024]{1,0:T(8,128)(2,1)} %second.3), custom_call_target="tpu_custom_call" | custom-call | bytes 1048576 | tf_op jit(solution)/shard_map/pallas_call | solution.py:185
  21.5 1.7 %collective-permute-start = (bf16[256,1024]{1,0:T(8,128)(2,1)}, bf16[256,1024]{1,0:T(8,128)(2,1)S(1)}, u32[]{:S(2)}, u32[]{:S(2)}) collective-permute-start(bf16[256,1024]{1,0:T(8,128)(2,1)} %shard_map.86.refs_0_), channel_id=1, source_target_pairs={{0,2},{1,3},{2,0},{3,1},{4,6},{5,7},{6,4},{7,5},{8,10},{9,11},{10,... | collective-permute-start | bytes 1572872 | tf_op jit(solution)/shard_map/ppermute | solution.py:304
  23.2 7.6 %collective-permute-done.6.refs_4_ = bf16[128,2048]{1,0:T(8,128)(2,1)S(1)} collective-permute-done((bf16[128,2048]{1,0:T(8,128)(2,1)S(1)}, bf16[128,2048]{1,0:T(8,128)(2,1)S(1)}, u32[]{:S(2)}, u32[]{:S(2)}) %collective-permute-start.6) | collective-permute-done | bytes 524320 | tf_op jit(solution)/shard_map/ppermute | solution.py:318
  30.7 1.4 %collective-permute-start.8 = (bf16[128,2048]{1,0:T(8,128)(2,1)S(1)}, bf16[128,2048]{1,0:T(8,128)(2,1)S(1)}, u32[]{:S(2)}, u32[]{:S(2)}) collective-permute-start(bf16[128,2048]{1,0:T(8,128)(2,1)S(1)} %collective-permute-done.6.refs_4_), channel_id=1, source_target_pairs={{8,0},{16,8},{24,16},{28,24},{20,28},{12,20},{4,12},{0,4},{9,1},{1... | collective-permute-start | bytes 1572872 | tf_op jit(solution)/shard_map/ppermute | solution.py:318
  32.1 2.2 %shard_map.88.refs_8_.weight = bf16[1024,2048]{1,0:T(8,128)(2,1)S(1)} custom-call(bf16[1024,2048]{1,0:T(8,128)(2,1)} %source.1), custom_call_target="tpu_custom_call" | custom-call | bytes 8388608 | tf_op jit(solution)/shard_map/pallas_call | solution.py:99
  34.3 0.7 collective-permute-start.7
  35.0 0.5 collective-permute-start.2
  35.5 7.4 %collective-permute-done.8.refs_6_ = bf16[128,2048]{1,0:T(8,128)(2,1)S(1)} collective-permute-done((bf16[128,2048]{1,0:T(8,128)(2,1)S(1)}, bf16[128,2048]{1,0:T(8,128)(2,1)S(1)}, u32[]{:S(2)}, u32[]{:S(2)}) %collective-permute-start.8) | collective-permute-done | bytes 524320 | tf_op jit(solution)/shard_map/ppermute | solution.py:318
  42.9 1.2 %collective-permute-start.13 = (bf16[64,2048]{1,0:T(8,128)(2,1)S(1)}, bf16[64,2048]{1,0:T(8,128)(2,1)S(1)}, u32[]{:S(2)}, u32[]{:S(2)}) collective-permute-start(bf16[64,2048]{1,0:T(8,128)(2,1)S(1)} %slice.9), channel_id=1, source_target_pairs={{8,0},{16,8},{24,16},{28,24},{20,28},{12,20},{4,12},{0,4},{9,1},{1... | collective-permute-start | bytes 786440 | tf_op jit(solution)/shard_map/ppermute | solution.py:328
  44.2 2.2 %collective-permute-done.7.refs_5_ = bf16[128,2048]{1,0:T(8,128)(2,1)S(1)} collective-permute-done((bf16[128,2048]{1,0:T(8,128)(2,1)S(1)}, bf16[128,2048]{1,0:T(8,128)(2,1)S(1)}, u32[]{:S(2)}, u32[]{:S(2)}) %collective-permute-start.7) | collective-permute-done | bytes 524320 | tf_op jit(solution)/shard_map/ppermute | solution.py:317
  46.4 0.7 collective-permute-start.9
  47.1 0.6 shard_map.87
  47.7 1.7 %collective-permute-done.13.refs_7_ = bf16[64,2048]{1,0:T(8,128)(2,1)S(1)} collective-permute-done((bf16[64,2048]{1,0:T(8,128)(2,1)S(1)}, bf16[64,2048]{1,0:T(8,128)(2,1)S(1)}, u32[]{:S(2)}, u32[]{:S(2)}) %collective-permute-start.13) | collective-permute-done | bytes 262176 | tf_op jit(solution)/shard_map/ppermute | solution.py:328
  49.4 2.5 %shard_map.92 = (f32[128,1024]{1,0:T(8,128)S(1)}, f32[128,1024]{1,0:T(8,128)S(1)}, f32[128,1024]{1,0:T(8,128)S(1)}, f32[128,1024]{1,0:T(8,128)S(1)}, bf16[512,2048]{1,0:T(8,128)(2,1)S(1)}) custom-call(bf16[128,2048]{1,0:T(8,128)(2,1)S(1)} %copy-done, bf16[128,2048]{1,0:T(8,128)(2,1)S(1)} %collective-permute-done.3.refs_1_, ...), custom_call_target="tpu_custom_call" | custom-call | flops 2147483648 | bytes 8388608 | tf_op jit(solution)/shard_map/pallas_call | solution.py:76
  52.0 0.9 %collective-permute-done.9.refs_7_ = bf16[64,2048]{1,0:T(8,128)(2,1)S(1)} collective-permute-done((bf16[64,2048]{1,0:T(8,128)(2,1)S(1)}, bf16[64,2048]{1,0:T(8,128)(2,1)S(1)}, u32[]{:S(2)}, u32[]{:S(2)}) %collective-permute-start.9) | collective-permute-done | bytes 262176 | tf_op jit(solution)/shard_map/ppermute | solution.py:327
  52.8 2.5 %shard_map.89 = (f32[128,1024]{1,0:T(8,128)S(1)}, f32[128,1024]{1,0:T(8,128)S(1)}, f32[128,1024]{1,0:T(8,128)S(1)}, f32[128,1024]{1,0:T(8,128)S(1)}, bf16[512,2048]{1,0:T(8,128)(2,1)S(1)}) custom-call(bf16[128,2048]{1,0:T(8,128)(2,1)S(1)} %copy-done, bf16[128,2048]{1,0:T(8,128)(2,1)S(1)} %collective-permute-done.3.refs_1_, ...), custom_call_target="tpu_custom_call" | custom-call | flops 2147483648 | bytes 8388608 | tf_op jit(solution)/shard_map/pallas_call | solution.py:76
  55.4 0.5 collective-permute-start.14
  56.0 0.2 shard_map.93
  56.2 1.6 %collective-permute-start.16 = (s16[128,1152]{1,0:T(8,128)(2,1)S(1)}, s16[128,1152]{1,0:T(8,128)(2,1)S(1)}, u32[]{:S(2)}, u32[]{:S(2)}) collective-permute-start(s16[128,1152]{1,0:T(8,128)(2,1)S(1)} %shard_map.93), channel_id=1, source_target_pairs={{0,2},{1,3},{2,0},{3,1},{4,6},{5,7},{6,4},{7,5},{8,10},{9,11},{10,... | collective-permute-start | bytes 884744 | tf_op jit(solution)/shard_map/ppermute | solution.py:304
  57.8 0.2 shard_map.90
  58.0 1.1 %collective-permute-start.12 = (s16[128,1152]{1,0:T(8,128)(2,1)S(1)}, s16[128,1152]{1,0:T(8,128)(2,1)S(1)}, u32[]{:S(2)}, u32[]{:S(2)}) collective-permute-start(s16[128,1152]{1,0:T(8,128)(2,1)S(1)} %shard_map.90), channel_id=1, source_target_pairs={{0,2},{1,3},{2,0},{3,1},{4,6},{5,7},{6,4},{7,5},{8,10},{9,11},{10,... | collective-permute-start | bytes 884744 | tf_op jit(solution)/shard_map/ppermute | solution.py:304
  59.1 2.8 %shard_map.95.center = f32[1024,2048]{1,0:T(8,128)S(1)} custom-call(bf16[1024,512]{1,0:T(8,128)(2,1)S(1)} %get-tuple-element.33.center, bf16[512,2048]{1,0:T(8,128)(2,1)S(1)} %get-tuple-element.34.grads), custom_call_target="tpu_custom_call" | custom-call | flops 2147483648 | bytes 11534336 | tf_op jit(solution)/shard_map/pallas_call | solution.py:236
  61.9 5.9 %shard_map.96 = f32[1024,2048]{1,0:T(8,128)} custom-call(f32[1024,2048]{1,0:T(8,128)S(1)} %shard_map.95.center, bf16[1024,512]{1,0:T(8,128)(2,1)S(1)} %get-tuple-element.35.radius, bf16[512,2048]{1,0:T(8,128)(2,1)S(1)} %get-tuple-element.36.grads, bf16[1024,2048]{1,0:T(8,128)(2,1)S(1)} %shard_map.88.refs_8_.weight), custom_call_target="tpu_custom_call" | custom-call | flops 2147483648 | bytes 24117248 | tf_op jit(solution)/shard_map/pallas_call | solution.py:275
  67.8 1.0 %shard_map.94 = f32[128,1024]{1,0:T(8,128)} custom-call(f32[128,1024]{1,0:T(8,128)S(1)} %get-tuple-element.29.refs_0_, f32[128,1024]{1,0:T(8,128)S(1)} %collective-permute-done.14.refs_1_, s16[128,1152]{1,0:T(8,128)(2,1)S(1)} %collective-permute-done.16.refs_2_, s32[128,1024]{1,0:T(8,128)S(1)} %copy-done.2), custom_call_target="tpu_custom_call" | custom-call | flops 1048576 | bytes 2621440 | tf_op jit(solution)/shard_map/pallas_call | solution.py:151
  68.8 3.1 %collective-permute-done.12.refs_2_ = s16[128,1152]{1,0:T(8,128)(2,1)S(1)} collective-permute-done((s16[128,1152]{1,0:T(8,128)(2,1)S(1)}, s16[128,1152]{1,0:T(8,128)(2,1)S(1)}, u32[]{:S(2)}, u32[]{:S(2)}) %collective-permute-start.12) | collective-permute-done | bytes 294944 | tf_op jit(solution)/shard_map/ppermute | solution.py:304
  71.9 1.0 %shard_map.91 = f32[128,1024]{1,0:T(8,128)} custom-call(f32[128,1024]{1,0:T(8,128)S(1)} %get-tuple-element.25.refs_0_, f32[128,1024]{1,0:T(8,128)S(1)} %collective-permute-done.10.refs_1_, s16[128,1152]{1,0:T(8,128)(2,1)S(1)} %collective-permute-done.12.refs_2_, s32[128,1024]{1,0:T(8,128)S(1)} %copy-done.2), custom_call_target="tpu_custom_call" | custom-call | flops 1048576 | bytes 2621440 | tf_op jit(solution)/shard_map/pallas_call | solution.py:151
  (22 shorter events, 0.3 us)
Async XLA Ops:
  2.4 15.2 %collective-permute-start.4 = (bf16[128,2048]{1,0:T(8,128)(2,1)}, bf16[128,2048]{1,0:T(8,128)(2,1)S(1)}, u32[]{:S(2)}, u32[]{:S(2)}) collective-permute-start(bf16[128,2048]{1,0:T(8,128)(2,1)} %shard_map.85.refs_0_), channel_id=1, source_target_pairs={{8,0},{16,8},{24,16},{28,24},{20,28},{12,20},{4,12},{0,4},{9,1},{1... | collective-permute-start | bytes 1572872 | tf_op jit(solution)/shard_map/ppermute | solution.py:318
  5.4 13.9 %collective-permute-start.3 = (bf16[128,2048]{1,0:T(8,128)(2,1)}, bf16[128,2048]{1,0:T(8,128)(2,1)S(1)}, u32[]{:S(2)}, u32[]{:S(2)}) collective-permute-start(bf16[128,2048]{1,0:T(8,128)(2,1)} %shard_map.85.refs_0_), channel_id=1, source_target_pairs={{0,8},{8,16},{16,24},{24,28},{28,20},{20,12},{12,4},{4,0},{1,9},{9... | collective-permute-start | bytes 1572872 | tf_op jit(solution)/shard_map/ppermute | solution.py:317
  17.6 13.1 %collective-permute-start.6 = (bf16[128,2048]{1,0:T(8,128)(2,1)S(1)}, bf16[128,2048]{1,0:T(8,128)(2,1)S(1)}, u32[]{:S(2)}, u32[]{:S(2)}) collective-permute-start(bf16[128,2048]{1,0:T(8,128)(2,1)S(1)} %collective-permute-done.4.refs_2_), channel_id=1, source_target_pairs={{8,0},{16,8},{24,16},{28,24},{20,28},{12,20},{4,12},{0,4},{9,1},{1... | collective-permute-start | bytes 1572872 | tf_op jit(solution)/shard_map/ppermute | solution.py:318
  19.3 15.0 %collective-permute-start.5 = (bf16[128,2048]{1,0:T(8,128)(2,1)S(1)}, bf16[128,2048]{1,0:T(8,128)(2,1)S(1)}, u32[]{:S(2)}, u32[]{:S(2)}) collective-permute-start(bf16[128,2048]{1,0:T(8,128)(2,1)S(1)} %collective-permute-done.3.refs_1_), channel_id=1, source_target_pairs={{0,8},{8,16},{16,24},{24,28},{28,20},{20,12},{12,4},{4,0},{1,9},{9... | collective-permute-start | bytes 1572872 | tf_op jit(solution)/shard_map/ppermute | solution.py:317
  21.4 13.6 %copy-start.1 = (bf16[256,1024]{1,0:T(8,128)(2,1)S(1)}, bf16[256,1024]{1,0:T(8,128)(2,1)}, u32[]{:S(2)}) copy-start(bf16[256,1024]{1,0:T(8,128)(2,1)} %shard_map.86.refs_0_) | copy-start | bytes 1572868
  21.4 27.9 %copy-start = (bf16[128,2048]{1,0:T(8,128)(2,1)S(1)}, bf16[128,2048]{1,0:T(8,128)(2,1)}, u32[]{:S(2)}) copy-start(bf16[128,2048]{1,0:T(8,128)(2,1)} %shard_map.85.refs_0_) | copy-start | bytes 1572868
  21.5 13.6 %collective-permute-start = (bf16[256,1024]{1,0:T(8,128)(2,1)}, bf16[256,1024]{1,0:T(8,128)(2,1)S(1)}, u32[]{:S(2)}, u32[]{:S(2)}) collective-permute-start(bf16[256,1024]{1,0:T(8,128)(2,1)} %shard_map.86.refs_0_), channel_id=1, source_target_pairs={{0,2},{1,3},{2,0},{3,1},{4,6},{5,7},{6,4},{7,5},{8,10},{9,11},{10,... | collective-permute-start | bytes 1572872 | tf_op jit(solution)/shard_map/ppermute | solution.py:304
  30.7 12.2 %collective-permute-start.8 = (bf16[128,2048]{1,0:T(8,128)(2,1)S(1)}, bf16[128,2048]{1,0:T(8,128)(2,1)S(1)}, u32[]{:S(2)}, u32[]{:S(2)}) collective-permute-start(bf16[128,2048]{1,0:T(8,128)(2,1)S(1)} %collective-permute-done.6.refs_4_), channel_id=1, source_target_pairs={{8,0},{16,8},{24,16},{28,24},{20,28},{12,20},{4,12},{0,4},{9,1},{1... | collective-permute-start | bytes 1572872 | tf_op jit(solution)/shard_map/ppermute | solution.py:318
  34.3 12.1 %collective-permute-start.7 = (bf16[128,2048]{1,0:T(8,128)(2,1)S(1)}, bf16[128,2048]{1,0:T(8,128)(2,1)S(1)}, u32[]{:S(2)}, u32[]{:S(2)}) collective-permute-start(bf16[128,2048]{1,0:T(8,128)(2,1)S(1)} %collective-permute-done.5.refs_3_), channel_id=1, source_target_pairs={{0,8},{8,16},{16,24},{24,28},{28,20},{20,12},{12,4},{4,0},{1,9},{9... | collective-permute-start | bytes 1572872 | tf_op jit(solution)/shard_map/ppermute | solution.py:317
  35.0 12.1 %collective-permute-start.1 = (bf16[256,1024]{1,0:T(8,128)(2,1)S(1)}, bf16[256,1024]{1,0:T(8,128)(2,1)S(1)}, u32[]{:S(2)}, u32[]{:S(2)}) collective-permute-start(bf16[256,1024]{1,0:T(8,128)(2,1)S(1)} %copy-done.1), channel_id=1, source_target_pairs={{0,1},{1,0},{2,3},{3,2},{4,5},{5,4},{6,7},{7,6},{8,9},{9,8},{10,11... | collective-permute-start | bytes 1572872 | tf_op jit(solution)/shard_map/ppermute | solution.py:301
  35.0 12.1 %collective-permute-start.2 = (bf16[256,1024]{1,0:T(8,128)(2,1)S(1)}, bf16[256,1024]{1,0:T(8,128)(2,1)S(1)}, u32[]{:S(2)}, u32[]{:S(2)}) collective-permute-start(bf16[256,1024]{1,0:T(8,128)(2,1)S(1)} %collective-permute-done.refs_1_), channel_id=1, source_target_pairs={{0,1},{1,0},{2,3},{3,2},{4,5},{5,4},{6,7},{7,6},{8,9},{9,8},{10,11... | collective-permute-start | bytes 1572872 | tf_op jit(solution)/shard_map/ppermute | solution.py:301
  42.9 6.4 %collective-permute-start.13 = (bf16[64,2048]{1,0:T(8,128)(2,1)S(1)}, bf16[64,2048]{1,0:T(8,128)(2,1)S(1)}, u32[]{:S(2)}, u32[]{:S(2)}) collective-permute-start(bf16[64,2048]{1,0:T(8,128)(2,1)S(1)} %slice.9), channel_id=1, source_target_pairs={{8,0},{16,8},{24,16},{28,24},{20,28},{12,20},{4,12},{0,4},{9,1},{1... | collective-permute-start | bytes 786440 | tf_op jit(solution)/shard_map/ppermute | solution.py:328
  46.4 6.4 %collective-permute-start.9 = (bf16[64,2048]{1,0:T(8,128)(2,1)S(1)}, bf16[64,2048]{1,0:T(8,128)(2,1)S(1)}, u32[]{:S(2)}, u32[]{:S(2)}) collective-permute-start(bf16[64,2048]{1,0:T(8,128)(2,1)S(1)} %slice.8), channel_id=1, source_target_pairs={{0,8},{8,16},{16,24},{24,28},{28,20},{20,12},{12,4},{4,0},{1,9},{9... | collective-permute-start | bytes 786440 | tf_op jit(solution)/shard_map/ppermute | solution.py:327
  51.9 4.1 %collective-permute-start.15 = (f32[128,1024]{1,0:T(8,128)S(1)}, f32[128,1024]{1,0:T(8,128)S(1)}, u32[]{:S(2)}, u32[]{:S(2)}) collective-permute-start(f32[128,1024]{1,0:T(8,128)S(1)} %get-tuple-element.32), channel_id=1, source_target_pairs={{0,1},{1,0},{2,3},{3,2},{4,5},{5,4},{6,7},{7,6},{8,9},{9,8},{10,11... | collective-permute-start | bytes 1572872 | tf_op jit(solution)/shard_map/ppermute | solution.py:301
  55.3 2.4 %collective-permute-start.11 = (f32[128,1024]{1,0:T(8,128)S(1)}, f32[128,1024]{1,0:T(8,128)S(1)}, u32[]{:S(2)}, u32[]{:S(2)}) collective-permute-start(f32[128,1024]{1,0:T(8,128)S(1)} %get-tuple-element.28), channel_id=1, source_target_pairs={{0,1},{1,0},{2,3},{3,2},{4,5},{5,4},{6,7},{7,6},{8,9},{9,8},{10,11... | collective-permute-start | bytes 1572872 | tf_op jit(solution)/shard_map/ppermute | solution.py:301
  55.4 12.4 %collective-permute-start.14 = (f32[128,1024]{1,0:T(8,128)S(1)}, f32[128,1024]{1,0:T(8,128)S(1)}, u32[]{:S(2)}, u32[]{:S(2)}) collective-permute-start(f32[128,1024]{1,0:T(8,128)S(1)} %get-tuple-element.30), channel_id=1, source_target_pairs={{0,1},{1,0},{2,3},{3,2},{4,5},{5,4},{6,7},{7,6},{8,9},{9,8},{10,11... | collective-permute-start | bytes 1572872 | tf_op jit(solution)/shard_map/ppermute | solution.py:301
  55.9 12.9 %collective-permute-start.10 = (f32[128,1024]{1,0:T(8,128)S(1)}, f32[128,1024]{1,0:T(8,128)S(1)}, u32[]{:S(2)}, u32[]{:S(2)}) collective-permute-start(f32[128,1024]{1,0:T(8,128)S(1)} %get-tuple-element.26), channel_id=1, source_target_pairs={{0,1},{1,0},{2,3},{3,2},{4,5},{5,4},{6,7},{7,6},{8,9},{9,8},{10,11... | collective-permute-start | bytes 1572872 | tf_op jit(solution)/shard_map/ppermute | solution.py:301
  56.2 11.6 %collective-permute-start.16 = (s16[128,1152]{1,0:T(8,128)(2,1)S(1)}, s16[128,1152]{1,0:T(8,128)(2,1)S(1)}, u32[]{:S(2)}, u32[]{:S(2)}) collective-permute-start(s16[128,1152]{1,0:T(8,128)(2,1)S(1)} %shard_map.93), channel_id=1, source_target_pairs={{0,2},{1,3},{2,0},{3,1},{4,6},{5,7},{6,4},{7,5},{8,10},{9,11},{10,... | collective-permute-start | bytes 884744 | tf_op jit(solution)/shard_map/ppermute | solution.py:304
  58.0 14.0 %collective-permute-start.12 = (s16[128,1152]{1,0:T(8,128)(2,1)S(1)}, s16[128,1152]{1,0:T(8,128)(2,1)S(1)}, u32[]{:S(2)}, u32[]{:S(2)}) collective-permute-start(s16[128,1152]{1,0:T(8,128)(2,1)S(1)} %shard_map.90), channel_id=1, source_target_pairs={{0,2},{1,3},{2,0},{3,1},{4,6},{5,7},{6,4},{7,5},{8,10},{9,11},{10,... | collective-permute-start | bytes 884744 | tf_op jit(solution)/shard_map/ppermute | solution.py:304
  61.9 5.9 %copy-start.2 = (s32[128,1024]{1,0:T(8,128)S(1)}, s32[128,1024]{1,0:T(8,128)}, u32[]{:S(2)}) copy-start(s32[128,1024]{1,0:T(8,128)} %refs_3_.3) | copy-start | bytes 1572868

commit v2 on v0

v2 whole, which is shorter than its diff:
```python
import functools

import jax
import jax.numpy as jnp
import numpy as np
from jax import lax
from jax.experimental import pallas as pl
from jax.experimental.pallas import tpu as pltpu
from jax.sharding import PartitionSpec as P

VMEM_LIMIT = 24 * 1024 * 1024
VMEM_MOST = 60 * 1024 * 1024
HERE = pl.BlockSpec(memory_space=pltpu.VMEM)
LANES = 128
LEVELS = np.float32(32000)
TINY = np.float32(2.0**-100)
ANYWHERE = pl.BlockSpec(memory_space=pl.ANY)
BY_LAST = (((1,), (1,)), ((), ()))
BY_TOKEN = (((1,), (0,)), ((), ()))
PAIR = 2


def ring_of(rows):
    return list(range(0, rows, PAIR)) + list(range(rows - 1, 0, -PAIR))


def on_ring(row, rows):
    return lax.select(lax.rem(row, PAIR) == 0, lax.div(row, PAIR), rows - 1 - lax.div(row, PAIR))


def off_ring(place, rows):
    return lax.select(place < rows // PAIR, PAIR * place, PAIR * (rows - place) - 1)


def apart(a, b, rows):
    ahead = lax.rem(a - b + rows, rows)
    return lax.min(ahead, rows - ahead)


def by_distance(rows):
    return [0] + [way * step for step in range(1, rows // 2) for way in (1, -1)] + [rows // 2]


def col_split(cols):
    return (cols // 2, 2) if cols % 2 == 0 else (cols, 1)


def spot(rows, cols, shift, all_near=False):
    chips, cores = col_split(cols)
    here, col = on_ring(lax.axis_index("row"), rows), lax.axis_index("col")
    x, my_core = lax.div(col, cores), lax.rem(col, cores)
    place = lax.rem(here + (rows - shift) % rows, rows)
    source = off_ring(place, rows)
    owner, half = lax.div(source, PAIR), lax.rem(source, PAIR)
    chip, core = lax.rem(lax.div(owner, cores) + chips - x, chips), lax.rem(owner, cores)
    near_core = lax.rem(core + cores - my_core, cores)
    far = abs(shift) > apart(here, rows - 1 - place, rows)
    piece = (near_core if all_near else lax.select(far | (chip == 0), near_core, core)) * chips + chip
    return piece, half, far


def shard_of(slot, half, held):
    first = half * held if slot.shape[0] > held else 0
    return slot[first : first + held, :]


def terms_of(lhs, weight, cores, own, others, kind):
    inner, chips = weight.shape[0], others[0].shape[1] + 1
    tile = min(256, inner)
    held = lhs.shape[0] // (cores * chips)
    rows = slice(kind * held, (kind + 1) * held)
    for i in range(inner // tile):
        span = slice(i * tile, (i + 1) * tile)
        block = weight[span, :]
        if kind:
            block = jnp.abs(block)
        terms = lax.dot_general(lhs, block, BY_LAST, preferred_element_type=jnp.float32)
        for n in range(cores * chips):
            core, chip = divmod(n, chips)
            part = terms[n * held : (n + 1) * held, :]
            if not chip:
                own[core][rows, span] = part
            elif len(others) == 1:
                others[0][core, chip - 1, rows, span] = part
            else:
                others[kind * cores + core][0, chip - 1, :, span] = part


def near_kernel(rows, cols, shifts, *refs):
    count = len(shifts)
    slots_c, slots_r, weight = refs[:count], refs[count : 2 * count], refs[2 * count]
    own, others, orders = refs[2 * count + 1 : -3], refs[-3:-2], refs[-2:]
    cores = len(own)
    middle = orders[0].shape[0] // 2
    held = middle // cols
    for n, shift in enumerate(shifts):
        piece, _, far = spot(rows, cols, shift)
        start = pl.multiple_of(lax.select(far, middle, 0) + piece * held, held)
        for half, (order, slots) in enumerate(zip(orders, (slots_c, slots_r))):
            order[pl.ds(start, held), :] = shard_of(slots[n], half, held)
    for kind, order in enumerate(orders):
        terms_of(order[:middle, :], weight, cores, own, others, kind)


def near_terms(rows, cols, held, shifts, slots_c, slots_r, weight):
    inner, width = weight.shape
    tokens = held * rows
    chips, cores = col_split(cols)
    found = pl.pallas_call(
        functools.partial(near_kernel, rows, cols, shifts),
        in_specs=[HERE] * (2 * len(shifts) + 1),
        out_specs=[HERE] * (cores + 3),
        out_shape=[jax.ShapeDtypeStruct((2 * held, inner), jnp.float32)] * cores
        + [jax.ShapeDtypeStruct((cores, chips - 1, 2 * held, inner), jnp.float32)]
        + [jax.ShapeDtypeStruct((tokens, width), jnp.bfloat16)] * 2,
        compiler_params=pltpu.CompilerParams(vmem_limit_bytes=VMEM_LIMIT),
    )(*slots_c, *slots_r, weight)
    return found[:-2], found[-2:]


def far_kernel(rows, cols, *refs):
    orders, lasts, (weight, *outs, work) = refs[:2], refs[2:4], refs[4:]
    cores = len(outs) // 3
    middle = work.shape[0]
    held = middle // cols
    piece, _, _ = spot(rows, cols, rows // 2, all_near=True)
    start = pl.multiple_of(piece * held, held)
    for half, (order, last) in enumerate(zip(orders, lasts)):
        work[...] = order[middle:, :]
        work[pl.ds(start, held), :] = last[...]
        terms_of(work[...], weight, cores, outs[:cores], outs[cores:], half)


def far_terms(rows, cols, orders, lasts, weight):
    inner, width = weight.shape
    held = lasts[0].shape[0]
    tokens = held * rows
    chips, cores = col_split(cols)
    return pl.pallas_call(
        functools.partial(far_kernel, rows, cols),
        in_specs=[HERE] * 5,
        out_specs=[HERE] * (3 * cores),
        out_shape=[jax.ShapeDtypeStruct((2 * held, inner), jnp.float32)] * cores
        + [jax.ShapeDtypeStruct((1, chips - 1, held, inner), jnp.float32)] * (2 * cores),
        scratch_shapes=[pltpu.VMEM((tokens // 2, width), jnp.bfloat16)],
        compiler_params=pltpu.CompilerParams(vmem_limit_bytes=VMEM_LIMIT),
    )(*orders, *lasts, weight)


def sum_kernel(chips, *refs):
    terms, outs = refs[: 1 - chips], refs[1 - chips :]
    rows, width = outs[0].shape[0] // 2, outs[0].shape[1] - LANES
    for k, out in enumerate(outs):
        for kind in range(2):
            mine = slice(kind * rows, (kind + 1) * rows)
            if len(terms) == 1:
                parts = [terms[0][j, k, mine, :] for j in range(terms[0].shape[0])]
            else:
                count = len(terms) // 2
                parts = [ref[0, k] for ref in terms[kind * count : (kind + 1) * count]]
            total = parts[0]
            for part in parts[1:]:
                total = total + part
            most = jnp.max(jnp.abs(total), axis=1, keepdims=True)
            exponent = jnp.ceil(jnp.log2(jnp.maximum(most, TINY)) + 1e-3)
            coded = jnp.round(total * (LEVELS / jnp.exp2(exponent)))
            out[mine, :width] = coded.astype(jnp.int16)
            out[mine, width:] = jnp.broadcast_to(exponent, (rows, LANES)).astype(jnp.int16)


def coded_sums(chips, rows, terms):
    width = terms[0].shape[3]
    return pl.pallas_call(
        functools.partial(sum_kernel, chips),
        in_specs=[HERE] * len(terms),
        out_specs=[HERE] * (chips - 1),
        out_shape=[jax.ShapeDtypeStruct((rows, width + LANES), jnp.int16)] * (chips - 1),
        compiler_params=pltpu.CompilerParams(vmem_limit_bytes=VMEM_LIMIT),
    )(*terms)


def gate_kernel(rows, cols, near, far, *refs):
    rounds, (active, *outs) = refs[:-3], refs[-3:]
    rounds = rounds[: near + far], rounds[near + far :]
    held = active.shape[0] // PAIR
    width = active.shape[1]
    here, col = on_ring(lax.axis_index("row"), rows), lax.axis_index("col")
    first = apart(here, on_ring(PAIR * col, rows), rows)
    second = apart(here, on_ring(PAIR * col + 1, rows), rows)
    halves = lax.select(first < second, 0, 1), lax.select(first < second, 1, 0)
    for half, parts in zip(halves, rounds):
        span = pl.ds(pl.multiple_of(half * held, held), held)
        gate = active[span, :].astype(jnp.float32)
        for n, out in enumerate(outs):
            mine = slice(n * held, (n + 1) * held)
            total = parts[0][mine, :]
            for part in parts[1:near]:
                total = total + part[mine, :]
            for part in parts[near:]:
                exponent = part[mine, width : width + 1].astype(jnp.float32)
                total = total + part[mine, :width].astype(jnp.float32) * (
                    jnp.exp2(exponent) / LEVELS
                )
            out[span, :] = gate * total


def gated(rows, cols, rounds, active):
    near, far = rounds[0]
    parts = [part for found in rounds for kind in found for part in kind]
    size = active.size
    return pl.pallas_call(
        functools.partial(gate_kernel, rows, cols, len(near), len(far)),
        in_specs=[HERE] * (len(parts) + 1),
        out_specs=[HERE] * 2,
        out_shape=[jax.ShapeDtypeStruct(active.shape, jnp.float32)] * 2,
        compiler_params=pltpu.CompilerParams(vmem_limit_bytes=VMEM_LIMIT),
    )(*parts, active)


def pack_kernel(first, second, out, both, sems):
    rows = first.shape[0]
    spans = [pl.ds(0, rows), pl.ds(rows, rows)]
    copies = [
        pltpu.make_async_copy(source, both.at[span, :], sem)
        for source, span, sem in zip((first, second), spans, (sems.at[0], sems.at[1]))
    ]
    onward = [
        pltpu.make_async_copy(both.at[span, :], out.at[span, :], sem)
        for span, sem in zip(spans, (sems.at[2], sems.at[3]))
    ]
    for copy in copies:
        copy.start()
    for copy, then in zip(copies, onward):
        copy.wait()
        then.start()
    for then in onward:
        then.wait()


def packed(first, second):
    rows, width = first.shape
    return pl.pallas_call(
        pack_kernel,
        in_specs=[ANYWHERE] * 2,
        out_specs=ANYWHERE,
        out_shape=jax.ShapeDtypeStruct((2 * rows, width), first.dtype),
        scratch_shapes=[pltpu.VMEM((2 * rows, width), first.dtype), pltpu.SemaphoreType.DMA((4,))],
        compiler_params=pltpu.CompilerParams(vmem_limit_bytes=VMEM_MOST),
    )(first, second)


def stack_kernel(*refs):
    *parts, out = refs
    rows = parts[0].shape[0]
    for n, part in enumerate(parts):
        out[n * rows : (n + 1) * rows, :] = part[...]


def stacked(parts):
    rows, width = parts[0].shape
    return pl.pallas_call(
        stack_kernel,
        in_specs=[HERE] * len(parts),
        out_specs=HERE,
        out_shape=jax.ShapeDtypeStruct((len(parts) * rows, width), parts[0].dtype),
        compiler_params=pltpu.CompilerParams(vmem_limit_bytes=VMEM_LIMIT),
    )(*parts)


def turn_kernel(rows, cols, *refs):
    held, outs, whole, order = refs[:-6], refs[-6:-2], refs[-2], refs[-1]
    chips = cols // len(held)
    owned = whole.shape[0] // cols
    shard = owned // PAIR
    near = outs[0].shape[1]
    for kind in range(2):
        for n in range(cols):
            first = (2 * (n % chips) + kind) * owned
            whole[n * owned : (n + 1) * owned, :] = held[n // chips][first : first + owned, :]
        for n, shift in enumerate(by_distance(rows)):
            piece, half, _ = spot(rows, cols, shift, all_near=True)
            start = pl.multiple_of((piece * PAIR + half) * shard, shard)
            order[n * shard : (n + 1) * shard, :] = whole[pl.ds(start, shard), :]
        outs[kind][...] = order[:near, :].T
        outs[2 + kind][...] = order[near:, :].T


def turned(rows, cols, held):
    both, inner = held[0].shape
    tokens = both // 2 * len(held)
    return pl.pallas_call(
        functools.partial(turn_kernel, rows, cols),
        in_specs=[HERE] * len(held),
        out_specs=[HERE] * 4,
        out_shape=[jax.ShapeDtypeStruct((inner, tokens // 2), jnp.bfloat16)] * 4,
        scratch_shapes=[pltpu.VMEM((tokens, inner), jnp.bfloat16)] * 2,
        compiler_params=pltpu.CompilerParams(vmem_limit_bytes=VMEM_LIMIT),
    )(*held)


def gather_slots(slots_c, slots_r, grads):
    held = grads[0].shape[0] // len(slots_c)
    for half, (grad, slots) in enumerate(zip(grads, (slots_c, slots_r))):
        for n, slot in enumerate(slots):
            grad[n * held : (n + 1) * held, :] = shard_of(slot, half, held)


def weight_part(inputs, grads, weight, span):
    through_center, through_radius = (
        lax.dot_general(ref[span, :], grad[...], BY_TOKEN, preferred_element_type=jnp.float32)
        for ref, grad in zip(inputs, grads)
    )
    w = weight[span, :].astype(jnp.float32)
    signed = jnp.where(w > 0, through_radius, jnp.where(w < 0, -through_radius, 0.0))
    return through_center + signed


def first_kernel(count, *refs):
    inputs, slots_c, slots_r = refs[:2], refs[2 : 2 + count], refs[2 + count : 2 + 2 * count]
    weight, out, *grads = refs[2 + 2 * count :]
    gather_slots(slots_c, slots_r, grads)
    tile = min(256, out.shape[0])
    for n in range(out.shape[0] // tile):
        span = slice(n * tile, (n + 1) * tile)
        out[span, :] = weight_part(inputs, grads, weight, span)


def first_weight_terms(inputs, slots_c, slots_r, weight):
    inner, width = weight.shape
    tokens = inputs[0].shape[1]
    return pl.pallas_call(
        functools.partial(first_kernel, len(slots_c)),
        in_specs=[HERE] * (3 + 2 * len(slots_c)),
        out_specs=HERE,
        out_shape=jax.ShapeDtypeStruct((inner, width), jnp.float32),
        scratch_shapes=[pltpu.VMEM((tokens, width), jnp.bfloat16)] * 2,
        compiler_params=pltpu.CompilerParams(vmem_limit_bytes=VMEM_LIMIT),
    )(*inputs, *slots_c, *slots_r, weight)


def weight_kernel(count, scale, begun, *refs):
    inputs, slots_c, slots_r = refs[:2], refs[2 : 2 + count], refs[2 + count : 2 + 2 * count]
    weight, out, grad_c, grad_r, parts, sems = refs[2 + 2 * count :]
    gather_slots(slots_c, slots_r, (grad_c, grad_r))
    tile = parts.shape[1]
    copies = []
    for n in range(out.shape[0] // tile):
        span = slice(n * tile, (n + 1) * tile)
        part, sem = parts.at[n % 2], sems.at[n % 2]
        if n >= 2:
            copies[n - 2].wait()
        part[...] = (begun[span, :] + weight_part(inputs, (grad_c, grad_r), weight, span)) * scale
        copies.append(pltpu.make_async_copy(part, out.at[pl.ds(n * tile, tile), :], sem))
        copies[n].start()
    for copy in copies[-2:]:
        copy.wait()


def weight_terms(begun, inputs, slots_c, slots_r, weight):
    inner, width = weight.shape
    tokens = inputs[0].shape[1]
    tile = min(256, inner)
    scale = np.float32(1.0) / np.sqrt(np.float32(2 * tokens))
    return pl.pallas_call(
        functools.partial(weight_kernel, len(slots_c), scale),
        in_specs=[HERE] * (4 + 2 * len(slots_c)),
        out_specs=ANYWHERE,
        out_shape=jax.ShapeDtypeStruct((inner, width), jnp.float32),
        scratch_shapes=[pltpu.VMEM((tokens, width), jnp.bfloat16)] * 2
        + [pltpu.VMEM((2, tile, width), jnp.float32), pltpu.SemaphoreType.DMA((2,))],
        compiler_params=pltpu.CompilerParams(vmem_limit_bytes=VMEM_LIMIT),
    )(begun, *inputs, *slots_c, *slots_r, weight)


def on_device(rows, cols, center, radius, grad_center, grad_radius, weight, active):
    chips, cores = col_split(cols)
    held = grad_center.shape[0]
    assert rows % 2 == 0 and center.shape[0] == PAIR * held
    ring = ring_of(rows)
    clockwise = [(ring[i], ring[(i + 1) % rows]) for i in range(rows)]
    counter = [(b, a) for a, b in clockwise]
    last = rows // 2

    def swap_cores(value, j):
        perm = [(i, i - i % cores + (i % cores + j) % cores) for i in range(cols)]
        return lax.ppermute(value, "col", perm)

    def hop_chips(value, k):
        return lax.ppermute(value, "col", [(i, (i + k * cores) % cols) for i in range(cols)])

    def summed(own, others, *done):
        if len(others) == 1:
            groups = [[k * cores + j for j in range(cores)] for k in range(chips)]
            parts = [lax.all_to_all(others[0], "col", 0, 0, axis_index_groups=groups, tiled=True)]
        else:
            parts = [swap_cores(part, n % cores) if n % cores else part for n, part in enumerate(others)]
        if done:
            parts, _ = lax.optimization_barrier((parts, done))
        own = [own[0]] + [swap_cores(own[j], j) for j in range(1, cores)]
        return own, coded_sums(chips, 2 * held, parts)

    def hopped(coded):
        return [hop_chips(value, k + 1) for k, value in enumerate(coded)]

    both = packed(center, radius)
    inputs = [both] + [hop_chips(both, -k) for k in range(1, chips)]
    slots_c, slots_r = {0: grad_center}, {0: grad_radius}
    shifts = by_distance(rows)
    first = shifts[:last]
    for step in range(1, last):
        if step == 3:
            heads = slots_c[2], slots_c[-2], slots_r[2], slots_r[-2]
            heads = lax.optimization_barrier(heads)
            slots_c[2], slots_c[-2], slots_r[2], slots_r[-2] = heads
            inputs, _ = lax.optimization_barrier((inputs, heads[0]))
            inputs = [stacked(inputs)]
            inputs += [swap_cores(inputs[0], -j) for j in range(1, cores)]
        for slots in (slots_c, slots_r):
            slots[step] = lax.ppermute(slots[step - 1], "row", clockwise)
            slots[-step] = lax.ppermute(slots[1 - step], "row", counter)
    nearer_c, nearer_r, further_c, further_r = turned(rows, cols, inputs)
    begun = first_weight_terms(
        (nearer_c, nearer_r), [slots_c[s] for s in first], [slots_r[s] for s in first], weight
    )
    slots_c[last - 1], begun = lax.optimization_barrier((slots_c[last - 1], begun))

    lasts = (
        lax.ppermute(slots_c[last - 1], "row", clockwise),
        lax.ppermute(slots_r[1 - last], "row", counter),
    )
    found = shifts[:-1]
    terms, orders = near_terms(
        rows, cols, held, found, [slots_c[s] for s in found], [slots_r[s] for s in found], weight
    )
    near_0, coded_0 = summed(terms[:-1], terms[-1:])
    lasts, coded_0 = lax.optimization_barrier((lasts, coded_0))
    far_0 = hopped(coded_0)
    terms = far_terms(rows, cols, orders, lasts, weight)
    near_1, coded_1 = summed(terms[:cores], terms[cores:], *far_0)
    far_1 = hopped(coded_1)
    rest = shifts[last:-1]
    weight_grad = weight_terms(
        begun,
        (further_c, further_r),
        [slots_c[s] for s in rest] + [lasts[0]],
        [slots_r[s] for s in rest] + [lasts[1]],
        weight,
    )
    return *gated(rows, cols, ((near_0, far_0), (near_1, far_1)), active), weight_grad


def solution(mesh):
    spec_in, spec_out, spec_weight = P("col", "row"), P("row", "col"), P("row", "col")
    return jax.shard_map(
        functools.partial(on_device, mesh.shape["row"], mesh.shape["col"]),
        mesh=mesh,
        in_specs=(spec_in, spec_in, spec_out, spec_out, spec_weight, spec_in),
        out_specs=(spec_in, spec_in, spec_weight),
        check_vma=False,
    )
```

time: 166 us -> 71.9 us (0.43)
  waiting for transfers between devices: 122 us -> 24 us
  starting transfers between devices: 0.12 us -> 21.8 us
  matrix products: 20.9 us -> 0 us
  Pallas kernels: 0 us -> 19.4 us
  between operations: 13.8 us -> 0.81 us
  other arithmetic: 8.6 us -> 0 us
  blocking collectives: 0 us -> 4.58 us
    all_gather x2 -> x0, waiting for transfers between devices: 88.5 us -> none  [the longest x1 75.8 us: on_device(): panels = lax.all_gather(stacked, 'row', axis=1, tiled=True)]
    reduce_scatter x1 -> x0, waiting for transfers between devices: 33.4 us -> none  [on_device(): lax.psum_scatter(partial_terms, 'col', scatter_dimension=1, tiled=True)]
    ppermute x0 -> x22, waiting for transfers between devices: none -> 24 us  [the longest x6 11 us: on_device(): slots[step] = lax.ppermute(slots[step - 1], 'row', clockwise)]
    ppermute x0 -> x22, starting transfers between devices: none -> 21.8 us  [the longest x6 12.7 us: on_device(): slots[step] = lax.ppermute(slots[step - 1], 'row', clockwise)]
    dot_general x4 -> x0, matrix products: 20.9 us -> none  [the longest x1 8.69 us: on_device(): lax.dot_general(inputs[1], panels[1], contract_tok, preferred_element_typ...]
    pallas_call x0 -> x10, Pallas kernels: none -> 19.4 us  [the longest x1 6.26 us: weight_terms(): pl.pallas_call(functools.partial(weight_kernel, len(slots_c), scale), in_...]
    another operation x3 -> x0, other arithmetic: 6.31 us -> none  [the longest x1 2.56 us: on_device(): partial_terms = jnp.stack((through_center, through_radius))]
    all_to_all x0 -> x1, blocking collectives: none -> 4.58 us  [summed(): lax.all_to_all(others[0], 'col', 0, 0, axis_index_groups=groups, tiled=True)]
  transfers between devices with their start and end apart: 3 -> 22, of which waited for: 3 -> 11; matrix products, arithmetic and copies ran while one was open for 15% -> 0% of each run, Pallas kernels for 0% -> 25%
where the time goes in v2:
time: 71.9 us; the launch traced here: 71.7 us
  waiting for transfers between devices  24 us (33%)
  starting transfers between devices  21.8 us (30%)
  Pallas kernels  19.4 us (27%)
  blocking collectives  4.58 us (6%)
  local copies, waits for them, and re-layouts  1.06 us (1%)
  between operations  0.81 us (1%)
    ppermute x6, starting transfers between devices, on_device(): slots[step] = lax.ppermute(slots[step - 1], 'row', clockwise)  12.7 us
    ppermute x6, waiting for transfers between devices, on_device(): slots[step] = lax.ppermute(slots[step - 1], 'row', clockwise)  11 us
    ppermute x6, waiting for transfers between devices, on_device(): slots[-step] = lax.ppermute(slots[1 - step], 'row', counter)  8.8 us
    pallas_call x1, Pallas kernels, weight_terms(): pl.pallas_call(functools.partial(weight_kernel, len(slots_c), scale), in_...  6.26 us
    ppermute x3, starting transfers between devices, hop_chips(): lax.ppermute(value, 'col', [(i, (i + k * cores) % cols) for i in range(co...  5.11 us
    all_to_all x1, blocking collectives, summed(): lax.all_to_all(others[0], 'col', 0, 0, axis_index_groups=groups, tiled=True)  4.58 us
    pallas_call x1, Pallas kernels, first_weight_terms(): pl.pallas_call(functools.partial(first_kernel, len(slots_c)), in_specs=[H...  3.52 us
    ppermute x3, waiting for transfers between devices, hop_chips(): lax.ppermute(value, 'col', [(i, (i + k * cores) % cols) for i in range(co...  3.3 us
  transfers between devices with their start and end apart: 22, of which 11 were waited for; matrix products, arithmetic and copies ran while one was open for 0% of the time, Pallas kernels for 25%

profile of v2, /device:TPU:0, one launch (start us, length us, event | category | flops | bytes accessed | tf_op | source)
XLA Modules:
  0.0 71.7 jit_solution(5020188502698727744)
XLA Ops:
  0.7 3.1 %collective-permute-start = (bf16[64,2048]{1,0:T(8,128)(2,1)}, bf16[64,2048]{1,0:T(8,128)(2,1)S(1)}, u32[]{:S(2)}, u32[]{:S(2)}) collective-permute-start(bf16[64,2048]{1,0:T(8,128)(2,1)} %refs_0_.1), channel_id=1, source_target_pairs={{0,8},{8,16},{16,24},{24,28},{28,20},{20,12},{12,4},{4,0},{1,9},{9... | collective-permute-start | bytes 786440 | tf_op jit(solution)/shard_map/ppermute | solution.py:419
  3.7 2.0 %collective-permute-start.4 = (bf16[64,2048]{1,0:T(8,128)(2,1)}, bf16[64,2048]{1,0:T(8,128)(2,1)S(1)}, u32[]{:S(2)}, u32[]{:S(2)}) collective-permute-start(bf16[64,2048]{1,0:T(8,128)(2,1)} %refs_7_.1), channel_id=1, source_target_pairs={{0,8},{8,16},{16,24},{24,28},{28,20},{20,12},{12,4},{4,0},{1,9},{9... | collective-permute-start | bytes 786440 | tf_op jit(solution)/shard_map/ppermute | solution.py:419
  5.8 1.8 %shard_map.85.refs_0_ = bf16[256,1024]{1,0:T(8,128)(2,1)} custom-call(bf16[128,1024]{1,0:T(8,128)(2,1)} %first.1, bf16[128,1024]{1,0:T(8,128)(2,1)} %second.1), custom_call_target="tpu_custom_call" | custom-call | tf_op jit(solution)/shard_map/pallas_call | solution.py:242
  7.6 2.0 %collective-permute-start.9 = (bf16[256,1024]{1,0:T(8,128)(2,1)}, bf16[256,1024]{1,0:T(8,128)(2,1)S(1)}, u32[]{:S(2)}, u32[]{:S(2)}) collective-permute-start(bf16[256,1024]{1,0:T(8,128)(2,1)} %shard_map.85.refs_0_), channel_id=1, source_target_pairs={{0,2},{1,3},{2,0},{3,1},{4,6},{5,7},{6,4},{7,5},{8,10},{9,11},{10,... | collective-permute-start | bytes 1572872 | tf_op jit(solution)/shard_map/ppermute | solution.py:389
  9.6 1.5 %collective-permute-done.refs_3_.refs_1_ = bf16[64,2048]{1,0:T(8,128)(2,1)S(1)} collective-permute-done((bf16[64,2048]{1,0:T(8,128)(2,1)}, bf16[64,2048]{1,0:T(8,128)(2,1)S(1)}, u32[]{:S(2)}, u32[]{:S(2)}) %collective-permute-start) | collective-permute-done | bytes 262176 | tf_op jit(solution)/shard_map/ppermute | solution.py:419
  11.0 2.1 %collective-permute-start.2 = (bf16[64,2048]{1,0:T(8,128)(2,1)S(1)}, bf16[64,2048]{1,0:T(8,128)(2,1)S(1)}, u32[]{:S(2)}, u32[]{:S(2)}) collective-permute-start(bf16[64,2048]{1,0:T(8,128)(2,1)S(1)} %collective-permute-done.refs_3_.refs_1_), channel_id=1, source_target_pairs={{0,8},{8,16},{16,24},{24,28},{28,20},{20,12},{12,4},{4,0},{1,9},{9... | collective-permute-start | bytes 786440 | tf_op jit(solution)/shard_map/ppermute | solution.py:419
  13.2 3.5 %collective-permute-done.4.refs_7_.refs_8_ = bf16[64,2048]{1,0:T(8,128)(2,1)S(1)} collective-permute-done((bf16[64,2048]{1,0:T(8,128)(2,1)}, bf16[64,2048]{1,0:T(8,128)(2,1)S(1)}, u32[]{:S(2)}, u32[]{:S(2)}) %collective-permute-start.4) | collective-permute-done | bytes 262176 | tf_op jit(solution)/shard_map/ppermute | solution.py:419
  16.6 2.1 %collective-permute-start.5 = (bf16[64,2048]{1,0:T(8,128)(2,1)S(1)}, bf16[64,2048]{1,0:T(8,128)(2,1)S(1)}, u32[]{:S(2)}, u32[]{:S(2)}) collective-permute-start(bf16[64,2048]{1,0:T(8,128)(2,1)S(1)} %collective-permute-done.4.refs_7_.refs_8_), channel_id=1, source_target_pairs={{0,8},{8,16},{16,24},{24,28},{28,20},{20,12},{12,4},{4,0},{1,9},{9... | collective-permute-start | bytes 786440 | tf_op jit(solution)/shard_map/ppermute | solution.py:419
  18.8 3.5 %collective-permute-done.2.refs_5_.refs_3_ = bf16[64,2048]{1,0:T(8,128)(2,1)S(1)} collective-permute-done((bf16[64,2048]{1,0:T(8,128)(2,1)S(1)}, bf16[64,2048]{1,0:T(8,128)(2,1)S(1)}, u32[]{:S(2)}, u32[]{:S(2)}) %collective-permute-start.2) | collective-permute-done | bytes 262176 | tf_op jit(solution)/shard_map/ppermute | solution.py:419
  22.2 2.2 %collective-permute-done.3.refs_4_.refs_2_ = bf16[64,2048]{1,0:T(8,128)(2,1)S(1)} collective-permute-done((bf16[64,2048]{1,0:T(8,128)(2,1)S(1)}, bf16[64,2048]{1,0:T(8,128)(2,1)S(1)}, u32[]{:S(2)}, u32[]{:S(2)}) %collective-permute-start.3) | collective-permute-done | bytes 262176 | tf_op jit(solution)/shard_map/ppermute | solution.py:420
  24.4 2.6 %collective-permute-done.5.refs_9_.refs_10_ = bf16[64,2048]{1,0:T(8,128)(2,1)S(1)} collective-permute-done((bf16[64,2048]{1,0:T(8,128)(2,1)S(1)}, bf16[64,2048]{1,0:T(8,128)(2,1)S(1)}, u32[]{:S(2)}, u32[]{:S(2)}) %collective-permute-start.5) | collective-permute-done | bytes 262176 | tf_op jit(solution)/shard_map/ppermute | solution.py:419
  27.0 1.5 %collective-permute-done.7.refs_11_.refs_6_ = bf16[64,2048]{1,0:T(8,128)(2,1)S(1)} collective-permute-done((bf16[64,2048]{1,0:T(8,128)(2,1)S(1)}, bf16[64,2048]{1,0:T(8,128)(2,1)S(1)}, u32[]{:S(2)}, u32[]{:S(2)}) %collective-permute-start.7) | collective-permute-done | bytes 262176 | tf_op jit(solution)/shard_map/ppermute | solution.py:420
  28.6 1.0 %copy-done.1 = bf16[256,1024]{1,0:T(8,128)(2,1)S(1)} copy-done((bf16[256,1024]{1,0:T(8,128)(2,1)S(1)}, bf16[256,1024]{1,0:T(8,128)(2,1)}, u32[]{:S(2)}) %copy-start.1) | copy-done | bytes 524312
  30.1 1.7 %collective-permute-start.8 = (bf16[64,2048]{1,0:T(8,128)(2,1)S(1)}, bf16[64,2048]{1,0:T(8,128)(2,1)S(1)}, u32[]{:S(2)}, u32[]{:S(2)}) collective-permute-start(bf16[64,2048]{1,0:T(8,128)(2,1)S(1)} %collective-permute-done.2.refs_5_.refs_3_), channel_id=1, source_target_pairs={{0,8},{8,16},{16,24},{24,28},{28,20},{20,12},{12,4},{4,0},{1,9},{9... | collective-permute-start | bytes 786440 | tf_op jit(solution)/shard_map/ppermute | solution.py:419
  32.1 1.7 %collective-permute-start.12 = (bf16[64,2048]{1,0:T(8,128)(2,1)S(1)}, bf16[64,2048]{1,0:T(8,128)(2,1)S(1)}, u32[]{:S(2)}, u32[]{:S(2)}) collective-permute-start(bf16[64,2048]{1,0:T(8,128)(2,1)S(1)} %collective-permute-done.5.refs_9_.refs_10_), channel_id=1, source_target_pairs={{0,8},{8,16},{16,24},{24,28},{28,20},{20,12},{12,4},{4,0},{1,9},{9... | collective-permute-start | bytes 786440 | tf_op jit(solution)/shard_map/ppermute | solution.py:419
  33.9 5.1 %collective-permute-done.13.refs_13_.refs_8_ = bf16[64,2048]{1,0:T(8,128)(2,1)S(1)} collective-permute-done((bf16[64,2048]{1,0:T(8,128)(2,1)S(1)}, bf16[64,2048]{1,0:T(8,128)(2,1)S(1)}, u32[]{:S(2)}, u32[]{:S(2)}) %collective-permute-start.13) | collective-permute-done | bytes 262176 | tf_op jit(solution)/shard_map/ppermute | solution.py:420
  39.2 0.7 shard_map.87
  40.0 3.5 %shard_map.88.begun = f32[1024,2048]{1,0:T(8,128)S(1)} custom-call(bf16[1024,256]{1,0:T(8,128)(2,1)S(1)} %get-tuple-element.39.refs_0_, bf16[1024,256]{1,0:T(8,128)(2,1)S(1)} %get-tuple-element.40.refs_1_, bf16[64,2048]{1,0:T(8,128)(2,1)S(1)} %copy-done.2, bf16[64,2048]{1,0:T(8,128)(2,1)S(1)} %collective-permute-done.refs_3_.refs_1_, ...), custom_call_target="tpu_custom_call" | custom-call | tf_op jit(solution)/shard_map/pallas_call | solution.py:331
  43.5 1.8 %collective-permute-start.15 = (bf16[64,2048]{1,0:T(8,128)(2,1)S(1)}, bf16[64,2048]{1,0:T(8,128)(2,1)S(1)}, u32[]{:S(2)}, u32[]{:S(2)}) collective-permute-start(bf16[64,2048]{1,0:T(8,128)(2,1)S(1)} %collective-permute-done.8.refs_5_.refs_3_), channel_id=1, source_target_pairs={{0,8},{8,16},{16,24},{24,28},{28,20},{20,12},{12,4},{4,0},{1,9},{9... | collective-permute-start | bytes 786440 | tf_op jit(solution)/shard_map/ppermute | solution.py:428
  45.3 2.6 %shard_map.89 = (f32[128,1024]{1,0:T(8,128)S(1)}, f32[128,1024]{1,0:T(8,128)S(1)}, f32[2,1,128,1024]{3,2,1,0:T(8,128)S(1)}, bf16[512,2048]{1,0:T(8,128)(2,1)S(1)}, bf16[512,2048]{1,0:T(8,128)(2,1)S(1)}) custom-call(bf16[64,2048]{1,0:T(8,128)(2,1)S(1)} %copy-done.2, bf16[64,2048]{1,0:T(8,128)(2,1)S(1)} %collective-permute-done.refs_3_.refs_1_, ...), custom_call_target="tpu_custom_call" | custom-call | tf_op jit(solution)/shard_map/pallas_call | solution.py:109
  47.9 4.6 %all_to_all.5.refs_0_ = f32[2,1,128,1024]{3,2,1,0:T(8,128)S(1)} all-to-all(f32[2,1,128,1024]{3,2,1,0:T(8,128)S(1)} %get-tuple-element.46), channel_id=1, replica_groups={{0,1},{2,3},{4,5},{6,7},{8,9},{10,11},{12,13},{14,15},{16,17},{18,19},{..., dimensions={0} | all-to-all | bytes 2097152 | tf_op jit(solution)/shard_map/all_to_all | solution.py:394
  52.7 1.6 %collective-permute-start.17 = (s16[128,1152]{1,0:T(8,128)(2,1)S(1)}, s16[128,1152]{1,0:T(8,128)(2,1)S(1)}, u32[]{:S(2)}, u32[]{:S(2)}) collective-permute-start(s16[128,1152]{1,0:T(8,128)(2,1)S(1)} %shard_map.90), channel_id=1, source_target_pairs={{0,2},{1,3},{2,0},{3,1},{4,6},{5,7},{6,4},{7,5},{8,10},{9,11},{10,... | collective-permute-start | bytes 884744 | tf_op jit(solution)/shard_map/ppermute | solution.py:389
  54.2 2.8 %shard_map.91 = (f32[128,1024]{1,0:T(8,128)S(1)}, f32[128,1024]{1,0:T(8,128)S(1)}, f32[1,1,64,1024]{3,2,1,0:T(8,128)S(1)}, f32[1,1,64,1024]{3,2,1,0:T(8,128)S(1)...) custom-call(bf16[512,2048]{1,0:T(8,128)(2,1)S(1)} %get-tuple-element.48.refs_0_, ...), custom_call_target="tpu_custom_call" | custom-call | tf_op jit(solution)/shard_map/pallas_call | solution.py:139
  57.2 0.5 collective-permute-start.20
  57.7 0.4 collective-permute-start.18
  58.2 0.5 collective-permute-done.19.refs_1_
  58.7 0.4 collective-permute-done.20.refs_3_
  59.0 2.8 %collective-permute-done.17.refs_2_ = s16[128,1152]{1,0:T(8,128)(2,1)S(1)} collective-permute-done((s16[128,1152]{1,0:T(8,128)(2,1)S(1)}, s16[128,1152]{1,0:T(8,128)(2,1)S(1)}, u32[]{:S(2)}, u32[]{:S(2)}) %collective-permute-start.17) | collective-permute-done | bytes 294944 | tf_op jit(solution)/shard_map/ppermute | solution.py:389
  62.1 1.6 %collective-permute-start.21 = (s16[128,1152]{1,0:T(8,128)(2,1)S(1)}, s16[128,1152]{1,0:T(8,128)(2,1)S(1)}, u32[]{:S(2)}, u32[]{:S(2)}) collective-permute-start(s16[128,1152]{1,0:T(8,128)(2,1)S(1)} %shard_map.92), channel_id=1, source_target_pairs={{0,2},{1,3},{2,0},{3,1},{4,6},{5,7},{6,4},{7,5},{8,10},{9,11},{10,... | collective-permute-start | bytes 884744 | tf_op jit(solution)/shard_map/ppermute | solution.py:389
  63.6 6.3 %shard_map.94 = f32[1024,2048]{1,0:T(8,128)} custom-call(f32[1024,2048]{1,0:T(8,128)S(1)} %shard_map.88.begun, bf16[1024,256]{1,0:T(8,128)(2,1)S(1)} %get-tuple-element.65.refs_0_, bf16[1024,256]{1,0:T(8,128)(2,1)S(1)} %get-tuple-element.66.refs_1_, bf16[64,2048]{1,0:T(8,128)(2,1)S(1)} %collective-permute-done.3.refs_4_.refs_2_, ...), custom_call_target="tpu_custom_call" | custom-call | tf_op jit(solution)/shard_map/pallas_call | solution.py:364
  69.9 0.5 collective-permute-done.21.refs_5_
  70.4 1.3 %shard_map.93 = (f32[128,1024]{1,0:T(8,128)}, f32[128,1024]{1,0:T(8,128)}) custom-call(f32[128,1024]{1,0:T(8,128)S(1)} %get-tuple-element.44.refs_0_, f32[128,1024]{1,0:T(8,128)S(1)} %collective-permute-done.14.refs_1_, s16[128,1152]{1,0:T(8,128)(2,1)S(1)} %collective-permute-done.17.refs_2_, f32[128,1024]{1,0:T(8,128)S(1)} %get-tuple-element.52.refs_3_, ...), custom_call_target="tpu_custom_call" | custom-call | tf_op jit(solution)/shard_map/pallas_call | solution.py:211
  (33 shorter events, 1.8 us)
Async XLA Ops:
  0.6 39.3 %copy-start.2 = (bf16[64,2048]{1,0:T(8,128)(2,1)S(1)}, bf16[64,2048]{1,0:T(8,128)(2,1)}, u32[]{:S(2)}) copy-start(bf16[64,2048]{1,0:T(8,128)(2,1)} %refs_0_.1) | copy-start | bytes 786436
  0.6 39.3 %copy-start.3 = (bf16[64,2048]{1,0:T(8,128)(2,1)S(1)}, bf16[64,2048]{1,0:T(8,128)(2,1)}, u32[]{:S(2)}) copy-start(bf16[64,2048]{1,0:T(8,128)(2,1)} %refs_7_.1) | copy-start | bytes 786436
  0.7 10.4 %collective-permute-start = (bf16[64,2048]{1,0:T(8,128)(2,1)}, bf16[64,2048]{1,0:T(8,128)(2,1)S(1)}, u32[]{:S(2)}, u32[]{:S(2)}) collective-permute-start(bf16[64,2048]{1,0:T(8,128)(2,1)} %refs_0_.1), channel_id=1, source_target_pairs={{0,8},{8,16},{16,24},{24,28},{28,20},{20,12},{12,4},{4,0},{1,9},{9... | collective-permute-start | bytes 786440 | tf_op jit(solution)/shard_map/ppermute | solution.py:419
  3.7 9.4 %collective-permute-start.1 = (bf16[64,2048]{1,0:T(8,128)(2,1)}, bf16[64,2048]{1,0:T(8,128)(2,1)S(1)}, u32[]{:S(2)}, u32[]{:S(2)}) collective-permute-start(bf16[64,2048]{1,0:T(8,128)(2,1)} %refs_0_.1), channel_id=1, source_target_pairs={{8,0},{16,8},{24,16},{28,24},{20,28},{12,20},{4,12},{0,4},{9,1},{1... | collective-permute-start | bytes 786440 | tf_op jit(solution)/shard_map/ppermute | solution.py:420
  3.7 12.9 %collective-permute-start.4 = (bf16[64,2048]{1,0:T(8,128)(2,1)}, bf16[64,2048]{1,0:T(8,128)(2,1)S(1)}, u32[]{:S(2)}, u32[]{:S(2)}) collective-permute-start(bf16[64,2048]{1,0:T(8,128)(2,1)} %refs_7_.1), channel_id=1, source_target_pairs={{0,8},{8,16},{16,24},{24,28},{28,20},{20,12},{12,4},{4,0},{1,9},{9... | collective-permute-start | bytes 786440 | tf_op jit(solution)/shard_map/ppermute | solution.py:419
  5.8 13.0 %collective-permute-start.6 = (bf16[64,2048]{1,0:T(8,128)(2,1)}, bf16[64,2048]{1,0:T(8,128)(2,1)S(1)}, u32[]{:S(2)}, u32[]{:S(2)}) collective-permute-start(bf16[64,2048]{1,0:T(8,128)(2,1)} %refs_7_.1), channel_id=1, source_target_pairs={{8,0},{16,8},{24,16},{28,24},{20,28},{12,20},{4,12},{0,4},{9,1},{1... | collective-permute-start | bytes 786440 | tf_op jit(solution)/shard_map/ppermute | solution.py:420
  7.5 32.4 %copy-start = (bf16[1024,2048]{1,0:T(8,128)(2,1)S(1)}, bf16[1024,2048]{1,0:T(8,128)(2,1)}, u32[]{:S(2)}) copy-start(bf16[1024,2048]{1,0:T(8,128)(2,1)} %refs_10_.3) | copy-start | bytes 12582916
  7.6 21.0 %collective-permute-start.9 = (bf16[256,1024]{1,0:T(8,128)(2,1)}, bf16[256,1024]{1,0:T(8,128)(2,1)S(1)}, u32[]{:S(2)}, u32[]{:S(2)}) collective-permute-start(bf16[256,1024]{1,0:T(8,128)(2,1)} %shard_map.85.refs_0_), channel_id=1, source_target_pairs={{0,2},{1,3},{2,0},{3,1},{4,6},{5,7},{6,4},{7,5},{8,10},{9,11},{10,... | collective-permute-start | bytes 1572872 | tf_op jit(solution)/shard_map/ppermute | solution.py:389
  11.0 11.2 %collective-permute-start.2 = (bf16[64,2048]{1,0:T(8,128)(2,1)S(1)}, bf16[64,2048]{1,0:T(8,128)(2,1)S(1)}, u32[]{:S(2)}, u32[]{:S(2)}) collective-permute-start(bf16[64,2048]{1,0:T(8,128)(2,1)S(1)} %collective-permute-done.refs_3_.refs_1_), channel_id=1, source_target_pairs={{0,8},{8,16},{16,24},{24,28},{28,20},{20,12},{12,4},{4,0},{1,9},{9... | collective-permute-start | bytes 786440 | tf_op jit(solution)/shard_map/ppermute | solution.py:419
  13.2 11.2 %collective-permute-start.3 = (bf16[64,2048]{1,0:T(8,128)(2,1)S(1)}, bf16[64,2048]{1,0:T(8,128)(2,1)S(1)}, u32[]{:S(2)}, u32[]{:S(2)}) collective-permute-start(bf16[64,2048]{1,0:T(8,128)(2,1)S(1)} %collective-permute-done.1.refs_4_.refs_2_), channel_id=1, source_target_pairs={{8,0},{16,8},{24,16},{28,24},{20,28},{12,20},{4,12},{0,4},{9,1},{1... | collective-permute-start | bytes 786440 | tf_op jit(solution)/shard_map/ppermute | solution.py:420
  16.6 10.4 %collective-permute-start.5 = (bf16[64,2048]{1,0:T(8,128)(2,1)S(1)}, bf16[64,2048]{1,0:T(8,128)(2,1)S(1)}, u32[]{:S(2)}, u32[]{:S(2)}) collective-permute-start(bf16[64,2048]{1,0:T(8,128)(2,1)S(1)} %collective-permute-done.4.refs_7_.refs_8_), channel_id=1, source_target_pairs={{0,8},{8,16},{16,24},{24,28},{28,20},{20,12},{12,4},{4,0},{1,9},{9... | collective-permute-start | bytes 786440 | tf_op jit(solution)/shard_map/ppermute | solution.py:419
  18.8 9.8 %collective-permute-start.7 = (bf16[64,2048]{1,0:T(8,128)(2,1)S(1)}, bf16[64,2048]{1,0:T(8,128)(2,1)S(1)}, u32[]{:S(2)}, u32[]{:S(2)}) collective-permute-start(bf16[64,2048]{1,0:T(8,128)(2,1)S(1)} %collective-permute-done.6.refs_8_.refs_9_), channel_id=1, source_target_pairs={{8,0},{16,8},{24,16},{28,24},{20,28},{12,20},{4,12},{0,4},{9,1},{1... | collective-permute-start | bytes 786440 | tf_op jit(solution)/shard_map/ppermute | solution.py:420
  28.6 1.0 %copy-start.1 = (bf16[256,1024]{1,0:T(8,128)(2,1)S(1)}, bf16[256,1024]{1,0:T(8,128)(2,1)}, u32[]{:S(2)}) copy-start(bf16[256,1024]{1,0:T(8,128)(2,1)} %shard_map.85.refs_0_) | copy-start | bytes 1572868
  29.7 9.6 %collective-permute-start.10 = (bf16[512,1024]{1,0:T(8,128)(2,1)S(1)}, bf16[512,1024]{1,0:T(8,128)(2,1)S(1)}, u32[]{:S(2)}, u32[]{:S(2)}) collective-permute-start(bf16[512,1024]{1,0:T(8,128)(2,1)S(1)} %shard_map.86.refs_0_), channel_id=1, source_target_pairs={{0,1},{1,0},{2,3},{3,2},{4,5},{5,4},{6,7},{7,6},{8,9},{9,8},{10,11... | collective-permute-start | bytes 3145736 | tf_op jit(solution)/shard_map/ppermute | solution.py:386
  29.8 9.2 %collective-permute-start.13 = (bf16[64,2048]{1,0:T(8,128)(2,1)S(1)}, bf16[64,2048]{1,0:T(8,128)(2,1)S(1)}, u32[]{:S(2)}, u32[]{:S(2)}) collective-permute-start(bf16[64,2048]{1,0:T(8,128)(2,1)S(1)} %collective-permute-done.7.refs_11_.refs_6_), channel_id=1, source_target_pairs={{8,0},{16,8},{24,16},{28,24},{20,28},{12,20},{4,12},{0,4},{9,1},{1... | collective-permute-start | bytes 786440 | tf_op jit(solution)/shard_map/ppermute | solution.py:420
  30.1 13.4 %collective-permute-start.8 = (bf16[64,2048]{1,0:T(8,128)(2,1)S(1)}, bf16[64,2048]{1,0:T(8,128)(2,1)S(1)}, u32[]{:S(2)}, u32[]{:S(2)}) collective-permute-start(bf16[64,2048]{1,0:T(8,128)(2,1)S(1)} %collective-permute-done.2.refs_5_.refs_3_), channel_id=1, source_target_pairs={{0,8},{8,16},{16,24},{24,28},{28,20},{20,12},{12,4},{4,0},{1,9},{9... | collective-permute-start | bytes 786440 | tf_op jit(solution)/shard_map/ppermute | solution.py:419
  31.8 13.4 %collective-permute-start.11 = (bf16[64,2048]{1,0:T(8,128)(2,1)S(1)}, bf16[64,2048]{1,0:T(8,128)(2,1)S(1)}, u32[]{:S(2)}, u32[]{:S(2)}) collective-permute-start(bf16[64,2048]{1,0:T(8,128)(2,1)S(1)} %collective-permute-done.3.refs_4_.refs_2_), channel_id=1, source_target_pairs={{8,0},{16,8},{24,16},{28,24},{20,28},{12,20},{4,12},{0,4},{9,1},{1... | collective-permute-start | bytes 786440 | tf_op jit(solution)/shard_map/ppermute | solution.py:420
  32.1 13.1 %collective-permute-start.12 = (bf16[64,2048]{1,0:T(8,128)(2,1)S(1)}, bf16[64,2048]{1,0:T(8,128)(2,1)S(1)}, u32[]{:S(2)}, u32[]{:S(2)}) collective-permute-start(bf16[64,2048]{1,0:T(8,128)(2,1)S(1)} %collective-permute-done.5.refs_9_.refs_10_), channel_id=1, source_target_pairs={{0,8},{8,16},{16,24},{24,28},{28,20},{20,12},{12,4},{4,0},{1,9},{9... | collective-permute-start | bytes 786440 | tf_op jit(solution)/shard_map/ppermute | solution.py:419
  38.9 13.7 %collective-permute-start.16 = (bf16[64,2048]{1,0:T(8,128)(2,1)S(1)}, bf16[64,2048]{1,0:T(8,128)(2,1)S(1)}, u32[]{:S(2)}, u32[]{:S(2)}) collective-permute-start(bf16[64,2048]{1,0:T(8,128)(2,1)S(1)} %collective-permute-done.13.refs_13_.refs_8_), channel_id=1, source_target_pairs={{8,0},{16,8},{24,16},{28,24},{20,28},{12,20},{4,12},{0,4},{9,1},{1... | collective-permute-start | bytes 786440 | tf_op jit(solution)/shard_map/ppermute | solution.py:429
  43.5 9.2 %collective-permute-start.15 = (bf16[64,2048]{1,0:T(8,128)(2,1)S(1)}, bf16[64,2048]{1,0:T(8,128)(2,1)S(1)}, u32[]{:S(2)}, u32[]{:S(2)}) collective-permute-start(bf16[64,2048]{1,0:T(8,128)(2,1)S(1)} %collective-permute-done.8.refs_5_.refs_3_), channel_id=1, source_target_pairs={{0,8},{8,16},{16,24},{24,28},{28,20},{20,12},{12,4},{4,0},{1,9},{9... | collective-permute-start | bytes 786440 | tf_op jit(solution)/shard_map/ppermute | solution.py:428
  52.7 9.2 %collective-permute-start.17 = (s16[128,1152]{1,0:T(8,128)(2,1)S(1)}, s16[128,1152]{1,0:T(8,128)(2,1)S(1)}, u32[]{:S(2)}, u32[]{:S(2)}) collective-permute-start(s16[128,1152]{1,0:T(8,128)(2,1)S(1)} %shard_map.90), channel_id=1, source_target_pairs={{0,2},{1,3},{2,0},{3,1},{4,6},{5,7},{6,4},{7,5},{8,10},{9,11},{10,... | collective-permute-start | bytes 884744 | tf_op jit(solution)/shard_map/ppermute | solution.py:389
  57.1 1.6 %collective-permute-start.19 = (f32[1,1,64,1024]{3,2,1,0:T(8,128)S(1)}, f32[1,1,64,1024]{3,2,1,0:T(8,128)S(1)}, u32[]{:S(2)}, u32[]{:S(2)}) collective-permute-start(f32[1,1,64,1024]{3,2,1,0:T(8,128)S(1)} %get-tuple-element.55), channel_id=1, source_target_pairs={{0,1},{1,0},{2,3},{3,2},{4,5},{5,4},{6,7},{7,6},{8,9},{9,8},{10,11... | collective-permute-start | bytes 786440 | tf_op jit(solution)/shard_map/ppermute | solution.py:386
  57.2 1.9 %collective-permute-start.20 = (f32[1,1,64,1024]{3,2,1,0:T(8,128)S(1)}, f32[1,1,64,1024]{3,2,1,0:T(8,128)S(1)}, u32[]{:S(2)}, u32[]{:S(2)}) collective-permute-start(f32[1,1,64,1024]{3,2,1,0:T(8,128)S(1)} %get-tuple-element.57), channel_id=1, source_target_pairs={{0,1},{1,0},{2,3},{3,2},{4,5},{5,4},{6,7},{7,6},{8,9},{9,8},{10,11... | collective-permute-start | bytes 786440 | tf_op jit(solution)/shard_map/ppermute | solution.py:386
  57.6 12.2 %collective-permute-start.14 = (f32[128,1024]{1,0:T(8,128)S(1)}, f32[128,1024]{1,0:T(8,128)S(1)}, u32[]{:S(2)}, u32[]{:S(2)}) collective-permute-start(f32[128,1024]{1,0:T(8,128)S(1)} %get-tuple-element.45), channel_id=1, source_target_pairs={{0,1},{1,0},{2,3},{3,2},{4,5},{5,4},{6,7},{7,6},{8,9},{9,8},{10,11... | collective-permute-start | bytes 1572872 | tf_op jit(solution)/shard_map/ppermute | solution.py:386
  57.7 12.2 %collective-permute-start.18 = (f32[128,1024]{1,0:T(8,128)S(1)}, f32[128,1024]{1,0:T(8,128)S(1)}, u32[]{:S(2)}, u32[]{:S(2)}) collective-permute-start(f32[128,1024]{1,0:T(8,128)S(1)} %get-tuple-element.53), channel_id=1, source_target_pairs={{0,1},{1,0},{2,3},{3,2},{4,5},{5,4},{6,7},{7,6},{8,9},{9,8},{10,11... | collective-permute-start | bytes 1572872 | tf_op jit(solution)/shard_map/ppermute | solution.py:386
  62.1 8.3 %collective-permute-start.21 = (s16[128,1152]{1,0:T(8,128)(2,1)S(1)}, s16[128,1152]{1,0:T(8,128)(2,1)S(1)}, u32[]{:S(2)}, u32[]{:S(2)}) collective-permute-start(s16[128,1152]{1,0:T(8,128)(2,1)S(1)} %shard_map.92), channel_id=1, source_target_pairs={{0,2},{1,3},{2,0},{3,1},{4,6},{5,7},{6,4},{7,5},{8,10},{9,11},{10,... | collective-permute-start | bytes 884744 | tf_op jit(solution)/shard_map/ppermute | solution.py:389
  63.6 6.8 %copy-start.4 = (s32[128,1024]{1,0:T(8,128)S(1)}, s32[128,1024]{1,0:T(8,128)}, u32[]{:S(2)}) copy-start(s32[128,1024]{1,0:T(8,128)} %refs_6_.3) | copy-start | bytes 1572868

commit v3 on v2

v3 whole, which is shorter than its diff:
```python
import functools

import jax
import jax.numpy as jnp
import numpy as np
from jax import lax
from jax.experimental import pallas as pl
from jax.experimental.pallas import tpu as pltpu
from jax.sharding import PartitionSpec as P

VMEM_LIMIT = 24 * 1024 * 1024
VMEM_MOST = 60 * 1024 * 1024
HERE = pl.BlockSpec(memory_space=pltpu.VMEM)
LANES = 128
LEVELS = np.float32(32000)
TINY = np.float32(2.0**-100)
ANYWHERE = pl.BlockSpec(memory_space=pl.ANY)
BY_LAST = (((1,), (1,)), ((), ()))
BY_TOKEN = (((1,), (0,)), ((), ()))
PAIR = 2


def ring_of(rows):
    return list(range(0, rows, PAIR)) + list(range(rows - 1, 0, -PAIR))


def on_ring(row, rows):
    return lax.select(lax.rem(row, PAIR) == 0, lax.div(row, PAIR), rows - 1 - lax.div(row, PAIR))


def off_ring(place, rows):
    return lax.select(place < rows // PAIR, PAIR * place, PAIR * (rows - place) - 1)


def apart(a, b, rows):
    ahead = lax.rem(a - b + rows, rows)
    return lax.min(ahead, rows - ahead)


def by_distance(rows):
    return [0] + [way * step for step in range(1, rows // 2) for way in (1, -1)] + [rows // 2]


def col_split(cols):
    return (cols // 2, 2) if cols % 2 == 0 else (cols, 1)


def spot(rows, cols, shift):
    chips, cores = col_split(cols)
    here, col = on_ring(lax.axis_index("row"), rows), lax.axis_index("col")
    x, core = lax.div(col, cores), lax.rem(col, cores)
    place = lax.rem(here + (rows - shift) % rows, rows)
    source = off_ring(place, rows)
    owner, half = lax.div(source, PAIR), lax.rem(source, PAIR)
    away = lax.rem(lax.rem(owner, cores) + cores - core, cores)
    piece = away * chips + lax.rem(lax.div(owner, cores) + chips - x, chips)
    return piece, half, abs(shift) > apart(here, rows - 1 - place, rows)


def row_of(rows, cols, shift, held):
    piece, _, far = spot(rows, cols, shift)
    return pl.multiple_of((lax.select(far, cols, 0) + piece) * held, held)


def terms_of(lhs, weight, outs, kind):
    cores, chips = len(outs) // 2, outs[-1].shape[0] + 1
    inner = weight.shape[0]
    tile = min(256, inner)
    held = lhs.shape[0] // (cores * chips)
    rows = slice(kind * held, (kind + 1) * held)
    for i in range(inner // tile):
        span = slice(i * tile, (i + 1) * tile)
        terms = lax.dot_general(
            lhs, weight[span, :], BY_LAST, preferred_element_type=jnp.float32
        )
        for n in range(cores * chips):
            core, chip = divmod(n, chips)
            part = terms[n * held : (n + 1) * held, :]
            if chip:
                outs[cores + core][chip - 1, rows, span] = part
            else:
                outs[core][rows, span] = part


def terms_shapes(cols, held, inner):
    chips, cores = col_split(cols)
    return [jax.ShapeDtypeStruct((2 * held, inner), jnp.float32)] * cores + [
        jax.ShapeDtypeStruct((chips - 1, 2 * held, inner), jnp.float32)
    ] * cores


def near_kernel(rows, cols, shifts, *refs):
    count = len(shifts)
    slots, weights, outs, orders = refs[: 2 * count], refs[2 * count : 2 * count + 2], refs[2 * count + 2 : -2], refs[-2:]
    held = slots[0].shape[0]
    for n, shift in enumerate(shifts):
        start = row_of(rows, cols, shift, held)
        for kind, order in enumerate(orders):
            order[pl.ds(start, held), :] = slots[kind * count + n][...]
    for kind, (order, weight) in enumerate(zip(orders, weights)):
        terms_of(order[: cols * held, :], weight, outs, kind)


def near_terms(rows, cols, shifts, slots_c, slots_r, weights):
    inner, width = weights[0].shape
    held = slots_c[0].shape[0]
    shapes = terms_shapes(cols, held, inner)
    found = pl.pallas_call(
        functools.partial(near_kernel, rows, cols, shifts),
        in_specs=[HERE] * (2 * len(shifts) + 2),
        out_specs=[HERE] * (len(shapes) + 2),
        out_shape=shapes + [jax.ShapeDtypeStruct((held * rows, width), jnp.bfloat16)] * 2,
        compiler_params=pltpu.CompilerParams(vmem_limit_bytes=VMEM_LIMIT),
    )(*slots_c, *slots_r, *weights)
    return found[:-2], found[-2:]


def far_kernel(rows, cols, *refs):
    lasts, weights, outs, orders = refs[2:4], refs[4:6], refs[6:-2], refs[-2:]
    held = lasts[0].shape[0]
    start = row_of(rows, cols, rows // 2, held)
    for kind, (order, last, weight) in enumerate(zip(orders, lasts, weights)):
        order[pl.ds(start, held), :] = last[...]
        terms_of(order[cols * held :, :], weight, outs, kind)


def far_terms(rows, cols, orders, lasts, weights):
    shapes = terms_shapes(cols, lasts[0].shape[0], weights[0].shape[0])
    found = pl.pallas_call(
        functools.partial(far_kernel, rows, cols),
        in_specs=[HERE] * 6,
        out_specs=[HERE] * (len(shapes) + 2),
        out_shape=shapes + [jax.ShapeDtypeStruct(order.shape, order.dtype) for order in orders],
        input_output_aliases={0: len(shapes), 1: len(shapes) + 1},
        compiler_params=pltpu.CompilerParams(vmem_limit_bytes=VMEM_LIMIT),
    )(*orders, *lasts, *weights)
    return found[:-2], found[-2:]


def sum_kernel(count, *refs):
    parts, outs = refs[:count], refs[count:]
    rows, width = parts[0].shape[1:]
    for k, out in enumerate(outs):
        total = parts[0][k]
        for part in parts[1:]:
            total = total + part[k]
        most = jnp.max(jnp.abs(total), axis=1, keepdims=True)
        exponent = jnp.ceil(jnp.log2(jnp.maximum(most, TINY)) + 1e-3)
        coded = jnp.round(total * (LEVELS / jnp.exp2(exponent)))
        out[:, :width] = coded.astype(jnp.int16)
        out[:, width:] = jnp.broadcast_to(exponent, (rows, LANES)).astype(jnp.int16)


def coded_sums(parts):
    others, rows, width = parts[0].shape
    return pl.pallas_call(
        functools.partial(sum_kernel, len(parts)),
        in_specs=[HERE] * len(parts),
        out_specs=[HERE] * others,
        out_shape=[jax.ShapeDtypeStruct((rows, width + LANES), jnp.int16)] * others,
        compiler_params=pltpu.CompilerParams(vmem_limit_bytes=VMEM_LIMIT),
    )(*parts)


def gate_kernel(rows, cols, near, far, *refs):
    rounds, (active, *outs) = refs[:-3], refs[-3:]
    rounds = rounds[: near + far], rounds[near + far :]
    held = active.shape[0] // PAIR
    width = active.shape[1]
    here, col = on_ring(lax.axis_index("row"), rows), lax.axis_index("col")
    first = apart(here, on_ring(PAIR * col, rows), rows)
    second = apart(here, on_ring(PAIR * col + 1, rows), rows)
    halves = lax.select(first < second, 0, 1), lax.select(first < second, 1, 0)
    for half, parts in zip(halves, rounds):
        span = pl.ds(pl.multiple_of(half * held, held), held)
        gate = active[span, :].astype(jnp.float32)
        for n, out in enumerate(outs):
            mine = slice(n * held, (n + 1) * held)
            total = parts[0][mine, :]
            for part in parts[1:near]:
                total = total + part[mine, :]
            for part in parts[near:]:
                exponent = part[mine, width : width + 1].astype(jnp.float32)
                total = total + part[mine, :width].astype(jnp.float32) * (
                    jnp.exp2(exponent) / LEVELS
                )
            out[span, :] = gate * total


def gated(rows, cols, rounds, active):
    near, far = rounds[0]
    parts = [part for found in rounds for kind in found for part in kind]
    size = active.size
    return pl.pallas_call(
        functools.partial(gate_kernel, rows, cols, len(near), len(far)),
        in_specs=[HERE] * (len(parts) + 1),
        out_specs=[HERE] * 2,
        out_shape=[jax.ShapeDtypeStruct(active.shape, jnp.float32)] * 2,
        compiler_params=pltpu.CompilerParams(vmem_limit_bytes=VMEM_LIMIT),
    )(*parts, active)


def parts_kernel(weight, *refs):
    magnitude, sign = refs[-2:]
    tile = min(256, weight.shape[0])
    for start in range(0, weight.shape[0], tile):
        span = slice(start, start + tile)
        w = weight[span, :].astype(jnp.float32)
        magnitude[span, :] = jnp.abs(w).astype(jnp.bfloat16)
        sign[span, :] = jnp.where(w > 0, 1.0, jnp.where(w < 0, -1.0, 0.0)).astype(jnp.bfloat16)


def parts_of(weight, *held):
    return pl.pallas_call(
        parts_kernel,
        in_specs=[HERE] * (1 + len(held)),
        out_specs=[HERE] * 2,
        out_shape=[jax.ShapeDtypeStruct(weight.shape, weight.dtype)] * 2,
        compiler_params=pltpu.CompilerParams(vmem_limit_bytes=VMEM_LIMIT),
    )(weight, *held)


def pack_kernel(first, second, out, both, sems):
    rows = first.shape[0]
    spans = [pl.ds(0, rows), pl.ds(rows, rows)]
    copies = [
        pltpu.make_async_copy(source, both.at[span, :], sem)
        for source, span, sem in zip((first, second), spans, (sems.at[0], sems.at[1]))
    ]
    onward = [
        pltpu.make_async_copy(both.at[span, :], out.at[span, :], sem)
        for span, sem in zip(spans, (sems.at[2], sems.at[3]))
    ]
    for copy in copies:
        copy.start()
    for copy, then in zip(copies, onward):
        copy.wait()
        then.start()
    for then in onward:
        then.wait()


def packed(first, second):
    rows, width = first.shape
    return pl.pallas_call(
        pack_kernel,
        in_specs=[ANYWHERE] * 2,
        out_specs=ANYWHERE,
        out_shape=jax.ShapeDtypeStruct((2 * rows, width), first.dtype),
        scratch_shapes=[pltpu.VMEM((2 * rows, width), first.dtype), pltpu.SemaphoreType.DMA((4,))],
        compiler_params=pltpu.CompilerParams(vmem_limit_bytes=VMEM_MOST),
    )(first, second)


def pack_kernel(first, second, out, both, sems):
    rows = first.shape[0]
    spans = [pl.ds(0, rows), pl.ds(rows, rows)]
    copies = [
        pltpu.make_async_copy(source, both.at[span, :], sem)
        for source, span, sem in zip((first, second), spans, (sems.at[0], sems.at[1]))
    ]
    onward = [
        pltpu.make_async_copy(both.at[span, :], out.at[span, :], sem)
        for span, sem in zip(spans, (sems.at[2], sems.at[3]))
    ]
    for copy in copies:
        copy.start()
    for copy, then in zip(copies, onward):
        copy.wait()
        then.start()
    for then in onward:
        then.wait()


def packed(first, second):
    rows, width = first.shape
    return pl.pallas_call(
        pack_kernel,
        in_specs=[ANYWHERE] * 2,
        out_specs=ANYWHERE,
        out_shape=jax.ShapeDtypeStruct((2 * rows, width), first.dtype),
        scratch_shapes=[pltpu.VMEM((2 * rows, width), first.dtype), pltpu.SemaphoreType.DMA((4,))],
        compiler_params=pltpu.CompilerParams(vmem_limit_bytes=VMEM_MOST),
    )(first, second)


def stack_kernel(*refs):
    *parts, out = refs
    rows = parts[0].shape[0]
    for n, part in enumerate(parts):
        out[n * rows : (n + 1) * rows, :] = part[...]


def stacked(parts):
    rows, width = parts[0].shape
    return pl.pallas_call(
        stack_kernel,
        in_specs=[HERE] * len(parts),
        out_specs=HERE,
        out_shape=jax.ShapeDtypeStruct((len(parts) * rows, width), parts[0].dtype),
        compiler_params=pltpu.CompilerParams(vmem_limit_bytes=VMEM_LIMIT),
    )(*parts)


def turn_kernel(rows, cols, *refs):
    held, outs, whole, order = refs[:cols], refs[cols:-2], refs[-2], refs[-1]
    owned = whole.shape[0] // cols
    shard = owned // PAIR
    for kind, out in enumerate(outs):
        for n, ref in enumerate(held):
            whole[n * owned : (n + 1) * owned, :] = ref[kind * owned : (kind + 1) * owned, :]
        for shift in by_distance(rows):
            piece, half, _ = spot(rows, cols, shift)
            start = pl.multiple_of((piece * PAIR + half) * shard, shard)
            to = row_of(rows, cols, shift, shard)
            order[pl.ds(to, shard), :] = whole[pl.ds(start, shard), :]
        out[...] = order[...].T


def turned(rows, cols, held):
    both, inner = held[0].shape
    tokens = both // 2 * cols
    return pl.pallas_call(
        functools.partial(turn_kernel, rows, cols),
        in_specs=[HERE] * cols,
        out_specs=[HERE] * 2,
        out_shape=[jax.ShapeDtypeStruct((inner, tokens), jnp.bfloat16)] * 2,
        scratch_shapes=[pltpu.VMEM((tokens, inner), jnp.bfloat16)] * 2,
        compiler_params=pltpu.CompilerParams(vmem_limit_bytes=VMEM_LIMIT),
    )(*held)


def weight_kernel(scale, center, radius, grad_c, grad_r, sign, out, parts, sems):
    tile = parts.shape[2]
    copies = []
    for n in range(out.shape[1] // tile):
        span = slice(n * tile, (n + 1) * tile)
        part, sem = parts.at[n % 2], sems.at[n % 2]
        if n >= 2:
            copies[n - 2].wait()
        through_center, through_radius = (
            lax.dot_general(ref[...], grad[:, span], BY_TOKEN, preferred_element_type=jnp.float32)
            for ref, grad in ((center, grad_c), (radius, grad_r))
        )
        signed = sign[:, span].astype(jnp.float32) * through_radius
        part[...] = (through_center + signed) * scale
        copies.append(pltpu.make_async_copy(part, out.at[:, pl.ds(n * tile, tile)], sem))
        copies[n].start()
    for copy in copies[-2:]:
        copy.wait()


def weight_terms(inputs, grads, sign):
    inner, width = sign.shape
    tile = min(256, width)
    scale = np.float32(1.0) / np.sqrt(np.float32(grads[0].shape[0]))
    return pl.pallas_call(
        functools.partial(weight_kernel, scale),
        in_specs=[HERE] * 5,
        out_specs=ANYWHERE,
        out_shape=jax.ShapeDtypeStruct((inner, width), jnp.float32),
        scratch_shapes=[pltpu.VMEM((2, inner, tile), jnp.float32), pltpu.SemaphoreType.DMA((2,))],
        compiler_params=pltpu.CompilerParams(vmem_limit_bytes=VMEM_LIMIT),
    )(*inputs, *grads, sign)


def on_device(rows, cols, center, radius, grad_center, grad_radius, weight, active):
    chips, cores = col_split(cols)
    held = grad_center.shape[0]
    assert rows % 2 == 0 and center.shape[0] == PAIR * held
    ring = ring_of(rows)
    clockwise = [(ring[i], ring[(i + 1) % rows]) for i in range(rows)]
    counter = [(b, a) for a, b in clockwise]
    last = rows // 2

    def swap_cores(value, j):
        perm = [(i, i - i % cores + (i % cores + j) % cores) for i in range(cols)]
        return lax.ppermute(value, "col", perm)

    def hop_chips(value, k):
        return lax.ppermute(value, "col", [(i, (i + k * cores) % cols) for i in range(cols)])

    def summed(terms):
        own, others = ([found[0]] + [swap_cores(found[j], j) for j in range(1, cores)]
                       for found in (terms[:cores], terms[cores:]))
        return own, [hop_chips(value, k + 1) for k, value in enumerate(coded_sums(others))]

    both = packed(center, radius)
    inputs = [both] + [hop_chips(both, -k) for k in range(1, chips)]
    slots_c, slots_r = {0: grad_center}, {0: grad_radius}
    shifts = by_distance(rows)
    for step in range(1, last):
        for slots in (slots_c, slots_r):
            slots[step] = lax.ppermute(slots[step - 1], "row", clockwise)
            slots[-step] = lax.ppermute(slots[1 - step], "row", counter)
    magnitude, sign = parts_of(weight, grad_center, grad_radius)
    weights = weight, magnitude
    slots_r[1 - last], weights = lax.optimization_barrier((slots_r[1 - last], weights))
    lasts = (
        lax.ppermute(slots_c[last - 1], "row", clockwise),
        lax.ppermute(slots_r[1 - last], "row", counter),
    )
    found = shifts[:-1]
    slots_c[0], inputs = lax.optimization_barrier((slots_c[0], inputs))
    terms, orders = near_terms(
        rows, cols, found, [slots_c[s] for s in found], [slots_r[s] for s in found], weights
    )
    near = summed(terms)
    terms, orders = far_terms(rows, cols, orders, lasts, weights)
    far = summed(terms)
    inputs, _ = lax.optimization_barrier((inputs, orders))
    for j in range(1, cores):
        inputs += [swap_cores(value, -j) for value in inputs[:chips]]
    weight_grad = weight_terms(turned(rows, cols, inputs), orders, sign)
    return *gated(rows, cols, (near, far), active), weight_grad


def solution(mesh):
    spec_in, spec_out, spec_weight = P("col", "row"), P("row", "col"), P("row", "col")
    return jax.shard_map(
        functools.partial(on_device, mesh.shape["row"], mesh.shape["col"]),
        mesh=mesh,
        in_specs=(spec_in, spec_in, spec_out, spec_out, spec_weight, spec_in),
        out_specs=(spec_in, spec_in, spec_weight),
        check_vma=False,
    )
```

time: 71.9 us -> 66.6 us (0.926)
  blocking collectives: 4.58 us -> 0 us
  local copies, waits for them, and re-layouts: 1.06 us -> 4.1 us
  waiting for transfers between devices: 24 us -> 21.7 us
  starting transfers between devices: 21.8 us -> 20.9 us
    ppermute x6, starting transfers between devices: 12.7 us -> 0.76 us  [on_device(): slots[step] = lax.ppermute(slots[step - 1], 'row', clockwise)]
    ppermute x6, starting transfers between devices: 0.7 us -> 12.6 us  [on_device(): slots[-step] = lax.ppermute(slots[1 - step], 'row', counter)]
    ppermute x6, waiting for transfers between devices: 11 us -> 2.49 us  [on_device(): slots[step] = lax.ppermute(slots[step - 1], 'row', clockwise)]
    all_to_all x1 -> x0, blocking collectives: 4.58 us -> none  [summed(): lax.all_to_all(others[0], 'col', 0, 0, axis_index_groups=groups, tiled=True)]
    ppermute x6, waiting for transfers between devices: 8.8 us -> 12.5 us  [on_device(): slots[-step] = lax.ppermute(slots[1 - step], 'row', counter)]
    unnamed x10 -> x12, local copies, waits for them, and re-layouts: 1.06 us -> 4.1 us
    ppermute x1, waiting for transfers between devices: 0.01 us -> 1.48 us  [on_device(): lax.ppermute(slots_c[last - 1], 'row', clockwise)]
    ppermute x3, waiting for transfers between devices: 3.3 us -> 4.63 us  [hop_chips(): lax.ppermute(value, 'col', [(i, (i + k * cores) % cols) for i in range(co...]
  transfers between devices with their start and end apart: 22 -> 23, of which waited for: 11 -> 8; matrix products, arithmetic and copies ran while one was open for 0% -> 0% of each run, Pallas kernels for 25% -> 26%
where the time goes in v3:
time: 66.6 us; the launch traced here: 66.3 us
  waiting for transfers between devices  21.7 us (33%)
  starting transfers between devices  20.9 us (31%)
  Pallas kernels  18.8 us (28%)
  local copies, waits for them, and re-layouts  4.1 us (6%)
  between operations  0.79 us (1%)
    ppermute x6, starting transfers between devices, on_device(): slots[-step] = lax.ppermute(slots[1 - step], 'row', counter)  12.6 us
    ppermute x6, waiting for transfers between devices, on_device(): slots[-step] = lax.ppermute(slots[1 - step], 'row', counter)  12.5 us
    pallas_call x1, Pallas kernels, weight_terms(): pl.pallas_call(functools.partial(weight_kernel, scale), in_specs=[HERE] *...  7.5 us
    ppermute x3, waiting for transfers between devices, hop_chips(): lax.ppermute(value, 'col', [(i, (i + k * cores) % cols) for i in range(co...  4.63 us
    unnamed x12, local copies, waits for them, and re-layouts  4.1 us
    ppermute x3, starting transfers between devices, hop_chips(): lax.ppermute(value, 'col', [(i, (i + k * cores) % cols) for i in range(co...  4.07 us
    pallas_call x1, Pallas kernels, near_terms(): pl.pallas_call(functools.partial(near_kernel, rows, cols, shifts), in_spe...  2.58 us
    ppermute x6, waiting for transfers between devices, on_device(): slots[step] = lax.ppermute(slots[step - 1], 'row', clockwise)  2.49 us
  transfers between devices with their start and end apart: 23, of which 8 were waited for; matrix products, arithmetic and copies ran while one was open for 0% of the time, Pallas kernels for 26%

profile of v3, /device:TPU:0, one launch (start us, length us, event | category | flops | bytes accessed | tf_op | source)
XLA Modules:
  0.0 66.3 jit_solution(15607825410641754489)
XLA Ops:
  0.6 3.0 %collective-permute-start.8 = (bf16[64,2048]{1,0:T(8,128)(2,1)}, bf16[64,2048]{1,0:T(8,128)(2,1)S(1)}, u32[]{:S(2)}, u32[]{:S(2)}) collective-permute-start(bf16[64,2048]{1,0:T(8,128)(2,1)} %refs_7_.1), channel_id=1, source_target_pairs={{8,0},{16,8},{24,16},{28,24},{20,28},{12,20},{4,12},{0,4},{9,1},{1... | collective-permute-start | bytes 786440 | tf_op jit(solution)/shard_map/ppermute | solution.py:395
  3.8 1.9 %collective-permute-start.2 = (bf16[64,2048]{1,0:T(8,128)(2,1)}, bf16[64,2048]{1,0:T(8,128)(2,1)S(1)}, u32[]{:S(2)}, u32[]{:S(2)}) collective-permute-start(bf16[64,2048]{1,0:T(8,128)(2,1)} %refs_0_.2), channel_id=1, source_target_pairs={{8,0},{16,8},{24,16},{28,24},{20,28},{12,20},{4,12},{0,4},{9,1},{1... | collective-permute-start | bytes 786440 | tf_op jit(solution)/shard_map/ppermute | solution.py:395
  5.8 5.3 %collective-permute-done.8.refs_9_ = bf16[64,2048]{1,0:T(8,128)(2,1)S(1)} collective-permute-done((bf16[64,2048]{1,0:T(8,128)(2,1)}, bf16[64,2048]{1,0:T(8,128)(2,1)S(1)}, u32[]{:S(2)}, u32[]{:S(2)}) %collective-permute-start.8) | collective-permute-done | bytes 262176 | tf_op jit(solution)/shard_map/ppermute | solution.py:395
  11.1 2.0 %collective-permute-start.10 = (bf16[64,2048]{1,0:T(8,128)(2,1)S(1)}, bf16[64,2048]{1,0:T(8,128)(2,1)S(1)}, u32[]{:S(2)}, u32[]{:S(2)}) collective-permute-start(bf16[64,2048]{1,0:T(8,128)(2,1)S(1)} %collective-permute-done.8.refs_9_), channel_id=1, source_target_pairs={{8,0},{16,8},{24,16},{28,24},{20,28},{12,20},{4,12},{0,4},{9,1},{1... | collective-permute-start | bytes 786440 | tf_op jit(solution)/shard_map/ppermute | solution.py:395
  13.2 1.8 %shard_map.85.refs_0_ = bf16[256,1024]{1,0:T(8,128)(2,1)} custom-call(bf16[128,1024]{1,0:T(8,128)(2,1)} %first.1, bf16[128,1024]{1,0:T(8,128)(2,1)} %second.1), custom_call_target="tpu_custom_call" | custom-call | tf_op jit(solution)/shard_map/pallas_call | solution.py:277
  15.0 2.0 %collective-permute-start = (bf16[256,1024]{1,0:T(8,128)(2,1)}, bf16[256,1024]{1,0:T(8,128)(2,1)S(1)}, u32[]{:S(2)}, u32[]{:S(2)}) collective-permute-start(bf16[256,1024]{1,0:T(8,128)(2,1)} %shard_map.85.refs_0_), channel_id=1, source_target_pairs={{0,2},{1,3},{2,0},{3,1},{4,6},{5,7},{6,4},{7,5},{8,10},{9,11},{10,... | collective-permute-start | bytes 1572872 | tf_op jit(solution)/shard_map/ppermute | solution.py:381
  16.9 1.7 %collective-permute-start.4 = (bf16[64,2048]{1,0:T(8,128)(2,1)S(1)}, bf16[64,2048]{1,0:T(8,128)(2,1)S(1)}, u32[]{:S(2)}, u32[]{:S(2)}) collective-permute-start(bf16[64,2048]{1,0:T(8,128)(2,1)S(1)} %collective-permute-done.2.refs_2_), channel_id=1, source_target_pairs={{8,0},{16,8},{24,16},{28,24},{20,28},{12,20},{4,12},{0,4},{9,1},{1... | collective-permute-start | bytes 786440 | tf_op jit(solution)/shard_map/ppermute | solution.py:395
  18.7 0.3 collective-permute-start.9
  19.0 3.3 %collective-permute-done.10.refs_11_ = bf16[64,2048]{1,0:T(8,128)(2,1)S(1)} collective-permute-done((bf16[64,2048]{1,0:T(8,128)(2,1)S(1)}, bf16[64,2048]{1,0:T(8,128)(2,1)S(1)}, u32[]{:S(2)}, u32[]{:S(2)}) %collective-permute-start.10) | collective-permute-done | bytes 262176 | tf_op jit(solution)/shard_map/ppermute | solution.py:395
  22.3 2.0 %collective-permute-start.12 = (bf16[64,2048]{1,0:T(8,128)(2,1)S(1)}, bf16[64,2048]{1,0:T(8,128)(2,1)S(1)}, u32[]{:S(2)}, u32[]{:S(2)}) collective-permute-start(bf16[64,2048]{1,0:T(8,128)(2,1)S(1)} %collective-permute-done.10.refs_11_), channel_id=1, source_target_pairs={{8,0},{16,8},{24,16},{28,24},{20,28},{12,20},{4,12},{0,4},{9,1},{1... | collective-permute-start | bytes 786440 | tf_op jit(solution)/shard_map/ppermute | solution.py:395
  24.4 3.5 %collective-permute-done.4.refs_4_ = bf16[64,2048]{1,0:T(8,128)(2,1)S(1)} collective-permute-done((bf16[64,2048]{1,0:T(8,128)(2,1)S(1)}, bf16[64,2048]{1,0:T(8,128)(2,1)S(1)}, u32[]{:S(2)}, u32[]{:S(2)}) %collective-permute-start.4) | collective-permute-done | bytes 262176 | tf_op jit(solution)/shard_map/ppermute | solution.py:395
  27.9 2.0 %collective-permute-start.6 = (bf16[64,2048]{1,0:T(8,128)(2,1)S(1)}, bf16[64,2048]{1,0:T(8,128)(2,1)S(1)}, u32[]{:S(2)}, u32[]{:S(2)}) collective-permute-start(bf16[64,2048]{1,0:T(8,128)(2,1)S(1)} %collective-permute-done.4.refs_4_), channel_id=1, source_target_pairs={{8,0},{16,8},{24,16},{28,24},{20,28},{12,20},{4,12},{0,4},{9,1},{1... | collective-permute-start | bytes 786440 | tf_op jit(solution)/shard_map/ppermute | solution.py:395
  30.0 2.2 %copy-done = bf16[1024,2048]{1,0:T(8,128)(2,1)S(1)} copy-done((bf16[1024,2048]{1,0:T(8,128)(2,1)S(1)}, bf16[1024,2048]{1,0:T(8,128)(2,1)}, u32[]{:S(2)}) %copy-start) | copy-done | bytes 4194328
  32.2 0.9 %copy-done.2 = bf16[64,2048]{1,0:T(8,128)(2,1)S(1)} copy-done((bf16[64,2048]{1,0:T(8,128)(2,1)S(1)}, bf16[64,2048]{1,0:T(8,128)(2,1)}, u32[]{:S(2)}) %copy-start.2) | copy-done | bytes 262168
  33.2 0.9 %copy-done.3 = bf16[64,2048]{1,0:T(8,128)(2,1)S(1)} copy-done((bf16[64,2048]{1,0:T(8,128)(2,1)S(1)}, bf16[64,2048]{1,0:T(8,128)(2,1)}, u32[]{:S(2)}) %copy-start.3) | copy-done | bytes 262168
  34.1 2.0 %shard_map.86 = (bf16[1024,2048]{1,0:T(8,128)(2,1)S(1)}, bf16[1024,2048]{1,0:T(8,128)(2,1)S(1)}) custom-call(bf16[1024,2048]{1,0:T(8,128)(2,1)S(1)} %copy-done, bf16[64,2048]{1,0:T(8,128)(2,1)S(1)} %copy-done.2, bf16[64,2048]{1,0:T(8,128)(2,1)S(1)} %copy-done.3), custom_call_target="tpu_custom_call" | custom-call | tf_op jit(solution)/shard_map/pallas_call | solution.py:214
  36.2 2.0 %collective-permute-start.16 = (bf16[64,2048]{1,0:T(8,128)(2,1)S(1)}, bf16[64,2048]{1,0:T(8,128)(2,1)S(1)}, u32[]{:S(2)}, u32[]{:S(2)}) collective-permute-start(bf16[64,2048]{1,0:T(8,128)(2,1)S(1)} %collective-permute-done.5.refs_5_), channel_id=1, source_target_pairs={{0,8},{8,16},{16,24},{24,28},{28,20},{20,12},{12,4},{4,0},{1,9},{9... | collective-permute-start | bytes 786440 | tf_op jit(solution)/shard_map/ppermute | solution.py:400
  38.4 0.5 collective-permute-done.6.refs_6_
  38.9 2.3 %collective-permute-done.11.refs_12_ = bf16[64,2048]{1,0:T(8,128)(2,1)S(1)} collective-permute-done((bf16[64,2048]{1,0:T(8,128)(2,1)S(1)}, bf16[64,2048]{1,0:T(8,128)(2,1)S(1)}, u32[]{:S(2)}, u32[]{:S(2)}) %collective-permute-start.11) | collective-permute-done | bytes 262176 | tf_op jit(solution)/shard_map/ppermute | solution.py:394
  41.2 2.6 %shard_map.87 = (f32[128,1024]{1,0:T(8,128)S(1)}, f32[128,1024]{1,0:T(8,128)S(1)}, f32[1,128,1024]{2,1,0:T(8,128)S(1)}, f32[1,128,1024]{2,1,0:T(8,128)S(1)}, bf1...) custom-call(bf16[64,2048]{1,0:T(8,128)(2,1)S(1)} %copy-done.2, ...), custom_call_target="tpu_custom_call" | custom-call | tf_op jit(solution)/shard_map/pallas_call | solution.py:108
  43.9 1.5 %collective-permute-done.16.refs_2_ = bf16[64,2048]{1,0:T(8,128)(2,1)S(1)} collective-permute-done((bf16[64,2048]{1,0:T(8,128)(2,1)S(1)}, bf16[64,2048]{1,0:T(8,128)(2,1)S(1)}, u32[]{:S(2)}, u32[]{:S(2)}) %collective-permute-start.16) | collective-permute-done | bytes 262176 | tf_op jit(solution)/shard_map/ppermute | solution.py:400
  45.3 2.4 %shard_map.89 = (f32[128,1024]{1,0:T(8,128)S(1)}, f32[128,1024]{1,0:T(8,128)S(1)}, f32[1,128,1024]{2,1,0:T(8,128)S(1)}, f32[1,128,1024]{2,1,0:T(8,128)S(1)}, bf1...) custom-call(bf16[512,2048]{1,0:T(8,128)(2,1)S(1)} %get-tuple-element.38.re, ...), custom_call_target="tpu_custom_call", output_to_operand_aliasing={{4}: (0, {}), {5}: (1, {})} | custom-call | tf_op jit(solution)/shard_map/pallas_call | solution.py:129
  47.8 0.5 collective-permute-start.21
  48.4 0.4 collective-permute-start.13
  48.9 0.2 shard_map.88
  49.1 0.6 collective-permute-done.19.refs_1_
  49.7 1.5 %collective-permute-start.15 = (s16[128,1152]{1,0:T(8,128)(2,1)S(1)}, s16[128,1152]{1,0:T(8,128)(2,1)S(1)}, u32[]{:S(2)}, u32[]{:S(2)}) collective-permute-start(s16[128,1152]{1,0:T(8,128)(2,1)S(1)} %shard_map.88), channel_id=1, source_target_pairs={{0,2},{1,3},{2,0},{3,1},{4,6},{5,7},{6,4},{7,5},{8,10},{9,11},{10,... | collective-permute-start | bytes 884744 | tf_op jit(solution)/shard_map/ppermute | solution.py:381
  51.4 0.6 collective-permute-start.20
  52.0 0.9 %shard_map.92 = (bf16[1024,512]{1,0:T(8,128)(2,1)S(1)}, bf16[1024,512]{1,0:T(8,128)(2,1)S(1)}) custom-call(bf16[256,1024]{1,0:T(8,128)(2,1)S(1)} %copy-done.1, bf16[256,1024]{1,0:T(8,128)(2,1)S(1)} %collective-permute-done.refs_1_, bf16[256,1024]{1,0:T(8,128)(2,1)S(1)} %collective-permute-done.21.refs_2_, bf16[256,1024]{1,0:T(8,128)(2,1)S(1)} %collective-permute-done.22.refs_3_), custom_call_target="tpu_custom_call" | custom-call | tf_op jit(solution)/shard_map/pallas_call | solution.py:323
  52.9 7.5 %shard_map.93 = f32[1024,2048]{1,0:T(8,128)} custom-call(bf16[1024,512]{1,0:T(8,128)(2,1)S(1)} %get-tuple-element.52.center, bf16[1024,512]{1,0:T(8,128)(2,1)S(1)} %get-tuple-element.53.radius, bf16[512,2048]{1,0:T(8,128)(2,1)S(1)} %get-tuple-element.48.grad_c, bf16[512,2048]{1,0:T(8,128)(2,1)S(1)} %get-tuple-element.49.grad_r, ...), custom_call_target="tpu_custom_call" | custom-call | tf_op jit(solution)/shard_map/pallas_call | solution.py:357
  60.4 4.6 %collective-permute-done.20.refs_5_ = s16[128,1152]{1,0:T(8,128)(2,1)S(1)} collective-permute-done((s16[128,1152]{1,0:T(8,128)(2,1)S(1)}, s16[128,1152]{1,0:T(8,128)(2,1)S(1)}, u32[]{:S(2)}, u32[]{:S(2)}) %collective-permute-start.20) | collective-permute-done | bytes 294944 | tf_op jit(solution)/shard_map/ppermute | solution.py:381
  65.1 1.3 %shard_map.91 = (f32[128,1024]{1,0:T(8,128)}, f32[128,1024]{1,0:T(8,128)}) custom-call(f32[128,1024]{1,0:T(8,128)S(1)} %get-tuple-element.34.refs_0_, f32[128,1024]{1,0:T(8,128)S(1)} %collective-permute-done.13.refs_1_, s16[128,1152]{1,0:T(8,128)(2,1)S(1)} %collective-permute-done.15.refs_2_, f32[128,1024]{1,0:T(8,128)S(1)} %get-tuple-element.40.refs_3_, ...), custom_call_target="tpu_custom_call" | custom-call | tf_op jit(solution)/shard_map/pallas_call | solution.py:194
  (35 shorter events, 1.4 us)
Async XLA Ops:
  0.6 40.6 %copy-start.4 = (bf16[64,2048]{1,0:T(8,128)(2,1)S(1)}, bf16[64,2048]{1,0:T(8,128)(2,1)}, u32[]{:S(2)}) copy-start(bf16[64,2048]{1,0:T(8,128)(2,1)} %refs_7_.1) | copy-start | bytes 786436
  0.6 10.4 %collective-permute-start.8 = (bf16[64,2048]{1,0:T(8,128)(2,1)}, bf16[64,2048]{1,0:T(8,128)(2,1)S(1)}, u32[]{:S(2)}, u32[]{:S(2)}) collective-permute-start(bf16[64,2048]{1,0:T(8,128)(2,1)} %refs_7_.1), channel_id=1, source_target_pairs={{8,0},{16,8},{24,16},{28,24},{20,28},{12,20},{4,12},{0,4},{9,1},{1... | collective-permute-start | bytes 786440 | tf_op jit(solution)/shard_map/ppermute | solution.py:395
  3.7 9.4 %collective-permute-start.1 = (bf16[64,2048]{1,0:T(8,128)(2,1)}, bf16[64,2048]{1,0:T(8,128)(2,1)S(1)}, u32[]{:S(2)}, u32[]{:S(2)}) collective-permute-start(bf16[64,2048]{1,0:T(8,128)(2,1)} %refs_0_.2), channel_id=1, source_target_pairs={{0,8},{8,16},{16,24},{24,28},{28,20},{20,12},{12,4},{4,0},{1,9},{9... | collective-permute-start | bytes 786440 | tf_op jit(solution)/shard_map/ppermute | solution.py:394
  3.8 13.2 %collective-permute-start.2 = (bf16[64,2048]{1,0:T(8,128)(2,1)}, bf16[64,2048]{1,0:T(8,128)(2,1)S(1)}, u32[]{:S(2)}, u32[]{:S(2)}) collective-permute-start(bf16[64,2048]{1,0:T(8,128)(2,1)} %refs_0_.2), channel_id=1, source_target_pairs={{8,0},{16,8},{24,16},{28,24},{20,28},{12,20},{4,12},{0,4},{9,1},{1... | collective-permute-start | bytes 786440 | tf_op jit(solution)/shard_map/ppermute | solution.py:395
  5.7 13.0 %collective-permute-start.7 = (bf16[64,2048]{1,0:T(8,128)(2,1)}, bf16[64,2048]{1,0:T(8,128)(2,1)S(1)}, u32[]{:S(2)}, u32[]{:S(2)}) collective-permute-start(bf16[64,2048]{1,0:T(8,128)(2,1)} %refs_7_.1), channel_id=1, source_target_pairs={{0,8},{8,16},{16,24},{24,28},{28,20},{20,12},{12,4},{4,0},{1,9},{9... | collective-permute-start | bytes 786440 | tf_op jit(solution)/shard_map/ppermute | solution.py:394
  11.1 11.2 %collective-permute-start.10 = (bf16[64,2048]{1,0:T(8,128)(2,1)S(1)}, bf16[64,2048]{1,0:T(8,128)(2,1)S(1)}, u32[]{:S(2)}, u32[]{:S(2)}) collective-permute-start(bf16[64,2048]{1,0:T(8,128)(2,1)S(1)} %collective-permute-done.8.refs_9_), channel_id=1, source_target_pairs={{8,0},{16,8},{24,16},{28,24},{20,28},{12,20},{4,12},{0,4},{9,1},{1... | collective-permute-start | bytes 786440 | tf_op jit(solution)/shard_map/ppermute | solution.py:395
  13.1 11.2 %collective-permute-start.3 = (bf16[64,2048]{1,0:T(8,128)(2,1)S(1)}, bf16[64,2048]{1,0:T(8,128)(2,1)S(1)}, u32[]{:S(2)}, u32[]{:S(2)}) collective-permute-start(bf16[64,2048]{1,0:T(8,128)(2,1)S(1)} %collective-permute-done.1.refs_1_), channel_id=1, source_target_pairs={{0,8},{8,16},{16,24},{24,28},{28,20},{20,12},{12,4},{4,0},{1,9},{9... | collective-permute-start | bytes 786440 | tf_op jit(solution)/shard_map/ppermute | solution.py:394
  15.0 23.4 %collective-permute-start = (bf16[256,1024]{1,0:T(8,128)(2,1)}, bf16[256,1024]{1,0:T(8,128)(2,1)S(1)}, u32[]{:S(2)}, u32[]{:S(2)}) collective-permute-start(bf16[256,1024]{1,0:T(8,128)(2,1)} %shard_map.85.refs_0_), channel_id=1, source_target_pairs={{0,2},{1,3},{2,0},{3,1},{4,6},{5,7},{6,4},{7,5},{8,10},{9,11},{10,... | collective-permute-start | bytes 1572872 | tf_op jit(solution)/shard_map/ppermute | solution.py:381
  16.9 11.0 %collective-permute-start.4 = (bf16[64,2048]{1,0:T(8,128)(2,1)S(1)}, bf16[64,2048]{1,0:T(8,128)(2,1)S(1)}, u32[]{:S(2)}, u32[]{:S(2)}) collective-permute-start(bf16[64,2048]{1,0:T(8,128)(2,1)S(1)} %collective-permute-done.2.refs_2_), channel_id=1, source_target_pairs={{8,0},{16,8},{24,16},{28,24},{20,28},{12,20},{4,12},{0,4},{9,1},{1... | collective-permute-start | bytes 786440 | tf_op jit(solution)/shard_map/ppermute | solution.py:395
  18.7 11.2 %collective-permute-start.9 = (bf16[64,2048]{1,0:T(8,128)(2,1)S(1)}, bf16[64,2048]{1,0:T(8,128)(2,1)S(1)}, u32[]{:S(2)}, u32[]{:S(2)}) collective-permute-start(bf16[64,2048]{1,0:T(8,128)(2,1)S(1)} %collective-permute-done.7.refs_8_), channel_id=1, source_target_pairs={{0,8},{8,16},{16,24},{24,28},{28,20},{20,12},{12,4},{4,0},{1,9},{9... | collective-permute-start | bytes 786440 | tf_op jit(solution)/shard_map/ppermute | solution.py:394
  22.3 13.8 %collective-permute-start.12 = (bf16[64,2048]{1,0:T(8,128)(2,1)S(1)}, bf16[64,2048]{1,0:T(8,128)(2,1)S(1)}, u32[]{:S(2)}, u32[]{:S(2)}) collective-permute-start(bf16[64,2048]{1,0:T(8,128)(2,1)S(1)} %collective-permute-done.10.refs_11_), channel_id=1, source_target_pairs={{8,0},{16,8},{24,16},{28,24},{20,28},{12,20},{4,12},{0,4},{9,1},{1... | collective-permute-start | bytes 786440 | tf_op jit(solution)/shard_map/ppermute | solution.py:395
  24.3 11.8 %collective-permute-start.5 = (bf16[64,2048]{1,0:T(8,128)(2,1)S(1)}, bf16[64,2048]{1,0:T(8,128)(2,1)S(1)}, u32[]{:S(2)}, u32[]{:S(2)}) collective-permute-start(bf16[64,2048]{1,0:T(8,128)(2,1)S(1)} %collective-permute-done.3.refs_3_), channel_id=1, source_target_pairs={{0,8},{8,16},{16,24},{24,28},{28,20},{20,12},{12,4},{4,0},{1,9},{9... | collective-permute-start | bytes 786440 | tf_op jit(solution)/shard_map/ppermute | solution.py:394
  27.9 10.9 %collective-permute-start.6 = (bf16[64,2048]{1,0:T(8,128)(2,1)S(1)}, bf16[64,2048]{1,0:T(8,128)(2,1)S(1)}, u32[]{:S(2)}, u32[]{:S(2)}) collective-permute-start(bf16[64,2048]{1,0:T(8,128)(2,1)S(1)} %collective-permute-done.4.refs_4_), channel_id=1, source_target_pairs={{8,0},{16,8},{24,16},{28,24},{20,28},{12,20},{4,12},{0,4},{9,1},{1... | collective-permute-start | bytes 786440 | tf_op jit(solution)/shard_map/ppermute | solution.py:395
  30.0 11.2 %collective-permute-start.11 = (bf16[64,2048]{1,0:T(8,128)(2,1)S(1)}, bf16[64,2048]{1,0:T(8,128)(2,1)S(1)}, u32[]{:S(2)}, u32[]{:S(2)}) collective-permute-start(bf16[64,2048]{1,0:T(8,128)(2,1)S(1)} %collective-permute-done.9.refs_10_), channel_id=1, source_target_pairs={{0,8},{8,16},{16,24},{24,28},{28,20},{20,12},{12,4},{4,0},{1,9},{9... | collective-permute-start | bytes 786440 | tf_op jit(solution)/shard_map/ppermute | solution.py:394
  30.0 2.2 %copy-start = (bf16[1024,2048]{1,0:T(8,128)(2,1)S(1)}, bf16[1024,2048]{1,0:T(8,128)(2,1)}, u32[]{:S(2)}) copy-start(bf16[1024,2048]{1,0:T(8,128)(2,1)} %refs_4_) | copy-start | bytes 12582916
  32.2 0.9 %copy-start.2 = (bf16[64,2048]{1,0:T(8,128)(2,1)S(1)}, bf16[64,2048]{1,0:T(8,128)(2,1)}, u32[]{:S(2)}) copy-start(bf16[64,2048]{1,0:T(8,128)(2,1)} %refs_0_.2) | copy-start | bytes 786436
  33.2 0.9 %copy-start.3 = (bf16[64,2048]{1,0:T(8,128)(2,1)S(1)}, bf16[64,2048]{1,0:T(8,128)(2,1)}, u32[]{:S(2)}) copy-start(bf16[64,2048]{1,0:T(8,128)(2,1)} %refs_7_.1) | copy-start | bytes 786436
  36.2 9.2 %collective-permute-start.16 = (bf16[64,2048]{1,0:T(8,128)(2,1)S(1)}, bf16[64,2048]{1,0:T(8,128)(2,1)S(1)}, u32[]{:S(2)}, u32[]{:S(2)}) collective-permute-start(bf16[64,2048]{1,0:T(8,128)(2,1)S(1)} %collective-permute-done.5.refs_5_), channel_id=1, source_target_pairs={{0,8},{8,16},{16,24},{24,28},{28,20},{20,12},{12,4},{4,0},{1,9},{9... | collective-permute-start | bytes 786440 | tf_op jit(solution)/shard_map/ppermute | solution.py:400
  38.2 7.1 %collective-permute-start.17 = (bf16[64,2048]{1,0:T(8,128)(2,1)S(1)}, bf16[64,2048]{1,0:T(8,128)(2,1)S(1)}, u32[]{:S(2)}, u32[]{:S(2)}) collective-permute-start(bf16[64,2048]{1,0:T(8,128)(2,1)S(1)} %collective-permute-done.12.refs_13_), channel_id=1, source_target_pairs={{8,0},{16,8},{24,16},{28,24},{20,28},{12,20},{4,12},{0,4},{9,1},{1... | collective-permute-start | bytes 786440 | tf_op jit(solution)/shard_map/ppermute | solution.py:401
  43.8 5.0 %collective-permute-start.14 = (f32[1,128,1024]{2,1,0:T(8,128)S(1)}, f32[1,128,1024]{2,1,0:T(8,128)S(1)}, u32[]{:S(2)}, u32[]{:S(2)}) collective-permute-start(f32[1,128,1024]{2,1,0:T(8,128)S(1)} %get-tuple-element.37), channel_id=1, source_target_pairs={{0,1},{1,0},{2,3},{3,2},{4,5},{5,4},{6,7},{7,6},{8,9},{9,8},{10,11... | collective-permute-start | bytes 1572872 | tf_op jit(solution)/shard_map/ppermute | solution.py:378
  45.3 2.5 %copy-start.1 = (bf16[256,1024]{1,0:T(8,128)(2,1)S(1)}, bf16[256,1024]{1,0:T(8,128)(2,1)}, u32[]{:S(2)}) copy-start(bf16[256,1024]{1,0:T(8,128)(2,1)} %shard_map.85.refs_0_) | copy-start | bytes 1572868
  47.7 2.0 %collective-permute-start.19 = (f32[1,128,1024]{2,1,0:T(8,128)S(1)}, f32[1,128,1024]{2,1,0:T(8,128)S(1)}, u32[]{:S(2)}, u32[]{:S(2)}) collective-permute-start(f32[1,128,1024]{2,1,0:T(8,128)S(1)} %get-tuple-element.43), channel_id=1, source_target_pairs={{0,1},{1,0},{2,3},{3,2},{4,5},{5,4},{6,7},{7,6},{8,9},{9,8},{10,11... | collective-permute-start | bytes 1572872 | tf_op jit(solution)/shard_map/ppermute | solution.py:378
  47.8 3.6 %collective-permute-start.21 = (bf16[256,1024]{1,0:T(8,128)(2,1)S(1)}, bf16[256,1024]{1,0:T(8,128)(2,1)S(1)}, u32[]{:S(2)}, u32[]{:S(2)}) collective-permute-start(bf16[256,1024]{1,0:T(8,128)(2,1)S(1)} %copy-done.1), channel_id=1, source_target_pairs={{0,1},{1,0},{2,3},{3,2},{4,5},{5,4},{6,7},{7,6},{8,9},{9,8},{10,11... | collective-permute-start | bytes 1572872 | tf_op jit(solution)/shard_map/ppermute | solution.py:378
  48.3 3.7 %collective-permute-start.22 = (bf16[256,1024]{1,0:T(8,128)(2,1)S(1)}, bf16[256,1024]{1,0:T(8,128)(2,1)S(1)}, u32[]{:S(2)}, u32[]{:S(2)}) collective-permute-start(bf16[256,1024]{1,0:T(8,128)(2,1)S(1)} %collective-permute-done.refs_1_), channel_id=1, source_target_pairs={{0,1},{1,0},{2,3},{3,2},{4,5},{5,4},{6,7},{7,6},{8,9},{9,8},{10,11... | collective-permute-start | bytes 1572872 | tf_op jit(solution)/shard_map/ppermute | solution.py:378
  48.4 12.0 %collective-permute-start.13 = (f32[128,1024]{1,0:T(8,128)S(1)}, f32[128,1024]{1,0:T(8,128)S(1)}, u32[]{:S(2)}, u32[]{:S(2)}) collective-permute-start(f32[128,1024]{1,0:T(8,128)S(1)} %get-tuple-element.35), channel_id=1, source_target_pairs={{0,1},{1,0},{2,3},{3,2},{4,5},{5,4},{6,7},{7,6},{8,9},{9,8},{10,11... | collective-permute-start | bytes 1572872 | tf_op jit(solution)/shard_map/ppermute | solution.py:378
  48.8 11.6 %collective-permute-start.18 = (f32[128,1024]{1,0:T(8,128)S(1)}, f32[128,1024]{1,0:T(8,128)S(1)}, u32[]{:S(2)}, u32[]{:S(2)}) collective-permute-start(f32[128,1024]{1,0:T(8,128)S(1)} %get-tuple-element.41), channel_id=1, source_target_pairs={{0,1},{1,0},{2,3},{3,2},{4,5},{5,4},{6,7},{7,6},{8,9},{9,8},{10,11... | collective-permute-start | bytes 1572872 | tf_op jit(solution)/shard_map/ppermute | solution.py:378
  49.7 10.7 %collective-permute-start.15 = (s16[128,1152]{1,0:T(8,128)(2,1)S(1)}, s16[128,1152]{1,0:T(8,128)(2,1)S(1)}, u32[]{:S(2)}, u32[]{:S(2)}) collective-permute-start(s16[128,1152]{1,0:T(8,128)(2,1)S(1)} %shard_map.88), channel_id=1, source_target_pairs={{0,2},{1,3},{2,0},{3,1},{4,6},{5,7},{6,4},{7,5},{8,10},{9,11},{10,... | collective-permute-start | bytes 884744 | tf_op jit(solution)/shard_map/ppermute | solution.py:381
  51.4 13.7 %collective-permute-start.20 = (s16[128,1152]{1,0:T(8,128)(2,1)S(1)}, s16[128,1152]{1,0:T(8,128)(2,1)S(1)}, u32[]{:S(2)}, u32[]{:S(2)}) collective-permute-start(s16[128,1152]{1,0:T(8,128)(2,1)S(1)} %shard_map.90), channel_id=1, source_target_pairs={{0,2},{1,3},{2,0},{3,1},{4,6},{5,7},{6,4},{7,5},{8,10},{9,11},{10,... | collective-permute-start | bytes 884744 | tf_op jit(solution)/shard_map/ppermute | solution.py:381
  52.9 12.2 %copy-start.5 = (s32[128,1024]{1,0:T(8,128)S(1)}, s32[128,1024]{1,0:T(8,128)}, u32[]{:S(2)}) copy-start(s32[128,1024]{1,0:T(8,128)} %refs_6_.1) | copy-start | bytes 1572868

commit v4 on v3

--- a/solution.py
+++ b/solution.py
@@ -12,6 +12,7 @@
 VMEM_MOST = 60 * 1024 * 1024
 HERE = pl.BlockSpec(memory_space=pltpu.VMEM)
 LANES = 128
+BITS, LOWEST = 8, 100
 LEVELS = np.float32(32000)
 TINY = np.float32(2.0**-100)
 ANYWHERE = pl.BlockSpec(memory_space=pl.ANY)
@@ -89,75 +90,88 @@
     ] * cores
 
 
-def near_kernel(rows, cols, shifts, *refs):
+def near_kernel(rows, cols, shifts, kind, *refs):
     count = len(shifts)
-    slots, weights, outs, orders = refs[: 2 * count], refs[2 * count : 2 * count + 2], refs[2 * count + 2 : -2], refs[-2:]
+    slots, weight, outs, order = refs[:count], refs[count], refs[-1 - 2 * col_split(cols)[1] : -1], refs[-1]
     held = slots[0].shape[0]
-    for n, shift in enumerate(shifts):
-        start = row_of(rows, cols, shift, held)
-        for kind, order in enumerate(orders):
-            order[pl.ds(start, held), :] = slots[kind * count + n][...]
-    for kind, (order, weight) in enumerate(zip(orders, weights)):
-        terms_of(order[: cols * held, :], weight, outs, kind)
-
-
-def near_terms(rows, cols, shifts, slots_c, slots_r, weights):
-    inner, width = weights[0].shape
-    held = slots_c[0].shape[0]
+    for shift, slot in zip(shifts, slots):
+        order[pl.ds(row_of(rows, cols, shift, held), held), :] = slot[...]
+    terms_of(order[: cols * held, :], weight, outs, kind)
+
+
+def near_terms(rows, cols, shifts, slots, weight, kind, begun=()):
+    inner, width = weight.shape
+    held = slots[0].shape[0]
     shapes = terms_shapes(cols, held, inner)
     found = pl.pallas_call(
-        functools.partial(near_kernel, rows, cols, shifts),
-        in_specs=[HERE] * (2 * len(shifts) + 2),
-        out_specs=[HERE] * (len(shapes) + 2),
-        out_shape=shapes + [jax.ShapeDtypeStruct((held * rows, width), jnp.bfloat16)] * 2,
-        compiler_params=pltpu.CompilerParams(vmem_limit_bytes=VMEM_LIMIT),
-    )(*slots_c, *slots_r, *weights)
-    return found[:-2], found[-2:]
-
-
-def far_kernel(rows, cols, *refs):
-    lasts, weights, outs, orders = refs[2:4], refs[4:6], refs[6:-2], refs[-2:]
-    held = lasts[0].shape[0]
-    start = row_of(rows, cols, rows // 2, held)
-    for kind, (order, last, weight) in enumerate(zip(orders, lasts, weights)):
-        order[pl.ds(start, held), :] = last[...]
-        terms_of(order[cols * held :, :], weight, outs, kind)
-
-
-def far_terms(rows, cols, orders, lasts, weights):
-    shapes = terms_shapes(cols, lasts[0].shape[0], weights[0].shape[0])
+        functools.partial(near_kernel, rows, cols, shifts, kind),
+        in_specs=[HERE] * (len(slots) + 1 + len(begun)),
+        out_specs=[HERE] * (len(shapes) + 1),
+        out_shape=shapes + [jax.ShapeDtypeStruct((held * rows, width), jnp.bfloat16)],
+        input_output_aliases={len(slots) + 1 + n: n for n in range(len(begun))},
+        compiler_params=pltpu.CompilerParams(vmem_limit_bytes=VMEM_LIMIT),
+    )(*slots, weight, *begun)
+    return found[:-1], found[-1]
+
+
+def far_kernel(rows, cols, kind, *refs):
+    last, weight, outs, order = refs[1], refs[2], refs[-1 - 2 * col_split(cols)[1] : -1], refs[-1]
+    held = last.shape[0]
+    order[pl.ds(row_of(rows, cols, rows // 2, held), held), :] = last[...]
+    terms_of(order[cols * held :, :], weight, outs, kind)
+
+
+def far_terms(rows, cols, order, last, weight, kind, begun=()):
+    shapes = terms_shapes(cols, last.shape[0], weight.shape[0])
+    aliases = {0: len(shapes)} | {3 + n: n for n in range(len(begun))}
     found = pl.pallas_call(
-        functools.partial(far_kernel, rows, cols),
-        in_specs=[HERE] * 6,
-        out_specs=[HERE] * (len(shapes) + 2),
-        out_shape=shapes + [jax.ShapeDtypeStruct(order.shape, order.dtype) for order in orders],
-        input_output_aliases={0: len(shapes), 1: len(shapes) + 1},
-        compiler_params=pltpu.CompilerParams(vmem_limit_bytes=VMEM_LIMIT),
-    )(*orders, *lasts, *weights)
-    return found[:-2], found[-2:]
-
-
-def sum_kernel(count, *refs):
-    parts, outs = refs[:count], refs[count:]
-    rows, width = parts[0].shape[1:]
+        functools.partial(far_kernel, rows, cols, kind),
+        in_specs=[HERE] * (3 + len(begun)),
+        out_specs=[HERE] * (len(shapes) + 1),
+        out_shape=shapes + [jax.ShapeDtypeStruct(order.shape, order.dtype)],
+        input_output_aliases=aliases,
+        compiler_params=pltpu.CompilerParams(vmem_limit_bytes=VMEM_LIMIT),
+    )(order, last, weight, *begun)
+    return found[:-1], found[-1]
+
+
+def coded(total):
+    most = jnp.max(jnp.abs(total), axis=1, keepdims=True)
+    exponent = jnp.ceil(jnp.log2(jnp.maximum(most, TINY)) + 1e-3)
+    steps = jnp.round(total * (LEVELS / jnp.exp2(exponent))).astype(jnp.int32)
+    first = steps[:, :LANES]
+    lane = lax.broadcasted_iota(jnp.int32, first.shape, 1)
+    shown = jnp.broadcast_to(exponent.astype(jnp.int32) + LOWEST, first.shape)
+    bit = lax.shift_right_logical(shown, jnp.minimum(lane, BITS)) & 1
+    first = jnp.where(lane < BITS, (first & -2) | bit, first)
+    return first.astype(jnp.int16), steps[:, LANES:].astype(jnp.int16)
+
+
+def decoded(part, rows):
+    first = part[rows, :LANES].astype(jnp.int32)
+    lane = lax.broadcasted_iota(jnp.int32, first.shape, 1)
+    bits = jnp.where(lane < BITS, lax.shift_left(first & 1, jnp.minimum(lane, BITS)), 0)
+    exponent = jnp.sum(bits.astype(jnp.float32), axis=1, keepdims=True) - LOWEST
+    return part[rows, :].astype(jnp.float32) * (jnp.exp2(exponent) / LEVELS)
+
+
+def sum_kernel(*refs):
+    others = refs[0].shape[0]
+    parts, outs = refs[:-others], refs[-others:]
     for k, out in enumerate(outs):
         total = parts[0][k]
         for part in parts[1:]:
             total = total + part[k]
-        most = jnp.max(jnp.abs(total), axis=1, keepdims=True)
-        exponent = jnp.ceil(jnp.log2(jnp.maximum(most, TINY)) + 1e-3)
-        coded = jnp.round(total * (LEVELS / jnp.exp2(exponent)))
-        out[:, :width] = coded.astype(jnp.int16)
-        out[:, width:] = jnp.broadcast_to(exponent, (rows, LANES)).astype(jnp.int16)
+        out[:, :LANES], out[:, LANES:] = coded(total)
 
 
 def coded_sums(parts):
     others, rows, width = parts[0].shape
     return pl.pallas_call(
-        functools.partial(sum_kernel, len(parts)),
+        sum_kernel,
         in_specs=[HERE] * len(parts),
         out_specs=[HERE] * others,
-        out_shape=[jax.ShapeDtypeStruct((rows, width + LANES), jnp.int16)] * others,
+        out_shape=[jax.ShapeDtypeStruct((rows, width), jnp.int16)] * others,
         compiler_params=pltpu.CompilerParams(vmem_limit_bytes=VMEM_LIMIT),
     )(*parts)
 
@@ -166,7 +180,6 @@
     rounds, (active, *outs) = refs[:-3], refs[-3:]
     rounds = rounds[: near + far], rounds[near + far :]
     held = active.shape[0] // PAIR
-    width = active.shape[1]
     here, col = on_ring(lax.axis_index("row"), rows), lax.axis_index("col")
     first = apart(here, on_ring(PAIR * col, rows), rows)
     second = apart(here, on_ring(PAIR * col + 1, rows), rows)
@@ -180,10 +193,7 @@
             for part in parts[1:near]:
                 total = total + part[mine, :]
             for part in parts[near:]:
-                exponent = part[mine, width : width + 1].astype(jnp.float32)
-                total = total + part[mine, :width].astype(jnp.float32) * (
-                    jnp.exp2(exponent) / LEVELS
-                )
+                total = total + decoded(part, mine)
             out[span, :] = gate * total
 
 
@@ -332,16 +342,23 @@
 
 def weight_kernel(scale, center, radius, grad_c, grad_r, sign, out, parts, sems):
     tile = parts.shape[2]
+    spans = [slice(start, start + tile) for start in range(0, out.shape[1], tile)]
     copies = []
-    for n in range(out.shape[1] // tile):
-        span = slice(n * tile, (n + 1) * tile)
+
+    def products(span):
+        return [
+            lax.dot_general(ref[...], grad[:, span], BY_TOKEN, preferred_element_type=jnp.float32)
+            for ref, grad in ((center, grad_c), (radius, grad_r))
+        ]
+
+    ahead = products(spans[0])
+    for n, span in enumerate(spans):
+        through_center, through_radius = ahead
+        if n + 1 < len(spans):
+            ahead = products(spans[n + 1])
         part, sem = parts.at[n % 2], sems.at[n % 2]
         if n >= 2:
             copies[n - 2].wait()
-        through_center, through_radius = (
-            lax.dot_general(ref[...], grad[:, span], BY_TOKEN, preferred_element_type=jnp.float32)
-            for ref, grad in ((center, grad_c), (radius, grad_r))
-        )
         signed = sign[:, span].astype(jnp.float32) * through_radius
         part[...] = (through_center + signed) * scale
         copies.append(pltpu.make_async_copy(part, out.at[:, pl.ds(n * tile, tile)], sem))
@@ -394,20 +411,24 @@
             slots[step] = lax.ppermute(slots[step - 1], "row", clockwise)
             slots[-step] = lax.ppermute(slots[1 - step], "row", counter)
     magnitude, sign = parts_of(weight, grad_center, grad_radius)
-    weights = weight, magnitude
-    slots_r[1 - last], weights = lax.optimization_barrier((slots_r[1 - last], weights))
+    slots_r[1 - last], weight, magnitude = lax.optimization_barrier(
+        (slots_r[1 - last], weight, magnitude)
+    )
     lasts = (
         lax.ppermute(slots_c[last - 1], "row", clockwise),
         lax.ppermute(slots_r[1 - last], "row", counter),
     )
     found = shifts[:-1]
     slots_c[0], inputs = lax.optimization_barrier((slots_c[0], inputs))
-    terms, orders = near_terms(
-        rows, cols, found, [slots_c[s] for s in found], [slots_r[s] for s in found], weights
+    terms, order_c = near_terms(rows, cols, found, [slots_c[s] for s in found], weight, 0)
+    terms, order_r = near_terms(
+        rows, cols, found, [slots_r[s] for s in found], magnitude, 1, terms
     )
     near = summed(terms)
-    terms, orders = far_terms(rows, cols, orders, lasts, weights)
+    terms, order_c = far_terms(rows, cols, order_c, lasts[0], weight, 0)
+    terms, order_r = far_terms(rows, cols, order_r, lasts[1], magnitude, 1, terms)
     far = summed(terms)
+    orders = order_c, order_r
     inputs, _ = lax.optimization_barrier((inputs, orders))
     for j in range(1, cores):
         inputs += [swap_cores(value, -j) for value in inputs[:chips]]

time: 66.6 us -> 64.9 us (0.974)
  waiting for transfers between devices: 21.7 us -> 19 us
  Pallas kernels: 18.8 us -> 19.9 us
    ppermute x6, starting transfers between devices: 0.76 us -> 11.4 us  [on_device(): slots[step] = lax.ppermute(slots[step - 1], 'row', clockwise)]
    ppermute x6, starting transfers between devices: 12.6 us -> 1.98 us  [on_device(): slots[-step] = lax.ppermute(slots[1 - step], 'row', counter)]
    ppermute x3, waiting for transfers between devices: 4.63 us -> 2.49 us  [hop_chips(): lax.ppermute(value, 'col', [(i, (i + k * cores) % cols) for i in range(co...]
    pallas_call x1, Pallas kernels: 7.5 us -> 8.26 us  [weight_terms(): pl.pallas_call(functools.partial(weight_kernel, scale), in_specs=[HERE] *...]
    ppermute x6, waiting for transfers between devices: 12.5 us -> 11.8 us  [on_device(): slots[-step] = lax.ppermute(slots[1 - step], 'row', counter)]
    pallas_call x4 -> x6, Pallas kernels: 5.36 us -> 5.74 us  [the longest x2 2.81 us: near_terms(): pl.pallas_call(functools.partial(near_kernel, rows, cols, shifts, kind),...]
    unnamed x12 -> x14, local copies, waits for them, and re-layouts: 4.1 us -> 4.11 us
  transfers between devices with their start and end apart: 23 -> 23, of which waited for: 8 -> 9; matrix products, arithmetic and copies ran while one was open for 0% -> 0% of each run, Pallas kernels for 26% -> 29%
where the time goes in v4:
time: 64.9 us; the launch traced here: 64.6 us
  starting transfers between devices  20.8 us (32%)
  Pallas kernels  19.9 us (31%)
  waiting for transfers between devices  19 us (29%)
  local copies, waits for them, and re-layouts  4.11 us (6%)
  between operations  0.82 us (1%)
    ppermute x6, waiting for transfers between devices, on_device(): slots[-step] = lax.ppermute(slots[1 - step], 'row', counter)  11.8 us
    ppermute x6, starting transfers between devices, on_device(): slots[step] = lax.ppermute(slots[step - 1], 'row', clockwise)  11.4 us
    pallas_call x1, Pallas kernels, weight_terms(): pl.pallas_call(functools.partial(weight_kernel, scale), in_specs=[HERE] *...  8.26 us
    unnamed x14, local copies, waits for them, and re-layouts  4.11 us
    ppermute x3, starting transfers between devices, hop_chips(): lax.ppermute(value, 'col', [(i, (i + k * cores) % cols) for i in range(co...  4.06 us
    ppermute x6, waiting for transfers between devices, on_device(): slots[step] = lax.ppermute(slots[step - 1], 'row', clockwise)  2.92 us
    pallas_call x2, Pallas kernels, near_terms(): pl.pallas_call(functools.partial(near_kernel, rows, cols, shifts, kind),...  2.81 us
    pallas_call x2, Pallas kernels, far_terms(): pl.pallas_call(functools.partial(far_kernel, rows, cols, kind), in_specs=...  2.56 us
  transfers between devices with their start and end apart: 23, of which 9 were waited for; matrix products, arithmetic and copies ran while one was open for 0% of the time, Pallas kernels for 29%

profile of v4, /device:TPU:0, one launch (start us, length us, event | category | flops | bytes accessed | tf_op | source)
XLA Modules:
  0.0 64.6 jit_solution(6744211697211744753)
XLA Ops:
  0.6 3.1 %collective-permute-start.7 = (bf16[64,2048]{1,0:T(8,128)(2,1)}, bf16[64,2048]{1,0:T(8,128)(2,1)S(1)}, u32[]{:S(2)}, u32[]{:S(2)}) collective-permute-start(bf16[64,2048]{1,0:T(8,128)(2,1)} %refs_0_.3), channel_id=1, source_target_pairs={{0,8},{8,16},{16,24},{24,28},{28,20},{20,12},{12,4},{4,0},{1,9},{9... | collective-permute-start | bytes 786440 | tf_op jit(solution)/shard_map/ppermute | solution.py:411
  3.7 2.0 %collective-permute-start.8 = (bf16[64,2048]{1,0:T(8,128)(2,1)}, bf16[64,2048]{1,0:T(8,128)(2,1)S(1)}, u32[]{:S(2)}, u32[]{:S(2)}) collective-permute-start(bf16[64,2048]{1,0:T(8,128)(2,1)} %refs_0_.3), channel_id=1, source_target_pairs={{8,0},{16,8},{24,16},{28,24},{20,28},{12,20},{4,12},{0,4},{9,1},{1... | collective-permute-start | bytes 786440 | tf_op jit(solution)/shard_map/ppermute | solution.py:412
  5.8 1.8 %shard_map.86.refs_0_ = bf16[256,1024]{1,0:T(8,128)(2,1)} custom-call(bf16[128,1024]{1,0:T(8,128)(2,1)} %first.1, bf16[128,1024]{1,0:T(8,128)(2,1)} %second.1), custom_call_target="tpu_custom_call" | custom-call | tf_op jit(solution)/shard_map/pallas_call | solution.py:287
  7.5 2.0 %collective-permute-start.6 = (bf16[256,1024]{1,0:T(8,128)(2,1)}, bf16[256,1024]{1,0:T(8,128)(2,1)S(1)}, u32[]{:S(2)}, u32[]{:S(2)}) collective-permute-start(bf16[256,1024]{1,0:T(8,128)(2,1)} %shard_map.86.refs_0_), channel_id=1, source_target_pairs={{0,2},{1,3},{2,0},{3,1},{4,6},{5,7},{6,4},{7,5},{8,10},{9,11},{10,... | collective-permute-start | bytes 1572872 | tf_op jit(solution)/shard_map/ppermute | solution.py:398
  9.5 1.5 %collective-permute-done.7.refs_1_ = bf16[64,2048]{1,0:T(8,128)(2,1)S(1)} collective-permute-done((bf16[64,2048]{1,0:T(8,128)(2,1)}, bf16[64,2048]{1,0:T(8,128)(2,1)S(1)}, u32[]{:S(2)}, u32[]{:S(2)}) %collective-permute-start.7) | collective-permute-done | bytes 262176 | tf_op jit(solution)/shard_map/ppermute | solution.py:411
  11.0 2.1 %collective-permute-start.9 = (bf16[64,2048]{1,0:T(8,128)(2,1)S(1)}, bf16[64,2048]{1,0:T(8,128)(2,1)S(1)}, u32[]{:S(2)}, u32[]{:S(2)}) collective-permute-start(bf16[64,2048]{1,0:T(8,128)(2,1)S(1)} %collective-permute-done.7.refs_1_), channel_id=1, source_target_pairs={{0,8},{8,16},{16,24},{24,28},{28,20},{20,12},{12,4},{4,0},{1,9},{9... | collective-permute-start | bytes 786440 | tf_op jit(solution)/shard_map/ppermute | solution.py:411
  13.2 5.6 %collective-permute-done.8.refs_2_ = bf16[64,2048]{1,0:T(8,128)(2,1)S(1)} collective-permute-done((bf16[64,2048]{1,0:T(8,128)(2,1)}, bf16[64,2048]{1,0:T(8,128)(2,1)S(1)}, u32[]{:S(2)}, u32[]{:S(2)}) %collective-permute-start.8) | collective-permute-done | bytes 262176 | tf_op jit(solution)/shard_map/ppermute | solution.py:412
  18.8 2.0 %collective-permute-start.2 = (bf16[64,2048]{1,0:T(8,128)(2,1)S(1)}, bf16[64,2048]{1,0:T(8,128)(2,1)S(1)}, u32[]{:S(2)}, u32[]{:S(2)}) collective-permute-start(bf16[64,2048]{1,0:T(8,128)(2,1)S(1)} %collective-permute-done.refs_1_), channel_id=1, source_target_pairs={{0,8},{8,16},{16,24},{24,28},{28,20},{20,12},{12,4},{4,0},{1,9},{9... | collective-permute-start | bytes 786440 | tf_op jit(solution)/shard_map/ppermute | solution.py:411
  20.8 1.4 %collective-permute-done.9.refs_3_ = bf16[64,2048]{1,0:T(8,128)(2,1)S(1)} collective-permute-done((bf16[64,2048]{1,0:T(8,128)(2,1)S(1)}, bf16[64,2048]{1,0:T(8,128)(2,1)S(1)}, u32[]{:S(2)}, u32[]{:S(2)}) %collective-permute-start.9) | collective-permute-done | bytes 262176 | tf_op jit(solution)/shard_map/ppermute | solution.py:411
  22.2 2.1 %collective-permute-start.11 = (bf16[64,2048]{1,0:T(8,128)(2,1)S(1)}, bf16[64,2048]{1,0:T(8,128)(2,1)S(1)}, u32[]{:S(2)}, u32[]{:S(2)}) collective-permute-start(bf16[64,2048]{1,0:T(8,128)(2,1)S(1)} %collective-permute-done.9.refs_3_), channel_id=1, source_target_pairs={{0,8},{8,16},{16,24},{24,28},{28,20},{20,12},{12,4},{4,0},{1,9},{9... | collective-permute-start | bytes 786440 | tf_op jit(solution)/shard_map/ppermute | solution.py:411
  24.4 5.6 %collective-permute-done.10.refs_4_ = bf16[64,2048]{1,0:T(8,128)(2,1)S(1)} collective-permute-done((bf16[64,2048]{1,0:T(8,128)(2,1)S(1)}, bf16[64,2048]{1,0:T(8,128)(2,1)S(1)}, u32[]{:S(2)}, u32[]{:S(2)}) %collective-permute-start.10) | collective-permute-done | bytes 262176 | tf_op jit(solution)/shard_map/ppermute | solution.py:412
  30.0 2.0 %collective-permute-start.4 = (bf16[64,2048]{1,0:T(8,128)(2,1)S(1)}, bf16[64,2048]{1,0:T(8,128)(2,1)S(1)}, u32[]{:S(2)}, u32[]{:S(2)}) collective-permute-start(bf16[64,2048]{1,0:T(8,128)(2,1)S(1)} %collective-permute-done.2.refs_3_), channel_id=1, source_target_pairs={{0,8},{8,16},{16,24},{24,28},{28,20},{20,12},{12,4},{4,0},{1,9},{9... | collective-permute-start | bytes 786440 | tf_op jit(solution)/shard_map/ppermute | solution.py:411
  32.0 2.2 %copy-done = bf16[1024,2048]{1,0:T(8,128)(2,1)S(1)} copy-done((bf16[1024,2048]{1,0:T(8,128)(2,1)S(1)}, bf16[1024,2048]{1,0:T(8,128)(2,1)}, u32[]{:S(2)}) %copy-start) | copy-done | bytes 4194328
  34.2 0.9 %copy-done.3 = bf16[64,2048]{1,0:T(8,128)(2,1)S(1)} copy-done((bf16[64,2048]{1,0:T(8,128)(2,1)S(1)}, bf16[64,2048]{1,0:T(8,128)(2,1)}, u32[]{:S(2)}) %copy-start.3) | copy-done | bytes 262168
  35.2 0.9 %copy-done.4 = bf16[64,2048]{1,0:T(8,128)(2,1)S(1)} copy-done((bf16[64,2048]{1,0:T(8,128)(2,1)S(1)}, bf16[64,2048]{1,0:T(8,128)(2,1)}, u32[]{:S(2)}) %copy-start.4) | copy-done | bytes 262168
  36.1 2.0 %shard_map.85 = (bf16[1024,2048]{1,0:T(8,128)(2,1)S(1)}, bf16[1024,2048]{1,0:T(8,128)(2,1)S(1)}) custom-call(bf16[1024,2048]{1,0:T(8,128)(2,1)S(1)} %copy-done, bf16[64,2048]{1,0:T(8,128)(2,1)S(1)} %copy-done.3, bf16[64,2048]{1,0:T(8,128)(2,1)S(1)} %copy-done.4), custom_call_target="tpu_custom_call" | custom-call | tf_op jit(solution)/shard_map/pallas_call | solution.py:224
  38.2 1.6 %collective-permute-start.17 = (bf16[64,2048]{1,0:T(8,128)(2,1)S(1)}, bf16[64,2048]{1,0:T(8,128)(2,1)S(1)}, u32[]{:S(2)}, u32[]{:S(2)}) collective-permute-start(bf16[64,2048]{1,0:T(8,128)(2,1)S(1)} %collective-permute-done.11.refs_5_), channel_id=1, source_target_pairs={{0,8},{8,16},{16,24},{24,28},{28,20},{20,12},{12,4},{4,0},{1,9},{9... | collective-permute-start | bytes 786440 | tf_op jit(solution)/shard_map/ppermute | solution.py:418
  39.8 0.5 collective-permute-start.16
  40.2 0.5 collective-permute-done.12.refs_6_
  40.8 1.4 %shard_map.87 = (f32[128,1024]{1,0:T(8,128)S(1)}, f32[128,1024]{1,0:T(8,128)S(1)}, f32[1,128,1024]{2,1,0:T(8,128)S(1)}, f32[1,128,1024]{2,1,0:T(8,128)S(1)}, bf16[512,2048]{1,0:T(8,128)(2,1)S(1)}) custom-call(bf16[64,2048]{1,0:T(8,128)(2,1)S(1)} %copy-done.3, bf16[64,2048]{1,0:T(8,128)(2,1)S(1)} %collective-permute-done.7.refs_1_, ...), custom_call_target="tpu_custom_call" | custom-call | tf_op jit(solution)/shard_map/pallas_call | solution.py:106
  42.2 1.4 %shard_map.88 = (f32[128,1024]{1,0:T(8,128)S(1)}, f32[128,1024]{1,0:T(8,128)S(1)}, f32[1,128,1024]{2,1,0:T(8,128)S(1)}, f32[1,128,1024]{2,1,0:T(8,128)S(1)}, bf16[512,2048]{1,0:T(8,128)(2,1)S(1)}) custom-call(bf16[64,2048]{1,0:T(8,128)(2,1)S(1)} %copy-done.5, ...), custom_call_target="tpu_custom_call", output_to_operand_aliasing={{0}: (8, {}), {1}: (9, {}), {2}: (10, {}), {3}: (11, {})} | custom-call | tf_op jit(solution)/shard_map/pallas_call | solution.py:106
  43.7 0.9 %collective-permute-done.17.refs_1_ = bf16[64,2048]{1,0:T(8,128)(2,1)S(1)} collective-permute-done((bf16[64,2048]{1,0:T(8,128)(2,1)S(1)}, bf16[64,2048]{1,0:T(8,128)(2,1)S(1)}, u32[]{:S(2)}, u32[]{:S(2)}) %collective-permute-start.17) | collective-permute-done | bytes 262176 | tf_op jit(solution)/shard_map/ppermute | solution.py:418
  44.6 1.3 %shard_map.90 = (f32[128,1024]{1,0:T(8,128)S(1)}, f32[128,1024]{1,0:T(8,128)S(1)}, f32[1,128,1024]{2,1,0:T(8,128)S(1)}, f32[1,128,1024]{2,1,0:T(8,128)S(1)}, bf16[512,2048]{1,0:T(8,128)(2,1)S(1)}) custom-call(bf16[512,2048]{1,0:T(8,128)(2,1)S(1)} %get-tuple-element.51.refs_0_, ...), custom_call_target="tpu_custom_call", output_to_operand_aliasing={{4}: (0, {})} | custom-call | tf_op jit(solution)/shard_map/pallas_call | solution.py:127
  46.2 1.3 %shard_map.91 = (f32[128,1024]{1,0:T(8,128)S(1)}, f32[128,1024]{1,0:T(8,128)S(1)}, f32[1,128,1024]{2,1,0:T(8,128)S(1)}, f32[1,128,1024]{2,1,0:T(8,128)S(1)}, bf16[512,2048]{1,0:T(8,128)(2,1)S(1)}) custom-call(bf16[512,2048]{1,0:T(8,128)(2,1)S(1)} %get-tuple-element.50.refs_0_, ...), custom_call_target="tpu_custom_call", output_to_operand_aliasing={{4}: (0, {}), {0}: (3, {}), {1}: (4, {}), {2}: (5, {}), {3}... | custom-call | tf_op jit(solution)/shard_map/pallas_call | solution.py:127
  47.5 0.5 collective-permute-start.21
  48.8 0.6 collective-permute-done.19.refs_1_
  49.4 1.5 %collective-permute-start.15 = (s16[128,1024]{1,0:T(8,128)(2,1)S(1)}, s16[128,1024]{1,0:T(8,128)(2,1)S(1)}, u32[]{:S(2)}, u32[]{:S(2)}) collective-permute-start(s16[128,1024]{1,0:T(8,128)(2,1)S(1)} %shard_map.89), channel_id=1, source_target_pairs={{0,2},{1,3},{2,0},{3,1},{4,6},{5,7},{6,4},{7,5},{8,10},{9,11},{10,... | collective-permute-start | bytes 786440 | tf_op jit(solution)/shard_map/ppermute | solution.py:398
  51.1 0.6 collective-permute-start.20
  51.7 0.9 %shard_map.94 = (bf16[1024,512]{1,0:T(8,128)(2,1)S(1)}, bf16[1024,512]{1,0:T(8,128)(2,1)S(1)}) custom-call(bf16[256,1024]{1,0:T(8,128)(2,1)S(1)} %copy-done.2, bf16[256,1024]{1,0:T(8,128)(2,1)S(1)} %collective-permute-done.6.refs_1_, bf16[256,1024]{1,0:T(8,128)(2,1)S(1)} %collective-permute-done.21.refs_2_, bf16[256,1024]{1,0:T(8,128)(2,1)S(1)} %collective-permute-done.22.refs_3_), custom_call_target="tpu_custom_call" | custom-call | tf_op jit(solution)/shard_map/pallas_call | solution.py:333
  52.6 8.3 %shard_map.95 = f32[1024,2048]{1,0:T(8,128)} custom-call(bf16[1024,512]{1,0:T(8,128)(2,1)S(1)} %get-tuple-element.68.center, bf16[1024,512]{1,0:T(8,128)(2,1)S(1)} %get-tuple-element.69.radius, bf16[512,2048]{1,0:T(8,128)(2,1)S(1)} %get-tuple-element.64.grad_c, bf16[512,2048]{1,0:T(8,128)(2,1)S(1)} %get-tuple-element.65.grad_r, ...), custom_call_target="tpu_custom_call" | custom-call | tf_op jit(solution)/shard_map/pallas_call | solution.py:374
  60.9 2.5 %collective-permute-done.20.refs_5_ = s16[128,1024]{1,0:T(8,128)(2,1)S(1)} collective-permute-done((s16[128,1024]{1,0:T(8,128)(2,1)S(1)}, s16[128,1024]{1,0:T(8,128)(2,1)S(1)}, u32[]{:S(2)}, u32[]{:S(2)}) %collective-permute-start.20) | collective-permute-done | bytes 262176 | tf_op jit(solution)/shard_map/ppermute | solution.py:398
  63.4 1.2 %shard_map.93 = (f32[128,1024]{1,0:T(8,128)}, f32[128,1024]{1,0:T(8,128)}) custom-call(f32[128,1024]{1,0:T(8,128)S(1)} %get-tuple-element.46.refs_0_, f32[128,1024]{1,0:T(8,128)S(1)} %collective-permute-done.13.refs_1_, s16[128,1024]{1,0:T(8,128)(2,1)S(1)} %collective-permute-done.15.refs_2_, f32[128,1024]{1,0:T(8,128)S(1)} %get-tuple-element.56.refs_3_, ...), custom_call_target="tpu_custom_call" | custom-call | tf_op jit(solution)/shard_map/pallas_call | solution.py:204
  (39 shorter events, 1.6 us)
Async XLA Ops:
  0.6 10.4 %collective-permute-start.7 = (bf16[64,2048]{1,0:T(8,128)(2,1)}, bf16[64,2048]{1,0:T(8,128)(2,1)S(1)}, u32[]{:S(2)}, u32[]{:S(2)}) collective-permute-start(bf16[64,2048]{1,0:T(8,128)(2,1)} %refs_0_.3), channel_id=1, source_target_pairs={{0,8},{8,16},{16,24},{24,28},{28,20},{20,12},{12,4},{4,0},{1,9},{9... | collective-permute-start | bytes 786440 | tf_op jit(solution)/shard_map/ppermute | solution.py:411
  3.7 9.4 %collective-permute-start.1 = (bf16[64,2048]{1,0:T(8,128)(2,1)}, bf16[64,2048]{1,0:T(8,128)(2,1)S(1)}, u32[]{:S(2)}, u32[]{:S(2)}) collective-permute-start(bf16[64,2048]{1,0:T(8,128)(2,1)} %refs_0_.4), channel_id=1, source_target_pairs={{8,0},{16,8},{24,16},{28,24},{20,28},{12,20},{4,12},{0,4},{9,1},{1... | collective-permute-start | bytes 786440 | tf_op jit(solution)/shard_map/ppermute | solution.py:412
  3.7 15.0 %collective-permute-start.8 = (bf16[64,2048]{1,0:T(8,128)(2,1)}, bf16[64,2048]{1,0:T(8,128)(2,1)S(1)}, u32[]{:S(2)}, u32[]{:S(2)}) collective-permute-start(bf16[64,2048]{1,0:T(8,128)(2,1)} %refs_0_.3), channel_id=1, source_target_pairs={{8,0},{16,8},{24,16},{28,24},{20,28},{12,20},{4,12},{0,4},{9,1},{1... | collective-permute-start | bytes 786440 | tf_op jit(solution)/shard_map/ppermute | solution.py:412
  5.7 13.1 %collective-permute-start = (bf16[64,2048]{1,0:T(8,128)(2,1)}, bf16[64,2048]{1,0:T(8,128)(2,1)S(1)}, u32[]{:S(2)}, u32[]{:S(2)}) collective-permute-start(bf16[64,2048]{1,0:T(8,128)(2,1)} %refs_0_.4), channel_id=1, source_target_pairs={{0,8},{8,16},{16,24},{24,28},{28,20},{20,12},{12,4},{4,0},{1,9},{9... | collective-permute-start | bytes 786440 | tf_op jit(solution)/shard_map/ppermute | solution.py:411
  7.5 30.6 %collective-permute-start.6 = (bf16[256,1024]{1,0:T(8,128)(2,1)}, bf16[256,1024]{1,0:T(8,128)(2,1)S(1)}, u32[]{:S(2)}, u32[]{:S(2)}) collective-permute-start(bf16[256,1024]{1,0:T(8,128)(2,1)} %shard_map.86.refs_0_), channel_id=1, source_target_pairs={{0,2},{1,3},{2,0},{3,1},{4,6},{5,7},{6,4},{7,5},{8,10},{9,11},{10,... | collective-permute-start | bytes 1572872 | tf_op jit(solution)/shard_map/ppermute | solution.py:398
  11.0 11.2 %collective-permute-start.9 = (bf16[64,2048]{1,0:T(8,128)(2,1)S(1)}, bf16[64,2048]{1,0:T(8,128)(2,1)S(1)}, u32[]{:S(2)}, u32[]{:S(2)}) collective-permute-start(bf16[64,2048]{1,0:T(8,128)(2,1)S(1)} %collective-permute-done.7.refs_1_), channel_id=1, source_target_pairs={{0,8},{8,16},{16,24},{24,28},{28,20},{20,12},{12,4},{4,0},{1,9},{9... | collective-permute-start | bytes 786440 | tf_op jit(solution)/shard_map/ppermute | solution.py:411
  13.1 11.2 %collective-permute-start.3 = (bf16[64,2048]{1,0:T(8,128)(2,1)S(1)}, bf16[64,2048]{1,0:T(8,128)(2,1)S(1)}, u32[]{:S(2)}, u32[]{:S(2)}) collective-permute-start(bf16[64,2048]{1,0:T(8,128)(2,1)S(1)} %collective-permute-done.1.refs_2_), channel_id=1, source_target_pairs={{8,0},{16,8},{24,16},{28,24},{20,28},{12,20},{4,12},{0,4},{9,1},{1... | collective-permute-start | bytes 786440 | tf_op jit(solution)/shard_map/ppermute | solution.py:412
  18.8 11.2 %collective-permute-start.10 = (bf16[64,2048]{1,0:T(8,128)(2,1)S(1)}, bf16[64,2048]{1,0:T(8,128)(2,1)S(1)}, u32[]{:S(2)}, u32[]{:S(2)}) collective-permute-start(bf16[64,2048]{1,0:T(8,128)(2,1)S(1)} %collective-permute-done.8.refs_2_), channel_id=1, source_target_pairs={{8,0},{16,8},{24,16},{28,24},{20,28},{12,20},{4,12},{0,4},{9,1},{1... | collective-permute-start | bytes 786440 | tf_op jit(solution)/shard_map/ppermute | solution.py:412
  18.8 11.2 %collective-permute-start.2 = (bf16[64,2048]{1,0:T(8,128)(2,1)S(1)}, bf16[64,2048]{1,0:T(8,128)(2,1)S(1)}, u32[]{:S(2)}, u32[]{:S(2)}) collective-permute-start(bf16[64,2048]{1,0:T(8,128)(2,1)S(1)} %collective-permute-done.refs_1_), channel_id=1, source_target_pairs={{0,8},{8,16},{16,24},{24,28},{28,20},{20,12},{12,4},{4,0},{1,9},{9... | collective-permute-start | bytes 786440 | tf_op jit(solution)/shard_map/ppermute | solution.py:411
  22.2 15.9 %collective-permute-start.11 = (bf16[64,2048]{1,0:T(8,128)(2,1)S(1)}, bf16[64,2048]{1,0:T(8,128)(2,1)S(1)}, u32[]{:S(2)}, u32[]{:S(2)}) collective-permute-start(bf16[64,2048]{1,0:T(8,128)(2,1)S(1)} %collective-permute-done.9.refs_3_), channel_id=1, source_target_pairs={{0,8},{8,16},{16,24},{24,28},{28,20},{20,12},{12,4},{4,0},{1,9},{9... | collective-permute-start | bytes 786440 | tf_op jit(solution)/shard_map/ppermute | solution.py:411
  24.4 15.4 %collective-permute-start.5 = (bf16[64,2048]{1,0:T(8,128)(2,1)S(1)}, bf16[64,2048]{1,0:T(8,128)(2,1)S(1)}, u32[]{:S(2)}, u32[]{:S(2)}) collective-permute-start(bf16[64,2048]{1,0:T(8,128)(2,1)S(1)} %collective-permute-done.3.refs_4_), channel_id=1, source_target_pairs={{8,0},{16,8},{24,16},{28,24},{20,28},{12,20},{4,12},{0,4},{9,1},{1... | collective-permute-start | bytes 786440 | tf_op jit(solution)/shard_map/ppermute | solution.py:412
  30.0 10.8 %collective-permute-start.12 = (bf16[64,2048]{1,0:T(8,128)(2,1)S(1)}, bf16[64,2048]{1,0:T(8,128)(2,1)S(1)}, u32[]{:S(2)}, u32[]{:S(2)}) collective-permute-start(bf16[64,2048]{1,0:T(8,128)(2,1)S(1)} %collective-permute-done.10.refs_4_), channel_id=1, source_target_pairs={{8,0},{16,8},{24,16},{28,24},{20,28},{12,20},{4,12},{0,4},{9,1},{1... | collective-permute-start | bytes 786440 | tf_op jit(solution)/shard_map/ppermute | solution.py:412
  30.0 12.2 %collective-permute-start.4 = (bf16[64,2048]{1,0:T(8,128)(2,1)S(1)}, bf16[64,2048]{1,0:T(8,128)(2,1)S(1)}, u32[]{:S(2)}, u32[]{:S(2)}) collective-permute-start(bf16[64,2048]{1,0:T(8,128)(2,1)S(1)} %collective-permute-done.2.refs_3_), channel_id=1, source_target_pairs={{0,8},{8,16},{16,24},{24,28},{28,20},{20,12},{12,4},{4,0},{1,9},{9... | collective-permute-start | bytes 786440 | tf_op jit(solution)/shard_map/ppermute | solution.py:411
  32.0 2.2 %copy-start = (bf16[1024,2048]{1,0:T(8,128)(2,1)S(1)}, bf16[1024,2048]{1,0:T(8,128)(2,1)}, u32[]{:S(2)}) copy-start(bf16[1024,2048]{1,0:T(8,128)(2,1)} %refs_2_) | copy-start | bytes 12582916
  34.2 0.9 %copy-start.3 = (bf16[64,2048]{1,0:T(8,128)(2,1)S(1)}, bf16[64,2048]{1,0:T(8,128)(2,1)}, u32[]{:S(2)}) copy-start(bf16[64,2048]{1,0:T(8,128)(2,1)} %refs_0_.3) | copy-start | bytes 786436
  35.2 0.9 %copy-start.4 = (bf16[64,2048]{1,0:T(8,128)(2,1)S(1)}, bf16[64,2048]{1,0:T(8,128)(2,1)}, u32[]{:S(2)}) copy-start(bf16[64,2048]{1,0:T(8,128)(2,1)} %refs_0_.4) | copy-start | bytes 786436
  38.1 4.1 %copy-start.5 = (bf16[64,2048]{1,0:T(8,128)(2,1)S(1)}, bf16[64,2048]{1,0:T(8,128)(2,1)}, u32[]{:S(2)}) copy-start(bf16[64,2048]{1,0:T(8,128)(2,1)} %refs_0_.4) | copy-start | bytes 786436
  38.2 6.4 %collective-permute-start.17 = (bf16[64,2048]{1,0:T(8,128)(2,1)S(1)}, bf16[64,2048]{1,0:T(8,128)(2,1)S(1)}, u32[]{:S(2)}, u32[]{:S(2)}) collective-permute-start(bf16[64,2048]{1,0:T(8,128)(2,1)S(1)} %collective-permute-done.11.refs_5_), channel_id=1, source_target_pairs={{0,8},{8,16},{16,24},{24,28},{28,20},{20,12},{12,4},{4,0},{1,9},{9... | collective-permute-start | bytes 786440 | tf_op jit(solution)/shard_map/ppermute | solution.py:418
  39.8 6.4 %collective-permute-start.16 = (bf16[64,2048]{1,0:T(8,128)(2,1)S(1)}, bf16[64,2048]{1,0:T(8,128)(2,1)S(1)}, u32[]{:S(2)}, u32[]{:S(2)}) collective-permute-start(bf16[64,2048]{1,0:T(8,128)(2,1)S(1)} %collective-permute-done.5.refs_6_), channel_id=1, source_target_pairs={{8,0},{16,8},{24,16},{28,24},{20,28},{12,20},{4,12},{0,4},{9,1},{1... | collective-permute-start | bytes 786440 | tf_op jit(solution)/shard_map/ppermute | solution.py:419
  42.2 2.4 %copy-start.1 = (bf16[1024,2048]{1,0:T(8,128)(2,1)S(1)}, bf16[1024,2048]{1,0:T(8,128)(2,1)}, u32[]{:S(2)}) copy-start(bf16[1024,2048]{1,0:T(8,128)(2,1)} %refs_2_) | copy-start | bytes 12582916
  43.6 4.9 %collective-permute-start.14 = (f32[1,128,1024]{2,1,0:T(8,128)S(1)}, f32[1,128,1024]{2,1,0:T(8,128)S(1)}, u32[]{:S(2)}, u32[]{:S(2)}) collective-permute-start(f32[1,128,1024]{2,1,0:T(8,128)S(1)} %get-tuple-element.49), channel_id=1, source_target_pairs={{0,1},{1,0},{2,3},{3,2},{4,5},{5,4},{6,7},{7,6},{8,9},{9,8},{10,11... | collective-permute-start | bytes 1572872 | tf_op jit(solution)/shard_map/ppermute | solution.py:395
  46.2 1.4 %copy-start.2 = (bf16[256,1024]{1,0:T(8,128)(2,1)S(1)}, bf16[256,1024]{1,0:T(8,128)(2,1)}, u32[]{:S(2)}) copy-start(bf16[256,1024]{1,0:T(8,128)(2,1)} %shard_map.86.refs_0_) | copy-start | bytes 1572868
  47.5 2.0 %collective-permute-start.19 = (f32[1,128,1024]{2,1,0:T(8,128)S(1)}, f32[1,128,1024]{2,1,0:T(8,128)S(1)}, u32[]{:S(2)}, u32[]{:S(2)}) collective-permute-start(f32[1,128,1024]{2,1,0:T(8,128)S(1)} %get-tuple-element.59), channel_id=1, source_target_pairs={{0,1},{1,0},{2,3},{3,2},{4,5},{5,4},{6,7},{7,6},{8,9},{9,8},{10,11... | collective-permute-start | bytes 1572872 | tf_op jit(solution)/shard_map/ppermute | solution.py:395
  47.5 3.6 %collective-permute-start.21 = (bf16[256,1024]{1,0:T(8,128)(2,1)S(1)}, bf16[256,1024]{1,0:T(8,128)(2,1)S(1)}, u32[]{:S(2)}, u32[]{:S(2)}) collective-permute-start(bf16[256,1024]{1,0:T(8,128)(2,1)S(1)} %copy-done.2), channel_id=1, source_target_pairs={{0,1},{1,0},{2,3},{3,2},{4,5},{5,4},{6,7},{7,6},{8,9},{9,8},{10,11... | collective-permute-start | bytes 1572872 | tf_op jit(solution)/shard_map/ppermute | solution.py:395
  48.0 3.7 %collective-permute-start.22 = (bf16[256,1024]{1,0:T(8,128)(2,1)S(1)}, bf16[256,1024]{1,0:T(8,128)(2,1)S(1)}, u32[]{:S(2)}, u32[]{:S(2)}) collective-permute-start(bf16[256,1024]{1,0:T(8,128)(2,1)S(1)} %collective-permute-done.6.refs_1_), channel_id=1, source_target_pairs={{0,1},{1,0},{2,3},{3,2},{4,5},{5,4},{6,7},{7,6},{8,9},{9,8},{10,11... | collective-permute-start | bytes 1572872 | tf_op jit(solution)/shard_map/ppermute | solution.py:395
  48.1 12.8 %collective-permute-start.13 = (f32[128,1024]{1,0:T(8,128)S(1)}, f32[128,1024]{1,0:T(8,128)S(1)}, u32[]{:S(2)}, u32[]{:S(2)}) collective-permute-start(f32[128,1024]{1,0:T(8,128)S(1)} %get-tuple-element.47), channel_id=1, source_target_pairs={{0,1},{1,0},{2,3},{3,2},{4,5},{5,4},{6,7},{7,6},{8,9},{9,8},{10,11... | collective-permute-start | bytes 1572872 | tf_op jit(solution)/shard_map/ppermute | solution.py:395
  48.5 12.3 %collective-permute-start.18 = (f32[128,1024]{1,0:T(8,128)S(1)}, f32[128,1024]{1,0:T(8,128)S(1)}, u32[]{:S(2)}, u32[]{:S(2)}) collective-permute-start(f32[128,1024]{1,0:T(8,128)S(1)} %get-tuple-element.57), channel_id=1, source_target_pairs={{0,1},{1,0},{2,3},{3,2},{4,5},{5,4},{6,7},{7,6},{8,9},{9,8},{10,11... | collective-permute-start | bytes 1572872 | tf_op jit(solution)/shard_map/ppermute | solution.py:395
  49.4 11.5 %collective-permute-start.15 = (s16[128,1024]{1,0:T(8,128)(2,1)S(1)}, s16[128,1024]{1,0:T(8,128)(2,1)S(1)}, u32[]{:S(2)}, u32[]{:S(2)}) collective-permute-start(s16[128,1024]{1,0:T(8,128)(2,1)S(1)} %shard_map.89), channel_id=1, source_target_pairs={{0,2},{1,3},{2,0},{3,1},{4,6},{5,7},{6,4},{7,5},{8,10},{9,11},{10,... | collective-permute-start | bytes 786440 | tf_op jit(solution)/shard_map/ppermute | solution.py:398
  51.1 12.3 %collective-permute-start.20 = (s16[128,1024]{1,0:T(8,128)(2,1)S(1)}, s16[128,1024]{1,0:T(8,128)(2,1)S(1)}, u32[]{:S(2)}, u32[]{:S(2)}) collective-permute-start(s16[128,1024]{1,0:T(8,128)(2,1)S(1)} %shard_map.92), channel_id=1, source_target_pairs={{0,2},{1,3},{2,0},{3,1},{4,6},{5,7},{6,4},{7,5},{8,10},{9,11},{10,... | collective-permute-start | bytes 786440 | tf_op jit(solution)/shard_map/ppermute | solution.py:398
  52.6 10.8 %copy-start.6 = (s32[128,1024]{1,0:T(8,128)S(1)}, s32[128,1024]{1,0:T(8,128)}, u32[]{:S(2)}) copy-start(s32[128,1024]{1,0:T(8,128)} %refs_6_.1) | copy-start | bytes 1572868

commit v5 on v4

--- a/solution.py
+++ b/solution.py
@@ -19,6 +19,7 @@
 BY_LAST = (((1,), (1,)), ((), ()))
 BY_TOKEN = (((1,), (0,)), ((), ()))
 PAIR = 2
+BUFFERS = 4
 
 
 def ring_of(rows):
@@ -64,9 +65,9 @@
 
 
 def terms_of(lhs, weight, outs, kind):
-    cores, chips = len(outs) // 2, outs[-1].shape[0] + 1
+    cores, chips = len(outs), outs[0].shape[0]
     inner = weight.shape[0]
-    tile = min(256, inner)
+    tile = min(1024, inner)
     held = lhs.shape[0] // (cores * chips)
     rows = slice(kind * held, (kind + 1) * held)
     for i in range(inner // tile):
@@ -76,23 +77,17 @@
         )
         for n in range(cores * chips):
             core, chip = divmod(n, chips)
-            part = terms[n * held : (n + 1) * held, :]
-            if chip:
-                outs[cores + core][chip - 1, rows, span] = part
-            else:
-                outs[core][rows, span] = part
+            outs[core][chip, rows, span] = terms[n * held : (n + 1) * held, :]
 
 
 def terms_shapes(cols, held, inner):
     chips, cores = col_split(cols)
-    return [jax.ShapeDtypeStruct((2 * held, inner), jnp.float32)] * cores + [
-        jax.ShapeDtypeStruct((chips - 1, 2 * held, inner), jnp.float32)
-    ] * cores
+    return [jax.ShapeDtypeStruct((chips, 2 * held, inner), jnp.float32)] * cores
 
 
 def near_kernel(rows, cols, shifts, kind, *refs):
     count = len(shifts)
-    slots, weight, outs, order = refs[:count], refs[count], refs[-1 - 2 * col_split(cols)[1] : -1], refs[-1]
+    slots, weight, outs, order = refs[:count], refs[count], refs[-1 - col_split(cols)[1] : -1], refs[-1]
     held = slots[0].shape[0]
     for shift, slot in zip(shifts, slots):
         order[pl.ds(row_of(rows, cols, shift, held), held), :] = slot[...]
@@ -115,7 +110,7 @@
 
 
 def far_kernel(rows, cols, kind, *refs):
-    last, weight, outs, order = refs[1], refs[2], refs[-1 - 2 * col_split(cols)[1] : -1], refs[-1]
+    last, weight, outs, order = refs[1], refs[2], refs[-1 - col_split(cols)[1] : -1], refs[-1]
     held = last.shape[0]
     order[pl.ds(row_of(rows, cols, rows // 2, held), held), :] = last[...]
     terms_of(order[cols * held :, :], weight, outs, kind)
@@ -156,9 +151,9 @@
 
 
 def sum_kernel(*refs):
-    others = refs[0].shape[0]
+    others = refs[0].shape[0] - 1
     parts, outs = refs[:-others], refs[-others:]
-    for k, out in enumerate(outs):
+    for k, out in enumerate(outs, 1):
         total = parts[0][k]
         for part in parts[1:]:
             total = total + part[k]
@@ -166,48 +161,56 @@
 
 
 def coded_sums(parts):
-    others, rows, width = parts[0].shape
+    chips, rows, width = parts[0].shape
     return pl.pallas_call(
         sum_kernel,
         in_specs=[HERE] * len(parts),
-        out_specs=[HERE] * others,
-        out_shape=[jax.ShapeDtypeStruct((rows, width), jnp.int16)] * others,
+        out_specs=[HERE] * (chips - 1),
+        out_shape=[jax.ShapeDtypeStruct((rows, width), jnp.int16)] * (chips - 1),
         compiler_params=pltpu.CompilerParams(vmem_limit_bytes=VMEM_LIMIT),
     )(*parts)
 
 
-def gate_kernel(rows, cols, near, far, *refs):
-    rounds, (active, *outs) = refs[:-3], refs[-3:]
-    rounds = rounds[: near + far], rounds[near + far :]
+def gate_kernel(rows, n, near, far, *refs):
+    parts, active = refs[: near + far], refs[near + far]
+    outs, (work, sems) = refs[-4:-2], refs[-2:]
     held = active.shape[0] // PAIR
     here, col = on_ring(lax.axis_index("row"), rows), lax.axis_index("col")
     first = apart(here, on_ring(PAIR * col, rows), rows)
     second = apart(here, on_ring(PAIR * col + 1, rows), rows)
-    halves = lax.select(first < second, 0, 1), lax.select(first < second, 1, 0)
-    for half, parts in zip(halves, rounds):
-        span = pl.ds(pl.multiple_of(half * held, held), held)
-        gate = active[span, :].astype(jnp.float32)
-        for n, out in enumerate(outs):
-            mine = slice(n * held, (n + 1) * held)
-            total = parts[0][mine, :]
-            for part in parts[1:near]:
-                total = total + part[mine, :]
-            for part in parts[near:]:
-                total = total + decoded(part, mine)
-            out[span, :] = gate * total
-
-
-def gated(rows, cols, rounds, active):
-    near, far = rounds[0]
-    parts = [part for found in rounds for kind in found for part in kind]
-    size = active.size
-    return pl.pallas_call(
-        functools.partial(gate_kernel, rows, cols, len(near), len(far)),
-        in_specs=[HERE] * (len(parts) + 1),
-        out_specs=[HERE] * 2,
+    half = lax.select(first < second, n, 1 - n)
+    span = pl.ds(pl.multiple_of(half * held, held), held)
+    gate = active[span, :].astype(jnp.float32)
+    copies = []
+    for kind, out in enumerate(outs):
+        mine = slice(kind * held, (kind + 1) * held)
+        total = parts[0][0, mine, :]
+        for part in parts[1:near]:
+            total = total + part[0, mine, :]
+        for part in parts[near:]:
+            total = total + decoded(part, mine)
+        work[mine, :] = gate * total
+        copies.append(pltpu.make_async_copy(work.at[pl.ds(kind * held, held), :], out.at[span, :], sems.at[kind]))
+        copies[kind].start()
+    for copy in copies:
+        copy.wait()
+
+
+def gated(rows, n, found, active, begun=()):
+    near, far = found
+    parts = [*near, *far]
+    return pl.pallas_call(
+        functools.partial(gate_kernel, rows, n, len(near), len(far)),
+        in_specs=[HERE] * (len(parts) + 1) + [ANYWHERE] * len(begun),
+        out_specs=[ANYWHERE] * 2,
         out_shape=[jax.ShapeDtypeStruct(active.shape, jnp.float32)] * 2,
-        compiler_params=pltpu.CompilerParams(vmem_limit_bytes=VMEM_LIMIT),
-    )(*parts, active)
+        scratch_shapes=[
+            pltpu.VMEM(active.shape, jnp.float32),
+            pltpu.SemaphoreType.DMA((2,)),
+        ],
+        input_output_aliases={len(parts) + 1 + k: k for k in range(len(begun))},
+        compiler_params=pltpu.CompilerParams(vmem_limit_bytes=VMEM_LIMIT),
+    )(*parts, active, *begun)
 
 
 def parts_kernel(weight, *refs):
@@ -215,9 +218,10 @@
     tile = min(256, weight.shape[0])
     for start in range(0, weight.shape[0], tile):
         span = slice(start, start + tile)
-        w = weight[span, :].astype(jnp.float32)
-        magnitude[span, :] = jnp.abs(w).astype(jnp.bfloat16)
-        sign[span, :] = jnp.where(w > 0, 1.0, jnp.where(w < 0, -1.0, 0.0)).astype(jnp.bfloat16)
+        w = weight[span, :]
+        one = jnp.ones_like(w)
+        magnitude[span, :] = jnp.abs(w)
+        sign[span, :] = jnp.where(w > 0, one, jnp.where(w < 0, -one, jnp.zeros_like(w)))
 
 
 def parts_of(weight, *held):
@@ -342,28 +346,21 @@
 
 def weight_kernel(scale, center, radius, grad_c, grad_r, sign, out, parts, sems):
     tile = parts.shape[2]
-    spans = [slice(start, start + tile) for start in range(0, out.shape[1], tile)]
     copies = []
-
-    def products(span):
-        return [
+    for n in range(out.shape[1] // tile):
+        span = slice(n * tile, (n + 1) * tile)
+        part, sem = parts.at[n % BUFFERS], sems.at[n % BUFFERS]
+        if n >= BUFFERS:
+            copies[n - BUFFERS].wait()
+        through_center, through_radius = (
             lax.dot_general(ref[...], grad[:, span], BY_TOKEN, preferred_element_type=jnp.float32)
             for ref, grad in ((center, grad_c), (radius, grad_r))
-        ]
-
-    ahead = products(spans[0])
-    for n, span in enumerate(spans):
-        through_center, through_radius = ahead
-        if n + 1 < len(spans):
-            ahead = products(spans[n + 1])
-        part, sem = parts.at[n % 2], sems.at[n % 2]
-        if n >= 2:
-            copies[n - 2].wait()
+        )
         signed = sign[:, span].astype(jnp.float32) * through_radius
         part[...] = (through_center + signed) * scale
         copies.append(pltpu.make_async_copy(part, out.at[:, pl.ds(n * tile, tile)], sem))
         copies[n].start()
-    for copy in copies[-2:]:
+    for copy in copies[-BUFFERS:]:
         copy.wait()
 
 
@@ -376,7 +373,10 @@
         in_specs=[HERE] * 5,
         out_specs=ANYWHERE,
         out_shape=jax.ShapeDtypeStruct((inner, width), jnp.float32),
-        scratch_shapes=[pltpu.VMEM((2, inner, tile), jnp.float32), pltpu.SemaphoreType.DMA((2,))],
+        scratch_shapes=[
+            pltpu.VMEM((BUFFERS, inner, tile), jnp.float32),
+            pltpu.SemaphoreType.DMA((BUFFERS,)),
+        ],
         compiler_params=pltpu.CompilerParams(vmem_limit_bytes=VMEM_LIMIT),
     )(*inputs, *grads, sign)
 
@@ -398,9 +398,8 @@
         return lax.ppermute(value, "col", [(i, (i + k * cores) % cols) for i in range(cols)])
 
     def summed(terms):
-        own, others = ([found[0]] + [swap_cores(found[j], j) for j in range(1, cores)]
-                       for found in (terms[:cores], terms[cores:]))
-        return own, [hop_chips(value, k + 1) for k, value in enumerate(coded_sums(others))]
+        parts = [terms[0]] + [swap_cores(terms[j], j) for j in range(1, cores)]
+        return parts, [hop_chips(value, k + 1) for k, value in enumerate(coded_sums(parts))]
 
     both = packed(center, radius)
     inputs = [both] + [hop_chips(both, -k) for k in range(1, chips)]
@@ -410,7 +409,7 @@
         for slots in (slots_c, slots_r):
             slots[step] = lax.ppermute(slots[step - 1], "row", clockwise)
             slots[-step] = lax.ppermute(slots[1 - step], "row", counter)
-    magnitude, sign = parts_of(weight, grad_center, grad_radius)
+    magnitude, sign = parts_of(weight)
     slots_r[1 - last], weight, magnitude = lax.optimization_barrier(
         (slots_r[1 - last], weight, magnitude)
     )
@@ -428,12 +427,13 @@
     terms, order_c = far_terms(rows, cols, order_c, lasts[0], weight, 0)
     terms, order_r = far_terms(rows, cols, order_r, lasts[1], magnitude, 1, terms)
     far = summed(terms)
-    orders = order_c, order_r
-    inputs, _ = lax.optimization_barrier((inputs, orders))
+    inputs, _ = lax.optimization_barrier((inputs, (order_c, order_r)))
     for j in range(1, cores):
         inputs += [swap_cores(value, -j) for value in inputs[:chips]]
-    weight_grad = weight_terms(turned(rows, cols, inputs), orders, sign)
-    return *gated(rows, cols, (near, far), active), weight_grad
+    inputs = turned(rows, cols, inputs)
+    weight_grad = weight_terms(inputs, (order_c, order_r), sign)
+    begun = gated(rows, 0, near, active)
+    return *gated(rows, 1, far, active, begun), weight_grad
 
 
 def solution(mesh):

time: 64.9 us -> 64 us (0.986)
  Pallas kernels: 19.9 us -> 17.6 us
  waiting for transfers between devices: 19 us -> 21 us
  local copies, waits for them, and re-layouts: 4.11 us -> 2.87 us
    ppermute x6, waiting for transfers between devices: 2.92 us -> 6.69 us  [on_device(): slots[step] = lax.ppermute(slots[step - 1], 'row', clockwise)]
    pallas_call x1, Pallas kernels: 8.26 us -> 6.22 us  [weight_terms(): pl.pallas_call(functools.partial(weight_kernel, scale), in_specs=[HERE] *...]
    unnamed x14 -> x12, local copies, waits for them, and re-layouts: 4.11 us -> 2.87 us
    ppermute x3, starting transfers between devices: 4.06 us -> 5.1 us  [hop_chips(): lax.ppermute(value, 'col', [(i, (i + k * cores) % cols) for i in range(co...]
    pallas_call x1, Pallas kernels: 2 us -> 1.07 us  [parts_of(): pl.pallas_call(parts_kernel, in_specs=[HERE] * (1 + len(held)), out_specs...]
    ppermute x1, waiting for transfers between devices: 0.89 us -> 0.01 us  [on_device(): lax.ppermute(slots_c[last - 1], 'row', clockwise)]
    pallas_call x1 -> x2, Pallas kernels: 1.23 us -> 1.9 us  [gated(): pl.pallas_call(functools.partial(gate_kernel, rows, n, len(near), len(far...]
  transfers between devices with their start and end apart: 23 -> 21, of which waited for: 9 -> 7; matrix products, arithmetic and copies ran while one was open for 0% -> 0% of each run, Pallas kernels for 29% -> 26%
where the time goes in v5:
time: 64 us; the launch traced here: 63.7 us
  starting transfers between devices  21.3 us (33%)
  waiting for transfers between devices  21 us (33%)
  Pallas kernels  17.6 us (28%)
  local copies, waits for them, and re-layouts  2.87 us (4%)
  between operations  0.99 us (2%)
    ppermute x6, starting transfers between devices, on_device(): slots[step] = lax.ppermute(slots[step - 1], 'row', clockwise)  11.4 us
    ppermute x6, waiting for transfers between devices, on_device(): slots[-step] = lax.ppermute(slots[1 - step], 'row', counter)  11.3 us
    ppermute x6, waiting for transfers between devices, on_device(): slots[step] = lax.ppermute(slots[step - 1], 'row', clockwise)  6.69 us
    pallas_call x1, Pallas kernels, weight_terms(): pl.pallas_call(functools.partial(weight_kernel, scale), in_specs=[HERE] *...  6.22 us
    ppermute x3, starting transfers between devices, hop_chips(): lax.ppermute(value, 'col', [(i, (i + k * cores) % cols) for i in range(co...  5.1 us
    unnamed x12, local copies, waits for them, and re-layouts  2.87 us
    pallas_call x2, Pallas kernels, near_terms(): pl.pallas_call(functools.partial(near_kernel, rows, cols, shifts, kind),...  2.8 us
    ppermute x3, waiting for transfers between devices, hop_chips(): lax.ppermute(value, 'col', [(i, (i + k * cores) % cols) for i in range(co...  2.63 us
  transfers between devices with their start and end apart: 21, of which 7 were waited for; matrix products, arithmetic and copies ran while one was open for 0% of the time, Pallas kernels for 26%

profile of v5, /device:TPU:0, one launch (start us, length us, event | category | flops | bytes accessed | tf_op | source)
XLA Modules:
  0.0 63.7 jit_solution(9320374604548694674)
XLA Ops:
  0.6 3.1 %collective-permute-start.7 = (bf16[64,2048]{1,0:T(8,128)(2,1)}, bf16[64,2048]{1,0:T(8,128)(2,1)S(1)}, u32[]{:S(2)}, u32[]{:S(2)}) collective-permute-start(bf16[64,2048]{1,0:T(8,128)(2,1)} %refs_0_.1), channel_id=1, source_target_pairs={{0,8},{8,16},{16,24},{24,28},{28,20},{20,12},{12,4},{4,0},{1,9},{9... | collective-permute-start | bytes 786440 | tf_op jit(solution)/shard_map/ppermute | solution.py:410
  3.7 2.0 %collective-permute-start.8 = (bf16[64,2048]{1,0:T(8,128)(2,1)}, bf16[64,2048]{1,0:T(8,128)(2,1)S(1)}, u32[]{:S(2)}, u32[]{:S(2)}) collective-permute-start(bf16[64,2048]{1,0:T(8,128)(2,1)} %refs_0_.1), channel_id=1, source_target_pairs={{8,0},{16,8},{24,16},{28,24},{20,28},{12,20},{4,12},{0,4},{9,1},{1... | collective-permute-start | bytes 786440 | tf_op jit(solution)/shard_map/ppermute | solution.py:411
  5.8 5.2 %collective-permute-done.7.refs_1_ = bf16[64,2048]{1,0:T(8,128)(2,1)S(1)} collective-permute-done((bf16[64,2048]{1,0:T(8,128)(2,1)}, bf16[64,2048]{1,0:T(8,128)(2,1)S(1)}, u32[]{:S(2)}, u32[]{:S(2)}) %collective-permute-start.7) | collective-permute-done | bytes 262176 | tf_op jit(solution)/shard_map/ppermute | solution.py:410
  11.0 2.1 %collective-permute-start.9 = (bf16[64,2048]{1,0:T(8,128)(2,1)S(1)}, bf16[64,2048]{1,0:T(8,128)(2,1)S(1)}, u32[]{:S(2)}, u32[]{:S(2)}) collective-permute-start(bf16[64,2048]{1,0:T(8,128)(2,1)S(1)} %collective-permute-done.7.refs_1_), channel_id=1, source_target_pairs={{0,8},{8,16},{16,24},{24,28},{28,20},{20,12},{12,4},{4,0},{1,9},{9... | collective-permute-start | bytes 786440 | tf_op jit(solution)/shard_map/ppermute | solution.py:410
  13.2 1.8 %shard_map.86.refs_0_ = bf16[256,1024]{1,0:T(8,128)(2,1)} custom-call(bf16[128,1024]{1,0:T(8,128)(2,1)} %first.1, bf16[128,1024]{1,0:T(8,128)(2,1)} %second.1), custom_call_target="tpu_custom_call" | custom-call | tf_op jit(solution)/shard_map/pallas_call | solution.py:291
  15.0 2.0 %collective-permute-start.6 = (bf16[256,1024]{1,0:T(8,128)(2,1)}, bf16[256,1024]{1,0:T(8,128)(2,1)S(1)}, u32[]{:S(2)}, u32[]{:S(2)}) collective-permute-start(bf16[256,1024]{1,0:T(8,128)(2,1)} %shard_map.86.refs_0_), channel_id=1, source_target_pairs={{0,2},{1,3},{2,0},{3,1},{4,6},{5,7},{6,4},{7,5},{8,10},{9,11},{10,... | collective-permute-start | bytes 1572872 | tf_op jit(solution)/shard_map/ppermute | solution.py:398
  17.0 1.8 %collective-permute-done.8.refs_2_ = bf16[64,2048]{1,0:T(8,128)(2,1)S(1)} collective-permute-done((bf16[64,2048]{1,0:T(8,128)(2,1)}, bf16[64,2048]{1,0:T(8,128)(2,1)S(1)}, u32[]{:S(2)}, u32[]{:S(2)}) %collective-permute-start.8) | collective-permute-done | bytes 262176 | tf_op jit(solution)/shard_map/ppermute | solution.py:411
  18.8 2.0 %collective-permute-start.2 = (bf16[64,2048]{1,0:T(8,128)(2,1)S(1)}, bf16[64,2048]{1,0:T(8,128)(2,1)S(1)}, u32[]{:S(2)}, u32[]{:S(2)}) collective-permute-start(bf16[64,2048]{1,0:T(8,128)(2,1)S(1)} %collective-permute-done.refs_1_), channel_id=1, source_target_pairs={{0,8},{8,16},{16,24},{24,28},{28,20},{20,12},{12,4},{4,0},{1,9},{9... | collective-permute-start | bytes 786440 | tf_op jit(solution)/shard_map/ppermute | solution.py:410
  20.8 1.4 %collective-permute-done.9.refs_3_ = bf16[64,2048]{1,0:T(8,128)(2,1)S(1)} collective-permute-done((bf16[64,2048]{1,0:T(8,128)(2,1)S(1)}, bf16[64,2048]{1,0:T(8,128)(2,1)S(1)}, u32[]{:S(2)}, u32[]{:S(2)}) %collective-permute-start.9) | collective-permute-done | bytes 262176 | tf_op jit(solution)/shard_map/ppermute | solution.py:410
  22.2 2.1 %collective-permute-start.11 = (bf16[64,2048]{1,0:T(8,128)(2,1)S(1)}, bf16[64,2048]{1,0:T(8,128)(2,1)S(1)}, u32[]{:S(2)}, u32[]{:S(2)}) collective-permute-start(bf16[64,2048]{1,0:T(8,128)(2,1)S(1)} %collective-permute-done.9.refs_3_), channel_id=1, source_target_pairs={{0,8},{8,16},{16,24},{24,28},{28,20},{20,12},{12,4},{4,0},{1,9},{9... | collective-permute-start | bytes 786440 | tf_op jit(solution)/shard_map/ppermute | solution.py:410
  24.4 5.6 %collective-permute-done.10.refs_4_ = bf16[64,2048]{1,0:T(8,128)(2,1)S(1)} collective-permute-done((bf16[64,2048]{1,0:T(8,128)(2,1)S(1)}, bf16[64,2048]{1,0:T(8,128)(2,1)S(1)}, u32[]{:S(2)}, u32[]{:S(2)}) %collective-permute-start.10) | collective-permute-done | bytes 262176 | tf_op jit(solution)/shard_map/ppermute | solution.py:411
  30.0 2.0 %collective-permute-start.4 = (bf16[64,2048]{1,0:T(8,128)(2,1)S(1)}, bf16[64,2048]{1,0:T(8,128)(2,1)S(1)}, u32[]{:S(2)}, u32[]{:S(2)}) collective-permute-start(bf16[64,2048]{1,0:T(8,128)(2,1)S(1)} %collective-permute-done.2.refs_3_), channel_id=1, source_target_pairs={{0,8},{8,16},{16,24},{24,28},{28,20},{20,12},{12,4},{4,0},{1,9},{9... | collective-permute-start | bytes 786440 | tf_op jit(solution)/shard_map/ppermute | solution.py:410
  32.0 2.2 %copy-done = bf16[1024,2048]{1,0:T(8,128)(2,1)S(1)} copy-done((bf16[1024,2048]{1,0:T(8,128)(2,1)S(1)}, bf16[1024,2048]{1,0:T(8,128)(2,1)}, u32[]{:S(2)}) %copy-start) | copy-done | bytes 4194328
  34.2 1.1 %shard_map.85 = (bf16[1024,2048]{1,0:T(8,128)(2,1)S(1)}, bf16[1024,2048]{1,0:T(8,128)(2,1)S(1)}) custom-call(bf16[1024,2048]{1,0:T(8,128)(2,1)S(1)} %copy-done), custom_call_target="tpu_custom_call" | custom-call | tf_op jit(solution)/shard_map/pallas_call | solution.py:228
  35.3 1.6 %collective-permute-start.14 = (bf16[64,2048]{1,0:T(8,128)(2,1)S(1)}, bf16[64,2048]{1,0:T(8,128)(2,1)S(1)}, u32[]{:S(2)}, u32[]{:S(2)}) collective-permute-start(bf16[64,2048]{1,0:T(8,128)(2,1)S(1)} %collective-permute-done.11.refs_5_), channel_id=1, source_target_pairs={{0,8},{8,16},{16,24},{24,28},{28,20},{20,12},{12,4},{4,0},{1,9},{9... | collective-permute-start | bytes 786440 | tf_op jit(solution)/shard_map/ppermute | solution.py:417
  37.0 0.5 collective-permute-start.13
  37.4 3.8 %collective-permute-done.12.refs_6_ = bf16[64,2048]{1,0:T(8,128)(2,1)S(1)} collective-permute-done((bf16[64,2048]{1,0:T(8,128)(2,1)S(1)}, bf16[64,2048]{1,0:T(8,128)(2,1)S(1)}, u32[]{:S(2)}, u32[]{:S(2)}) %collective-permute-start.12) | collective-permute-done | bytes 262176 | tf_op jit(solution)/shard_map/ppermute | solution.py:411
  41.2 1.4 %shard_map.87 = (f32[2,128,1024]{2,1,0:T(8,128)S(1)}, f32[2,128,1024]{2,1,0:T(8,128)S(1)}, bf16[512,2048]{1,0:T(8,128)(2,1)S(1)}) custom-call(bf16[64,2048]{1,0:T(8,128)(2,1)S(1)} %copy-done.4, bf16[64,2048]{1,0:T(8,128)(2,1)S(1)} %collective-permute-done.7.refs_1_, bf16[64,2048]{1,0:T(8,128)(2,1)S(1)} %collective-permute-done.8.refs_2_, ...), custom_call_target="tpu_custom_call" | custom-call | tf_op jit(solution)/shard_map/pallas_call | solution.py:101
  42.7 1.4 %shard_map.88 = (f32[2,128,1024]{2,1,0:T(8,128)S(1)}, f32[2,128,1024]{2,1,0:T(8,128)S(1)}, bf16[512,2048]{1,0:T(8,128)(2,1)S(1)}) custom-call(bf16[64,2048]{1,0:T(8,128)(2,1)S(1)} %copy-done.5, bf16[64,2048]{1,0:T(8,128)(2,1)S(1)} %collective-permute-done.refs_1_, ...), custom_call_target="tpu_custom_call", output_to_operand_aliasing={{0}: (8, {}), {1}: (9, {})} | custom-call | tf_op jit(solution)/shard_map/pallas_call | solution.py:101
  44.2 0.7 %copy-done.1 = bf16[1024,2048]{1,0:T(8,128)(2,1)S(1)} copy-done((bf16[1024,2048]{1,0:T(8,128)(2,1)S(1)}, bf16[1024,2048]{1,0:T(8,128)(2,1)}, u32[]{:S(2)}) %copy-start.1) | copy-done | bytes 4194328
  44.8 1.3 %shard_map.89 = (f32[2,128,1024]{2,1,0:T(8,128)S(1)}, f32[2,128,1024]{2,1,0:T(8,128)S(1)}, bf16[512,2048]{1,0:T(8,128)(2,1)S(1)}) custom-call(bf16[512,2048]{1,0:T(8,128)(2,1)S(1)} %get-tuple-element.39.refs_0_, bf16[64,2048]{1,0:T(8,128)(2,1)S(1)} %collective-permute-done.14.refs_1_, bf16[1024,2048]{1,0:T(8,128)(2,1)S(1)} %copy-done.1), custom_call_target="tpu_custom_call", output_to_operand_aliasing={{2}: (0, {})} | custom-call | tf_op jit(solution)/shard_map/pallas_call | solution.py:122
  46.2 1.3 %shard_map.90 = (f32[2,128,1024]{2,1,0:T(8,128)S(1)}, f32[2,128,1024]{2,1,0:T(8,128)S(1)}, bf16[512,2048]{1,0:T(8,128)(2,1)S(1)}) custom-call(bf16[512,2048]{1,0:T(8,128)(2,1)S(1)} %get-tuple-element.38.refs_0_, bf16[64,2048]{1,0:T(8,128)(2,1)S(1)} %collective-permute-done.13.refs_1_, ...), custom_call_target="tpu_custom_call", output_to_operand_aliasing={{2}: (0, {}), {0}: (3, {}), {1}: (4, {})} | custom-call | tf_op jit(solution)/shard_map/pallas_call | solution.py:122
  47.5 0.5 collective-permute-start.19
  48.3 1.6 %collective-permute-start.18 = (s16[128,1024]{1,0:T(8,128)(2,1)S(1)}, s16[128,1024]{1,0:T(8,128)(2,1)S(1)}, u32[]{:S(2)}, u32[]{:S(2)}) collective-permute-start(s16[128,1024]{1,0:T(8,128)(2,1)S(1)} %shard_map.92), channel_id=1, source_target_pairs={{0,2},{1,3},{2,0},{3,1},{4,6},{5,7},{6,4},{7,5},{8,10},{9,11},{10,... | collective-permute-start | bytes 786440 | tf_op jit(solution)/shard_map/ppermute | solution.py:398
  49.9 0.3 collective-permute-done.15.refs_1_
  50.2 0.2 shard_map.91
  50.4 1.6 %collective-permute-start.16 = (s16[128,1024]{1,0:T(8,128)(2,1)S(1)}, s16[128,1024]{1,0:T(8,128)(2,1)S(1)}, u32[]{:S(2)}, u32[]{:S(2)}) collective-permute-start(s16[128,1024]{1,0:T(8,128)(2,1)S(1)} %shard_map.91), channel_id=1, source_target_pairs={{0,2},{1,3},{2,0},{3,1},{4,6},{5,7},{6,4},{7,5},{8,10},{9,11},{10,... | collective-permute-start | bytes 786440 | tf_op jit(solution)/shard_map/ppermute | solution.py:398
  51.9 0.9 %shard_map.95 = (bf16[1024,512]{1,0:T(8,128)(2,1)S(1)}, bf16[1024,512]{1,0:T(8,128)(2,1)S(1)}) custom-call(bf16[256,1024]{1,0:T(8,128)(2,1)S(1)} %copy-done.3, bf16[256,1024]{1,0:T(8,128)(2,1)S(1)} %collective-permute-done.6.refs_1_, bf16[256,1024]{1,0:T(8,128)(2,1)S(1)} %collective-permute-done.19.refs_2_, bf16[256,1024]{1,0:T(8,128)(2,1)S(1)} %collective-permute-done.20.refs_3_), custom_call_target="tpu_custom_call" | custom-call | tf_op jit(solution)/shard_map/pallas_call | solution.py:337
  52.8 6.2 %shard_map.96 = f32[1024,2048]{1,0:T(8,128)} custom-call(bf16[1024,512]{1,0:T(8,128)(2,1)S(1)} %get-tuple-element.56.center, bf16[1024,512]{1,0:T(8,128)(2,1)S(1)} %get-tuple-element.57.radius, bf16[512,2048]{1,0:T(8,128)(2,1)S(1)} %get-tuple-element.52.grad_c, bf16[512,2048]{1,0:T(8,128)(2,1)S(1)} %get-tuple-element.53.grad_r, ...), custom_call_target="tpu_custom_call" | custom-call | tf_op jit(solution)/shard_map/pallas_call | solution.py:371
  59.1 0.9 %shard_map.93 = (f32[128,1024]{1,0:T(8,128)}, f32[128,1024]{1,0:T(8,128)}) custom-call(f32[2,128,1024]{2,1,0:T(8,128)S(1)} %get-tuple-element.44.refs_0_, f32[2,128,1024]{2,1,0:T(8,128)S(1)} %collective-permute-done.17.refs_1_, s16[128,1024]{1,0:T(8,128)(2,1)S(1)} %collective-permute-done.18.refs_2_, s32[128,1024]{1,0:T(8,128)S(1)} %copy-done.2), custom_call_target="tpu_custom_call" | custom-call | tf_op jit(solution)/shard_map/pallas_call | solution.py:202
  60.0 2.6 %collective-permute-done.16.refs_2_ = s16[128,1024]{1,0:T(8,128)(2,1)S(1)} collective-permute-done((s16[128,1024]{1,0:T(8,128)(2,1)S(1)}, s16[128,1024]{1,0:T(8,128)(2,1)S(1)}, u32[]{:S(2)}, u32[]{:S(2)}) %collective-permute-start.16) | collective-permute-done | bytes 262176 | tf_op jit(solution)/shard_map/ppermute | solution.py:398
  62.6 0.9 %shard_map.94 = (f32[128,1024]{1,0:T(8,128)}, f32[128,1024]{1,0:T(8,128)}) custom-call(f32[2,128,1024]{2,1,0:T(8,128)S(1)} %get-tuple-element.42.refs_0_, f32[2,128,1024]{2,1,0:T(8,128)S(1)} %collective-permute-done.15.refs_1_, s16[128,1024]{1,0:T(8,128)(2,1)S(1)} %collective-permute-done.16.refs_2_, ...), custom_call_target="tpu_custom_call", output_to_operand_aliasing={{0}: (4, {}), {1}: (5, {})} | custom-call | tf_op jit(solution)/shard_map/pallas_call | solution.py:202
  (34 shorter events, 0.7 us)
Async XLA Ops:
  0.6 40.6 %copy-start.4 = (bf16[64,2048]{1,0:T(8,128)(2,1)S(1)}, bf16[64,2048]{1,0:T(8,128)(2,1)}, u32[]{:S(2)}) copy-start(bf16[64,2048]{1,0:T(8,128)(2,1)} %refs_0_.1) | copy-start | bytes 786436
  0.6 10.4 %collective-permute-start.7 = (bf16[64,2048]{1,0:T(8,128)(2,1)}, bf16[64,2048]{1,0:T(8,128)(2,1)S(1)}, u32[]{:S(2)}, u32[]{:S(2)}) collective-permute-start(bf16[64,2048]{1,0:T(8,128)(2,1)} %refs_0_.1), channel_id=1, source_target_pairs={{0,8},{8,16},{16,24},{24,28},{28,20},{20,12},{12,4},{4,0},{1,9},{9... | collective-permute-start | bytes 786440 | tf_op jit(solution)/shard_map/ppermute | solution.py:410
  3.7 9.4 %collective-permute-start.1 = (bf16[64,2048]{1,0:T(8,128)(2,1)}, bf16[64,2048]{1,0:T(8,128)(2,1)S(1)}, u32[]{:S(2)}, u32[]{:S(2)}) collective-permute-start(bf16[64,2048]{1,0:T(8,128)(2,1)} %refs_0_.2), channel_id=1, source_target_pairs={{8,0},{16,8},{24,16},{28,24},{20,28},{12,20},{4,12},{0,4},{9,1},{1... | collective-permute-start | bytes 786440 | tf_op jit(solution)/shard_map/ppermute | solution.py:411
  3.7 15.1 %collective-permute-start.8 = (bf16[64,2048]{1,0:T(8,128)(2,1)}, bf16[64,2048]{1,0:T(8,128)(2,1)S(1)}, u32[]{:S(2)}, u32[]{:S(2)}) collective-permute-start(bf16[64,2048]{1,0:T(8,128)(2,1)} %refs_0_.1), channel_id=1, source_target_pairs={{8,0},{16,8},{24,16},{28,24},{20,28},{12,20},{4,12},{0,4},{9,1},{1... | collective-permute-start | bytes 786440 | tf_op jit(solution)/shard_map/ppermute | solution.py:411
  5.7 13.1 %collective-permute-start = (bf16[64,2048]{1,0:T(8,128)(2,1)}, bf16[64,2048]{1,0:T(8,128)(2,1)S(1)}, u32[]{:S(2)}, u32[]{:S(2)}) collective-permute-start(bf16[64,2048]{1,0:T(8,128)(2,1)} %refs_0_.2), channel_id=1, source_target_pairs={{0,8},{8,16},{16,24},{24,28},{28,20},{20,12},{12,4},{4,0},{1,9},{9... | collective-permute-start | bytes 786440 | tf_op jit(solution)/shard_map/ppermute | solution.py:410
  11.0 11.2 %collective-permute-start.9 = (bf16[64,2048]{1,0:T(8,128)(2,1)S(1)}, bf16[64,2048]{1,0:T(8,128)(2,1)S(1)}, u32[]{:S(2)}, u32[]{:S(2)}) collective-permute-start(bf16[64,2048]{1,0:T(8,128)(2,1)S(1)} %collective-permute-done.7.refs_1_), channel_id=1, source_target_pairs={{0,8},{8,16},{16,24},{24,28},{28,20},{20,12},{12,4},{4,0},{1,9},{9... | collective-permute-start | bytes 786440 | tf_op jit(solution)/shard_map/ppermute | solution.py:410
  13.2 11.2 %collective-permute-start.3 = (bf16[64,2048]{1,0:T(8,128)(2,1)S(1)}, bf16[64,2048]{1,0:T(8,128)(2,1)S(1)}, u32[]{:S(2)}, u32[]{:S(2)}) collective-permute-start(bf16[64,2048]{1,0:T(8,128)(2,1)S(1)} %collective-permute-done.1.refs_2_), channel_id=1, source_target_pairs={{8,0},{16,8},{24,16},{28,24},{20,28},{12,20},{4,12},{0,4},{9,1},{1... | collective-permute-start | bytes 786440 | tf_op jit(solution)/shard_map/ppermute | solution.py:411
  13.2 29.5 %copy-start.5 = (bf16[64,2048]{1,0:T(8,128)(2,1)S(1)}, bf16[64,2048]{1,0:T(8,128)(2,1)}, u32[]{:S(2)}) copy-start(bf16[64,2048]{1,0:T(8,128)(2,1)} %refs_0_.2) | copy-start | bytes 786436
  15.0 22.4 %collective-permute-start.6 = (bf16[256,1024]{1,0:T(8,128)(2,1)}, bf16[256,1024]{1,0:T(8,128)(2,1)S(1)}, u32[]{:S(2)}, u32[]{:S(2)}) collective-permute-start(bf16[256,1024]{1,0:T(8,128)(2,1)} %shard_map.86.refs_0_), channel_id=1, source_target_pairs={{0,2},{1,3},{2,0},{3,1},{4,6},{5,7},{6,4},{7,5},{8,10},{9,11},{10,... | collective-permute-start | bytes 1572872 | tf_op jit(solution)/shard_map/ppermute | solution.py:398
  18.8 11.2 %collective-permute-start.10 = (bf16[64,2048]{1,0:T(8,128)(2,1)S(1)}, bf16[64,2048]{1,0:T(8,128)(2,1)S(1)}, u32[]{:S(2)}, u32[]{:S(2)}) collective-permute-start(bf16[64,2048]{1,0:T(8,128)(2,1)S(1)} %collective-permute-done.8.refs_2_), channel_id=1, source_target_pairs={{8,0},{16,8},{24,16},{28,24},{20,28},{12,20},{4,12},{0,4},{9,1},{1... | collective-permute-start | bytes 786440 | tf_op jit(solution)/shard_map/ppermute | solution.py:411
  18.8 11.2 %collective-permute-start.2 = (bf16[64,2048]{1,0:T(8,128)(2,1)S(1)}, bf16[64,2048]{1,0:T(8,128)(2,1)S(1)}, u32[]{:S(2)}, u32[]{:S(2)}) collective-permute-start(bf16[64,2048]{1,0:T(8,128)(2,1)S(1)} %collective-permute-done.refs_1_), channel_id=1, source_target_pairs={{0,8},{8,16},{16,24},{24,28},{28,20},{20,12},{12,4},{4,0},{1,9},{9... | collective-permute-start | bytes 786440 | tf_op jit(solution)/shard_map/ppermute | solution.py:410
  22.2 13.1 %collective-permute-start.11 = (bf16[64,2048]{1,0:T(8,128)(2,1)S(1)}, bf16[64,2048]{1,0:T(8,128)(2,1)S(1)}, u32[]{:S(2)}, u32[]{:S(2)}) collective-permute-start(bf16[64,2048]{1,0:T(8,128)(2,1)S(1)} %collective-permute-done.9.refs_3_), channel_id=1, source_target_pairs={{0,8},{8,16},{16,24},{24,28},{28,20},{20,12},{12,4},{4,0},{1,9},{9... | collective-permute-start | bytes 786440 | tf_op jit(solution)/shard_map/ppermute | solution.py:410
  24.4 12.6 %collective-permute-start.5 = (bf16[64,2048]{1,0:T(8,128)(2,1)S(1)}, bf16[64,2048]{1,0:T(8,128)(2,1)S(1)}, u32[]{:S(2)}, u32[]{:S(2)}) collective-permute-start(bf16[64,2048]{1,0:T(8,128)(2,1)S(1)} %collective-permute-done.3.refs_4_), channel_id=1, source_target_pairs={{8,0},{16,8},{24,16},{28,24},{20,28},{12,20},{4,12},{0,4},{9,1},{1... | collective-permute-start | bytes 786440 | tf_op jit(solution)/shard_map/ppermute | solution.py:411
  30.0 11.2 %collective-permute-start.12 = (bf16[64,2048]{1,0:T(8,128)(2,1)S(1)}, bf16[64,2048]{1,0:T(8,128)(2,1)S(1)}, u32[]{:S(2)}, u32[]{:S(2)}) collective-permute-start(bf16[64,2048]{1,0:T(8,128)(2,1)S(1)} %collective-permute-done.10.refs_4_), channel_id=1, source_target_pairs={{8,0},{16,8},{24,16},{28,24},{20,28},{12,20},{4,12},{0,4},{9,1},{1... | collective-permute-start | bytes 786440 | tf_op jit(solution)/shard_map/ppermute | solution.py:411
  30.0 12.7 %collective-permute-start.4 = (bf16[64,2048]{1,0:T(8,128)(2,1)S(1)}, bf16[64,2048]{1,0:T(8,128)(2,1)S(1)}, u32[]{:S(2)}, u32[]{:S(2)}) collective-permute-start(bf16[64,2048]{1,0:T(8,128)(2,1)S(1)} %collective-permute-done.2.refs_3_), channel_id=1, source_target_pairs={{0,8},{8,16},{16,24},{24,28},{28,20},{20,12},{12,4},{4,0},{1,9},{9... | collective-permute-start | bytes 786440 | tf_op jit(solution)/shard_map/ppermute | solution.py:410
  32.0 2.2 %copy-start = (bf16[1024,2048]{1,0:T(8,128)(2,1)S(1)}, bf16[1024,2048]{1,0:T(8,128)(2,1)}, u32[]{:S(2)}) copy-start(bf16[1024,2048]{1,0:T(8,128)(2,1)} %refs_2_) | copy-start | bytes 12582916
  35.3 8.9 %collective-permute-start.14 = (bf16[64,2048]{1,0:T(8,128)(2,1)S(1)}, bf16[64,2048]{1,0:T(8,128)(2,1)S(1)}, u32[]{:S(2)}, u32[]{:S(2)}) collective-permute-start(bf16[64,2048]{1,0:T(8,128)(2,1)S(1)} %collective-permute-done.11.refs_5_), channel_id=1, source_target_pairs={{0,8},{8,16},{16,24},{24,28},{28,20},{20,12},{12,4},{4,0},{1,9},{9... | collective-permute-start | bytes 786440 | tf_op jit(solution)/shard_map/ppermute | solution.py:417
  37.0 9.2 %collective-permute-start.13 = (bf16[64,2048]{1,0:T(8,128)(2,1)S(1)}, bf16[64,2048]{1,0:T(8,128)(2,1)S(1)}, u32[]{:S(2)}, u32[]{:S(2)}) collective-permute-start(bf16[64,2048]{1,0:T(8,128)(2,1)S(1)} %collective-permute-done.5.refs_6_), channel_id=1, source_target_pairs={{8,0},{16,8},{24,16},{28,24},{20,28},{12,20},{4,12},{0,4},{9,1},{1... | collective-permute-start | bytes 786440 | tf_op jit(solution)/shard_map/ppermute | solution.py:418
  42.7 2.2 %copy-start.1 = (bf16[1024,2048]{1,0:T(8,128)(2,1)S(1)}, bf16[1024,2048]{1,0:T(8,128)(2,1)}, u32[]{:S(2)}) copy-start(bf16[1024,2048]{1,0:T(8,128)(2,1)} %refs_2_) | copy-start | bytes 12582916
  44.1 4.0 %collective-permute-start.17 = (f32[2,128,1024]{2,1,0:T(8,128)S(1)}, f32[2,128,1024]{2,1,0:T(8,128)S(1)}, u32[]{:S(2)}, u32[]{:S(2)}) collective-permute-start(f32[2,128,1024]{2,1,0:T(8,128)S(1)} %get-tuple-element.45), channel_id=1, source_target_pairs={{0,1},{1,0},{2,3},{3,2},{4,5},{5,4},{6,7},{7,6},{8,9},{9,8},{10,11... | collective-permute-start | bytes 3145736 | tf_op jit(solution)/shard_map/ppermute | solution.py:395
  46.1 1.4 %copy-start.3 = (bf16[256,1024]{1,0:T(8,128)(2,1)S(1)}, bf16[256,1024]{1,0:T(8,128)(2,1)}, u32[]{:S(2)}) copy-start(bf16[256,1024]{1,0:T(8,128)(2,1)} %shard_map.86.refs_0_) | copy-start | bytes 1572868
  47.5 2.7 %collective-permute-start.15 = (f32[2,128,1024]{2,1,0:T(8,128)S(1)}, f32[2,128,1024]{2,1,0:T(8,128)S(1)}, u32[]{:S(2)}, u32[]{:S(2)}) collective-permute-start(f32[2,128,1024]{2,1,0:T(8,128)S(1)} %get-tuple-element.43), channel_id=1, source_target_pairs={{0,1},{1,0},{2,3},{3,2},{4,5},{5,4},{6,7},{7,6},{8,9},{9,8},{10,11... | collective-permute-start | bytes 3145736 | tf_op jit(solution)/shard_map/ppermute | solution.py:395
  47.5 4.4 %collective-permute-start.19 = (bf16[256,1024]{1,0:T(8,128)(2,1)S(1)}, bf16[256,1024]{1,0:T(8,128)(2,1)S(1)}, u32[]{:S(2)}, u32[]{:S(2)}) collective-permute-start(bf16[256,1024]{1,0:T(8,128)(2,1)S(1)} %copy-done.3), channel_id=1, source_target_pairs={{0,1},{1,0},{2,3},{3,2},{4,5},{5,4},{6,7},{7,6},{8,9},{9,8},{10,11... | collective-permute-start | bytes 1572872 | tf_op jit(solution)/shard_map/ppermute | solution.py:395
  48.0 3.9 %collective-permute-start.20 = (bf16[256,1024]{1,0:T(8,128)(2,1)S(1)}, bf16[256,1024]{1,0:T(8,128)(2,1)S(1)}, u32[]{:S(2)}, u32[]{:S(2)}) collective-permute-start(bf16[256,1024]{1,0:T(8,128)(2,1)S(1)} %collective-permute-done.6.refs_1_), channel_id=1, source_target_pairs={{0,1},{1,0},{2,3},{3,2},{4,5},{5,4},{6,7},{7,6},{8,9},{9,8},{10,11... | collective-permute-start | bytes 1572872 | tf_op jit(solution)/shard_map/ppermute | solution.py:395
  48.3 10.7 %collective-permute-start.18 = (s16[128,1024]{1,0:T(8,128)(2,1)S(1)}, s16[128,1024]{1,0:T(8,128)(2,1)S(1)}, u32[]{:S(2)}, u32[]{:S(2)}) collective-permute-start(s16[128,1024]{1,0:T(8,128)(2,1)S(1)} %shard_map.92), channel_id=1, source_target_pairs={{0,2},{1,3},{2,0},{3,1},{4,6},{5,7},{6,4},{7,5},{8,10},{9,11},{10,... | collective-permute-start | bytes 786440 | tf_op jit(solution)/shard_map/ppermute | solution.py:398
  50.4 12.3 %collective-permute-start.16 = (s16[128,1024]{1,0:T(8,128)(2,1)S(1)}, s16[128,1024]{1,0:T(8,128)(2,1)S(1)}, u32[]{:S(2)}, u32[]{:S(2)}) collective-permute-start(s16[128,1024]{1,0:T(8,128)(2,1)S(1)} %shard_map.91), channel_id=1, source_target_pairs={{0,2},{1,3},{2,0},{3,1},{4,6},{5,7},{6,4},{7,5},{8,10},{9,11},{10,... | collective-permute-start | bytes 786440 | tf_op jit(solution)/shard_map/ppermute | solution.py:398
  52.8 6.3 %copy-start.2 = (s32[128,1024]{1,0:T(8,128)S(1)}, s32[128,1024]{1,0:T(8,128)}, u32[]{:S(2)}) copy-start(s32[128,1024]{1,0:T(8,128)} %refs_3_.3) | copy-start | bytes 1572868

commit v6 on v5

--- a/solution.py
+++ b/solution.py
@@ -20,6 +20,7 @@
 BY_TOKEN = (((1,), (0,)), ((), ()))
 PAIR = 2
 BUFFERS = 4
+BLOCKS = 2
 
 
 def ring_of(rows):
@@ -67,7 +68,7 @@
 def terms_of(lhs, weight, outs, kind):
     cores, chips = len(outs), outs[0].shape[0]
     inner = weight.shape[0]
-    tile = min(1024, inner)
+    tile = min(256, inner)
     held = lhs.shape[0] // (cores * chips)
     rows = slice(kind * held, (kind + 1) * held)
     for i in range(inner // tile):
@@ -182,16 +183,23 @@
     span = pl.ds(pl.multiple_of(half * held, held), held)
     gate = active[span, :].astype(jnp.float32)
     copies = []
+    block = held // BLOCKS
     for kind, out in enumerate(outs):
-        mine = slice(kind * held, (kind + 1) * held)
-        total = parts[0][0, mine, :]
-        for part in parts[1:near]:
-            total = total + part[0, mine, :]
-        for part in parts[near:]:
-            total = total + decoded(part, mine)
-        work[mine, :] = gate * total
-        copies.append(pltpu.make_async_copy(work.at[pl.ds(kind * held, held), :], out.at[span, :], sems.at[kind]))
-        copies[kind].start()
+        for i in range(BLOCKS):
+            first = kind * held + i * block
+            mine = slice(first, first + block)
+            total = parts[0][0, mine, :]
+            for part in parts[1:near]:
+                total = total + part[0, mine, :]
+            for part in parts[near:]:
+                total = total + decoded(part, mine)
+            work[mine, :] = gate[i * block : (i + 1) * block, :] * total
+            to = pl.ds(pl.multiple_of(half * held + i * block, block), block)
+            copy = pltpu.make_async_copy(
+                work.at[pl.ds(first, block), :], out.at[to, :], sems.at[kind * BLOCKS + i]
+            )
+            copy.start()
+            copies.append(copy)
     for copy in copies:
         copy.wait()
 
@@ -206,7 +214,7 @@
         out_shape=[jax.ShapeDtypeStruct(active.shape, jnp.float32)] * 2,
         scratch_shapes=[
             pltpu.VMEM(active.shape, jnp.float32),
-            pltpu.SemaphoreType.DMA((2,)),
+            pltpu.SemaphoreType.DMA((2 * BLOCKS,)),
         ],
         input_output_aliases={len(parts) + 1 + k: k for k in range(len(begun))},
         compiler_params=pltpu.CompilerParams(vmem_limit_bytes=VMEM_LIMIT),

time: 64 us -> 63.9 us (level)
  no operation moved by 1% of the time
where the time goes in v6:
time: 63.9 us; the launch traced here: 63.7 us
  starting transfers between devices  21.3 us (33%)
  waiting for transfers between devices  21 us (33%)
  Pallas kernels  17.6 us (28%)
  local copies, waits for them, and re-layouts  2.87 us (4%)
  between operations  0.99 us (2%)
    ppermute x6, starting transfers between devices, on_device(): slots[step] = lax.ppermute(slots[step - 1], 'row', clockwise)  11.4 us
    ppermute x6, waiting for transfers between devices, on_device(): slots[-step] = lax.ppermute(slots[1 - step], 'row', counter)  11.3 us
    ppermute x6, waiting for transfers between devices, on_device(): slots[step] = lax.ppermute(slots[step - 1], 'row', clockwise)  6.69 us
    pallas_call x1, Pallas kernels, weight_terms(): pl.pallas_call(functools.partial(weight_kernel, scale), in_specs=[HERE] *...  6.22 us
    ppermute x3, starting transfers between devices, hop_chips(): lax.ppermute(value, 'col', [(i, (i + k * cores) % cols) for i in range(co...  5.1 us
    unnamed x12, local copies, waits for them, and re-layouts  2.87 us
    pallas_call x2, Pallas kernels, near_terms(): pl.pallas_call(functools.partial(near_kernel, rows, cols, shifts, kind),...  2.8 us
    ppermute x3, waiting for transfers between devices, hop_chips(): lax.ppermute(value, 'col', [(i, (i + k * cores) % cols) for i in range(co...  2.64 us
  transfers between devices with their start and end apart: 21, of which 7 were waited for; matrix products, arithmetic and copies ran while one was open for 0% of the time, Pallas kernels for 26%

profile of v6, /device:TPU:0, one launch (start us, length us, event | category | flops | bytes accessed | tf_op | source)
XLA Modules:
  0.0 63.7 jit_solution(18090522659855588318)
XLA Ops:
  0.6 3.1 %collective-permute-start.7 = (bf16[64,2048]{1,0:T(8,128)(2,1)}, bf16[64,2048]{1,0:T(8,128)(2,1)S(1)}, u32[]{:S(2)}, u32[]{:S(2)}) collective-permute-start(bf16[64,2048]{1,0:T(8,128)(2,1)} %refs_0_.1), channel_id=1, source_target_pairs={{0,8},{8,16},{16,24},{24,28},{28,20},{20,12},{12,4},{4,0},{1,9},{9... | collective-permute-start | bytes 786440 | tf_op jit(solution)/shard_map/ppermute | solution.py:418
  3.7 2.0 %collective-permute-start.8 = (bf16[64,2048]{1,0:T(8,128)(2,1)}, bf16[64,2048]{1,0:T(8,128)(2,1)S(1)}, u32[]{:S(2)}, u32[]{:S(2)}) collective-permute-start(bf16[64,2048]{1,0:T(8,128)(2,1)} %refs_0_.1), channel_id=1, source_target_pairs={{8,0},{16,8},{24,16},{28,24},{20,28},{12,20},{4,12},{0,4},{9,1},{1... | collective-permute-start | bytes 786440 | tf_op jit(solution)/shard_map/ppermute | solution.py:419
  5.8 5.2 %collective-permute-done.7.refs_1_ = bf16[64,2048]{1,0:T(8,128)(2,1)S(1)} collective-permute-done((bf16[64,2048]{1,0:T(8,128)(2,1)}, bf16[64,2048]{1,0:T(8,128)(2,1)S(1)}, u32[]{:S(2)}, u32[]{:S(2)}) %collective-permute-start.7) | collective-permute-done | bytes 262176 | tf_op jit(solution)/shard_map/ppermute | solution.py:418
  11.0 2.1 %collective-permute-start.9 = (bf16[64,2048]{1,0:T(8,128)(2,1)S(1)}, bf16[64,2048]{1,0:T(8,128)(2,1)S(1)}, u32[]{:S(2)}, u32[]{:S(2)}) collective-permute-start(bf16[64,2048]{1,0:T(8,128)(2,1)S(1)} %collective-permute-done.7.refs_1_), channel_id=1, source_target_pairs={{0,8},{8,16},{16,24},{24,28},{28,20},{20,12},{12,4},{4,0},{1,9},{9... | collective-permute-start | bytes 786440 | tf_op jit(solution)/shard_map/ppermute | solution.py:418
  13.2 1.8 %shard_map.86.refs_0_ = bf16[256,1024]{1,0:T(8,128)(2,1)} custom-call(bf16[128,1024]{1,0:T(8,128)(2,1)} %first.1, bf16[128,1024]{1,0:T(8,128)(2,1)} %second.1), custom_call_target="tpu_custom_call" | custom-call | tf_op jit(solution)/shard_map/pallas_call | solution.py:299
  15.0 2.0 %collective-permute-start.6 = (bf16[256,1024]{1,0:T(8,128)(2,1)}, bf16[256,1024]{1,0:T(8,128)(2,1)S(1)}, u32[]{:S(2)}, u32[]{:S(2)}) collective-permute-start(bf16[256,1024]{1,0:T(8,128)(2,1)} %shard_map.86.refs_0_), channel_id=1, source_target_pairs={{0,2},{1,3},{2,0},{3,1},{4,6},{5,7},{6,4},{7,5},{8,10},{9,11},{10,... | collective-permute-start | bytes 1572872 | tf_op jit(solution)/shard_map/ppermute | solution.py:406
  17.0 1.8 %collective-permute-done.8.refs_2_ = bf16[64,2048]{1,0:T(8,128)(2,1)S(1)} collective-permute-done((bf16[64,2048]{1,0:T(8,128)(2,1)}, bf16[64,2048]{1,0:T(8,128)(2,1)S(1)}, u32[]{:S(2)}, u32[]{:S(2)}) %collective-permute-start.8) | collective-permute-done | bytes 262176 | tf_op jit(solution)/shard_map/ppermute | solution.py:419
  18.8 2.0 %collective-permute-start.2 = (bf16[64,2048]{1,0:T(8,128)(2,1)S(1)}, bf16[64,2048]{1,0:T(8,128)(2,1)S(1)}, u32[]{:S(2)}, u32[]{:S(2)}) collective-permute-start(bf16[64,2048]{1,0:T(8,128)(2,1)S(1)} %collective-permute-done.refs_1_), channel_id=1, source_target_pairs={{0,8},{8,16},{16,24},{24,28},{28,20},{20,12},{12,4},{4,0},{1,9},{9... | collective-permute-start | bytes 786440 | tf_op jit(solution)/shard_map/ppermute | solution.py:418
  20.8 1.4 %collective-permute-done.9.refs_3_ = bf16[64,2048]{1,0:T(8,128)(2,1)S(1)} collective-permute-done((bf16[64,2048]{1,0:T(8,128)(2,1)S(1)}, bf16[64,2048]{1,0:T(8,128)(2,1)S(1)}, u32[]{:S(2)}, u32[]{:S(2)}) %collective-permute-start.9) | collective-permute-done | bytes 262176 | tf_op jit(solution)/shard_map/ppermute | solution.py:418
  22.2 2.1 %collective-permute-start.11 = (bf16[64,2048]{1,0:T(8,128)(2,1)S(1)}, bf16[64,2048]{1,0:T(8,128)(2,1)S(1)}, u32[]{:S(2)}, u32[]{:S(2)}) collective-permute-start(bf16[64,2048]{1,0:T(8,128)(2,1)S(1)} %collective-permute-done.9.refs_3_), channel_id=1, source_target_pairs={{0,8},{8,16},{16,24},{24,28},{28,20},{20,12},{12,4},{4,0},{1,9},{9... | collective-permute-start | bytes 786440 | tf_op jit(solution)/shard_map/ppermute | solution.py:418
  24.4 5.6 %collective-permute-done.10.refs_4_ = bf16[64,2048]{1,0:T(8,128)(2,1)S(1)} collective-permute-done((bf16[64,2048]{1,0:T(8,128)(2,1)S(1)}, bf16[64,2048]{1,0:T(8,128)(2,1)S(1)}, u32[]{:S(2)}, u32[]{:S(2)}) %collective-permute-start.10) | collective-permute-done | bytes 262176 | tf_op jit(solution)/shard_map/ppermute | solution.py:419
  30.0 2.0 %collective-permute-start.4 = (bf16[64,2048]{1,0:T(8,128)(2,1)S(1)}, bf16[64,2048]{1,0:T(8,128)(2,1)S(1)}, u32[]{:S(2)}, u32[]{:S(2)}) collective-permute-start(bf16[64,2048]{1,0:T(8,128)(2,1)S(1)} %collective-permute-done.2.refs_3_), channel_id=1, source_target_pairs={{0,8},{8,16},{16,24},{24,28},{28,20},{20,12},{12,4},{4,0},{1,9},{9... | collective-permute-start | bytes 786440 | tf_op jit(solution)/shard_map/ppermute | solution.py:418
  32.0 2.2 %copy-done = bf16[1024,2048]{1,0:T(8,128)(2,1)S(1)} copy-done((bf16[1024,2048]{1,0:T(8,128)(2,1)S(1)}, bf16[1024,2048]{1,0:T(8,128)(2,1)}, u32[]{:S(2)}) %copy-start) | copy-done | bytes 4194328
  34.2 1.1 %shard_map.85 = (bf16[1024,2048]{1,0:T(8,128)(2,1)S(1)}, bf16[1024,2048]{1,0:T(8,128)(2,1)S(1)}) custom-call(bf16[1024,2048]{1,0:T(8,128)(2,1)S(1)} %copy-done), custom_call_target="tpu_custom_call" | custom-call | tf_op jit(solution)/shard_map/pallas_call | solution.py:236
  35.3 1.6 %collective-permute-start.14 = (bf16[64,2048]{1,0:T(8,128)(2,1)S(1)}, bf16[64,2048]{1,0:T(8,128)(2,1)S(1)}, u32[]{:S(2)}, u32[]{:S(2)}) collective-permute-start(bf16[64,2048]{1,0:T(8,128)(2,1)S(1)} %collective-permute-done.11.refs_5_), channel_id=1, source_target_pairs={{0,8},{8,16},{16,24},{24,28},{28,20},{20,12},{12,4},{4,0},{1,9},{9... | collective-permute-start | bytes 786440 | tf_op jit(solution)/shard_map/ppermute | solution.py:425
  37.0 0.5 collective-permute-start.13
  37.4 3.8 %collective-permute-done.12.refs_6_ = bf16[64,2048]{1,0:T(8,128)(2,1)S(1)} collective-permute-done((bf16[64,2048]{1,0:T(8,128)(2,1)S(1)}, bf16[64,2048]{1,0:T(8,128)(2,1)S(1)}, u32[]{:S(2)}, u32[]{:S(2)}) %collective-permute-start.12) | collective-permute-done | bytes 262176 | tf_op jit(solution)/shard_map/ppermute | solution.py:419
  41.2 1.4 %shard_map.87 = (f32[2,128,1024]{2,1,0:T(8,128)S(1)}, f32[2,128,1024]{2,1,0:T(8,128)S(1)}, bf16[512,2048]{1,0:T(8,128)(2,1)S(1)}) custom-call(bf16[64,2048]{1,0:T(8,128)(2,1)S(1)} %copy-done.4, bf16[64,2048]{1,0:T(8,128)(2,1)S(1)} %collective-permute-done.7.refs_1_, bf16[64,2048]{1,0:T(8,128)(2,1)S(1)} %collective-permute-done.8.refs_2_, ...), custom_call_target="tpu_custom_call" | custom-call | tf_op jit(solution)/shard_map/pallas_call | solution.py:102
  42.7 1.4 %shard_map.88 = (f32[2,128,1024]{2,1,0:T(8,128)S(1)}, f32[2,128,1024]{2,1,0:T(8,128)S(1)}, bf16[512,2048]{1,0:T(8,128)(2,1)S(1)}) custom-call(bf16[64,2048]{1,0:T(8,128)(2,1)S(1)} %copy-done.5, bf16[64,2048]{1,0:T(8,128)(2,1)S(1)} %collective-permute-done.refs_1_, ...), custom_call_target="tpu_custom_call", output_to_operand_aliasing={{0}: (8, {}), {1}: (9, {})} | custom-call | tf_op jit(solution)/shard_map/pallas_call | solution.py:102
  44.2 0.7 %copy-done.1 = bf16[1024,2048]{1,0:T(8,128)(2,1)S(1)} copy-done((bf16[1024,2048]{1,0:T(8,128)(2,1)S(1)}, bf16[1024,2048]{1,0:T(8,128)(2,1)}, u32[]{:S(2)}) %copy-start.1) | copy-done | bytes 4194328
  44.8 1.3 %shard_map.89 = (f32[2,128,1024]{2,1,0:T(8,128)S(1)}, f32[2,128,1024]{2,1,0:T(8,128)S(1)}, bf16[512,2048]{1,0:T(8,128)(2,1)S(1)}) custom-call(bf16[512,2048]{1,0:T(8,128)(2,1)S(1)} %get-tuple-element.39.refs_0_, bf16[64,2048]{1,0:T(8,128)(2,1)S(1)} %collective-permute-done.14.refs_1_, bf16[1024,2048]{1,0:T(8,128)(2,1)S(1)} %copy-done.1), custom_call_target="tpu_custom_call", output_to_operand_aliasing={{2}: (0, {})} | custom-call | tf_op jit(solution)/shard_map/pallas_call | solution.py:123
  46.2 1.3 %shard_map.90 = (f32[2,128,1024]{2,1,0:T(8,128)S(1)}, f32[2,128,1024]{2,1,0:T(8,128)S(1)}, bf16[512,2048]{1,0:T(8,128)(2,1)S(1)}) custom-call(bf16[512,2048]{1,0:T(8,128)(2,1)S(1)} %get-tuple-element.38.refs_0_, bf16[64,2048]{1,0:T(8,128)(2,1)S(1)} %collective-permute-done.13.refs_1_, ...), custom_call_target="tpu_custom_call", output_to_operand_aliasing={{2}: (0, {}), {0}: (3, {}), {1}: (4, {})} | custom-call | tf_op jit(solution)/shard_map/pallas_call | solution.py:123
  47.5 0.5 collective-permute-start.19
  48.3 1.6 %collective-permute-start.18 = (s16[128,1024]{1,0:T(8,128)(2,1)S(1)}, s16[128,1024]{1,0:T(8,128)(2,1)S(1)}, u32[]{:S(2)}, u32[]{:S(2)}) collective-permute-start(s16[128,1024]{1,0:T(8,128)(2,1)S(1)} %shard_map.92), channel_id=1, source_target_pairs={{0,2},{1,3},{2,0},{3,1},{4,6},{5,7},{6,4},{7,5},{8,10},{9,11},{10,... | collective-permute-start | bytes 786440 | tf_op jit(solution)/shard_map/ppermute | solution.py:406
  49.9 0.3 collective-permute-done.15.refs_1_
  50.2 0.2 shard_map.91
  50.4 1.6 %collective-permute-start.16 = (s16[128,1024]{1,0:T(8,128)(2,1)S(1)}, s16[128,1024]{1,0:T(8,128)(2,1)S(1)}, u32[]{:S(2)}, u32[]{:S(2)}) collective-permute-start(s16[128,1024]{1,0:T(8,128)(2,1)S(1)} %shard_map.91), channel_id=1, source_target_pairs={{0,2},{1,3},{2,0},{3,1},{4,6},{5,7},{6,4},{7,5},{8,10},{9,11},{10,... | collective-permute-start | bytes 786440 | tf_op jit(solution)/shard_map/ppermute | solution.py:406
  51.9 0.9 %shard_map.95 = (bf16[1024,512]{1,0:T(8,128)(2,1)S(1)}, bf16[1024,512]{1,0:T(8,128)(2,1)S(1)}) custom-call(bf16[256,1024]{1,0:T(8,128)(2,1)S(1)} %copy-done.3, bf16[256,1024]{1,0:T(8,128)(2,1)S(1)} %collective-permute-done.6.refs_1_, bf16[256,1024]{1,0:T(8,128)(2,1)S(1)} %collective-permute-done.19.refs_2_, bf16[256,1024]{1,0:T(8,128)(2,1)S(1)} %collective-permute-done.20.refs_3_), custom_call_target="tpu_custom_call" | custom-call | tf_op jit(solution)/shard_map/pallas_call | solution.py:345
  52.8 6.2 %shard_map.96 = f32[1024,2048]{1,0:T(8,128)} custom-call(bf16[1024,512]{1,0:T(8,128)(2,1)S(1)} %get-tuple-element.56.center, bf16[1024,512]{1,0:T(8,128)(2,1)S(1)} %get-tuple-element.57.radius, bf16[512,2048]{1,0:T(8,128)(2,1)S(1)} %get-tuple-element.52.grad_c, bf16[512,2048]{1,0:T(8,128)(2,1)S(1)} %get-tuple-element.53.grad_r, ...), custom_call_target="tpu_custom_call" | custom-call | tf_op jit(solution)/shard_map/pallas_call | solution.py:379
  59.1 0.9 %shard_map.93 = (f32[128,1024]{1,0:T(8,128)}, f32[128,1024]{1,0:T(8,128)}) custom-call(f32[2,128,1024]{2,1,0:T(8,128)S(1)} %get-tuple-element.44.refs_0_, f32[2,128,1024]{2,1,0:T(8,128)S(1)} %collective-permute-done.17.refs_1_, s16[128,1024]{1,0:T(8,128)(2,1)S(1)} %collective-permute-done.18.refs_2_, s32[128,1024]{1,0:T(8,128)S(1)} %copy-done.2), custom_call_target="tpu_custom_call" | custom-call | tf_op jit(solution)/shard_map/pallas_call | solution.py:210
  60.0 2.6 %collective-permute-done.16.refs_2_ = s16[128,1024]{1,0:T(8,128)(2,1)S(1)} collective-permute-done((s16[128,1024]{1,0:T(8,128)(2,1)S(1)}, s16[128,1024]{1,0:T(8,128)(2,1)S(1)}, u32[]{:S(2)}, u32[]{:S(2)}) %collective-permute-start.16) | collective-permute-done | bytes 262176 | tf_op jit(solution)/shard_map/ppermute | solution.py:406
  62.6 0.9 %shard_map.94 = (f32[128,1024]{1,0:T(8,128)}, f32[128,1024]{1,0:T(8,128)}) custom-call(f32[2,128,1024]{2,1,0:T(8,128)S(1)} %get-tuple-element.42.refs_0_, f32[2,128,1024]{2,1,0:T(8,128)S(1)} %collective-permute-done.15.refs_1_, s16[128,1024]{1,0:T(8,128)(2,1)S(1)} %collective-permute-done.16.refs_2_, ...), custom_call_target="tpu_custom_call", output_to_operand_aliasing={{0}: (4, {}), {1}: (5, {})} | custom-call | tf_op jit(solution)/shard_map/pallas_call | solution.py:210
  (34 shorter events, 0.7 us)
Async XLA Ops:
  0.6 40.6 %copy-start.4 = (bf16[64,2048]{1,0:T(8,128)(2,1)S(1)}, bf16[64,2048]{1,0:T(8,128)(2,1)}, u32[]{:S(2)}) copy-start(bf16[64,2048]{1,0:T(8,128)(2,1)} %refs_0_.1) | copy-start | bytes 786436
  0.6 10.4 %collective-permute-start.7 = (bf16[64,2048]{1,0:T(8,128)(2,1)}, bf16[64,2048]{1,0:T(8,128)(2,1)S(1)}, u32[]{:S(2)}, u32[]{:S(2)}) collective-permute-start(bf16[64,2048]{1,0:T(8,128)(2,1)} %refs_0_.1), channel_id=1, source_target_pairs={{0,8},{8,16},{16,24},{24,28},{28,20},{20,12},{12,4},{4,0},{1,9},{9... | collective-permute-start | bytes 786440 | tf_op jit(solution)/shard_map/ppermute | solution.py:418
  3.7 9.4 %collective-permute-start.1 = (bf16[64,2048]{1,0:T(8,128)(2,1)}, bf16[64,2048]{1,0:T(8,128)(2,1)S(1)}, u32[]{:S(2)}, u32[]{:S(2)}) collective-permute-start(bf16[64,2048]{1,0:T(8,128)(2,1)} %refs_0_.2), channel_id=1, source_target_pairs={{8,0},{16,8},{24,16},{28,24},{20,28},{12,20},{4,12},{0,4},{9,1},{1... | collective-permute-start | bytes 786440 | tf_op jit(solution)/shard_map/ppermute | solution.py:419
  3.7 15.1 %collective-permute-start.8 = (bf16[64,2048]{1,0:T(8,128)(2,1)}, bf16[64,2048]{1,0:T(8,128)(2,1)S(1)}, u32[]{:S(2)}, u32[]{:S(2)}) collective-permute-start(bf16[64,2048]{1,0:T(8,128)(2,1)} %refs_0_.1), channel_id=1, source_target_pairs={{8,0},{16,8},{24,16},{28,24},{20,28},{12,20},{4,12},{0,4},{9,1},{1... | collective-permute-start | bytes 786440 | tf_op jit(solution)/shard_map/ppermute | solution.py:419
  5.7 13.1 %collective-permute-start = (bf16[64,2048]{1,0:T(8,128)(2,1)}, bf16[64,2048]{1,0:T(8,128)(2,1)S(1)}, u32[]{:S(2)}, u32[]{:S(2)}) collective-permute-start(bf16[64,2048]{1,0:T(8,128)(2,1)} %refs_0_.2), channel_id=1, source_target_pairs={{0,8},{8,16},{16,24},{24,28},{28,20},{20,12},{12,4},{4,0},{1,9},{9... | collective-permute-start | bytes 786440 | tf_op jit(solution)/shard_map/ppermute | solution.py:418
  11.0 11.2 %collective-permute-start.9 = (bf16[64,2048]{1,0:T(8,128)(2,1)S(1)}, bf16[64,2048]{1,0:T(8,128)(2,1)S(1)}, u32[]{:S(2)}, u32[]{:S(2)}) collective-permute-start(bf16[64,2048]{1,0:T(8,128)(2,1)S(1)} %collective-permute-done.7.refs_1_), channel_id=1, source_target_pairs={{0,8},{8,16},{16,24},{24,28},{28,20},{20,12},{12,4},{4,0},{1,9},{9... | collective-permute-start | bytes 786440 | tf_op jit(solution)/shard_map/ppermute | solution.py:418
  13.2 11.2 %collective-permute-start.3 = (bf16[64,2048]{1,0:T(8,128)(2,1)S(1)}, bf16[64,2048]{1,0:T(8,128)(2,1)S(1)}, u32[]{:S(2)}, u32[]{:S(2)}) collective-permute-start(bf16[64,2048]{1,0:T(8,128)(2,1)S(1)} %collective-permute-done.1.refs_2_), channel_id=1, source_target_pairs={{8,0},{16,8},{24,16},{28,24},{20,28},{12,20},{4,12},{0,4},{9,1},{1... | collective-permute-start | bytes 786440 | tf_op jit(solution)/shard_map/ppermute | solution.py:419
  13.2 29.5 %copy-start.5 = (bf16[64,2048]{1,0:T(8,128)(2,1)S(1)}, bf16[64,2048]{1,0:T(8,128)(2,1)}, u32[]{:S(2)}) copy-start(bf16[64,2048]{1,0:T(8,128)(2,1)} %refs_0_.2) | copy-start | bytes 786436
  15.0 22.4 %collective-permute-start.6 = (bf16[256,1024]{1,0:T(8,128)(2,1)}, bf16[256,1024]{1,0:T(8,128)(2,1)S(1)}, u32[]{:S(2)}, u32[]{:S(2)}) collective-permute-start(bf16[256,1024]{1,0:T(8,128)(2,1)} %shard_map.86.refs_0_), channel_id=1, source_target_pairs={{0,2},{1,3},{2,0},{3,1},{4,6},{5,7},{6,4},{7,5},{8,10},{9,11},{10,... | collective-permute-start | bytes 1572872 | tf_op jit(solution)/shard_map/ppermute | solution.py:406
  18.8 11.2 %collective-permute-start.10 = (bf16[64,2048]{1,0:T(8,128)(2,1)S(1)}, bf16[64,2048]{1,0:T(8,128)(2,1)S(1)}, u32[]{:S(2)}, u32[]{:S(2)}) collective-permute-start(bf16[64,2048]{1,0:T(8,128)(2,1)S(1)} %collective-permute-done.8.refs_2_), channel_id=1, source_target_pairs={{8,0},{16,8},{24,16},{28,24},{20,28},{12,20},{4,12},{0,4},{9,1},{1... | collective-permute-start | bytes 786440 | tf_op jit(solution)/shard_map/ppermute | solution.py:419
  18.8 11.2 %collective-permute-start.2 = (bf16[64,2048]{1,0:T(8,128)(2,1)S(1)}, bf16[64,2048]{1,0:T(8,128)(2,1)S(1)}, u32[]{:S(2)}, u32[]{:S(2)}) collective-permute-start(bf16[64,2048]{1,0:T(8,128)(2,1)S(1)} %collective-permute-done.refs_1_), channel_id=1, source_target_pairs={{0,8},{8,16},{16,24},{24,28},{28,20},{20,12},{12,4},{4,0},{1,9},{9... | collective-permute-start | bytes 786440 | tf_op jit(solution)/shard_map/ppermute | solution.py:418
  22.2 13.1 %collective-permute-start.11 = (bf16[64,2048]{1,0:T(8,128)(2,1)S(1)}, bf16[64,2048]{1,0:T(8,128)(2,1)S(1)}, u32[]{:S(2)}, u32[]{:S(2)}) collective-permute-start(bf16[64,2048]{1,0:T(8,128)(2,1)S(1)} %collective-permute-done.9.refs_3_), channel_id=1, source_target_pairs={{0,8},{8,16},{16,24},{24,28},{28,20},{20,12},{12,4},{4,0},{1,9},{9... | collective-permute-start | bytes 786440 | tf_op jit(solution)/shard_map/ppermute | solution.py:418
  24.4 12.6 %collective-permute-start.5 = (bf16[64,2048]{1,0:T(8,128)(2,1)S(1)}, bf16[64,2048]{1,0:T(8,128)(2,1)S(1)}, u32[]{:S(2)}, u32[]{:S(2)}) collective-permute-start(bf16[64,2048]{1,0:T(8,128)(2,1)S(1)} %collective-permute-done.3.refs_4_), channel_id=1, source_target_pairs={{8,0},{16,8},{24,16},{28,24},{20,28},{12,20},{4,12},{0,4},{9,1},{1... | collective-permute-start | bytes 786440 | tf_op jit(solution)/shard_map/ppermute | solution.py:419
  30.0 11.2 %collective-permute-start.12 = (bf16[64,2048]{1,0:T(8,128)(2,1)S(1)}, bf16[64,2048]{1,0:T(8,128)(2,1)S(1)}, u32[]{:S(2)}, u32[]{:S(2)}) collective-permute-start(bf16[64,2048]{1,0:T(8,128)(2,1)S(1)} %collective-permute-done.10.refs_4_), channel_id=1, source_target_pairs={{8,0},{16,8},{24,16},{28,24},{20,28},{12,20},{4,12},{0,4},{9,1},{1... | collective-permute-start | bytes 786440 | tf_op jit(solution)/shard_map/ppermute | solution.py:419
  30.0 12.7 %collective-permute-start.4 = (bf16[64,2048]{1,0:T(8,128)(2,1)S(1)}, bf16[64,2048]{1,0:T(8,128)(2,1)S(1)}, u32[]{:S(2)}, u32[]{:S(2)}) collective-permute-start(bf16[64,2048]{1,0:T(8,128)(2,1)S(1)} %collective-permute-done.2.refs_3_), channel_id=1, source_target_pairs={{0,8},{8,16},{16,24},{24,28},{28,20},{20,12},{12,4},{4,0},{1,9},{9... | collective-permute-start | bytes 786440 | tf_op jit(solution)/shard_map/ppermute | solution.py:418
  32.0 2.2 %copy-start = (bf16[1024,2048]{1,0:T(8,128)(2,1)S(1)}, bf16[1024,2048]{1,0:T(8,128)(2,1)}, u32[]{:S(2)}) copy-start(bf16[1024,2048]{1,0:T(8,128)(2,1)} %refs_2_) | copy-start | bytes 12582916
  35.3 8.9 %collective-permute-start.14 = (bf16[64,2048]{1,0:T(8,128)(2,1)S(1)}, bf16[64,2048]{1,0:T(8,128)(2,1)S(1)}, u32[]{:S(2)}, u32[]{:S(2)}) collective-permute-start(bf16[64,2048]{1,0:T(8,128)(2,1)S(1)} %collective-permute-done.11.refs_5_), channel_id=1, source_target_pairs={{0,8},{8,16},{16,24},{24,28},{28,20},{20,12},{12,4},{4,0},{1,9},{9... | collective-permute-start | bytes 786440 | tf_op jit(solution)/shard_map/ppermute | solution.py:425
  37.0 9.2 %collective-permute-start.13 = (bf16[64,2048]{1,0:T(8,128)(2,1)S(1)}, bf16[64,2048]{1,0:T(8,128)(2,1)S(1)}, u32[]{:S(2)}, u32[]{:S(2)}) collective-permute-start(bf16[64,2048]{1,0:T(8,128)(2,1)S(1)} %collective-permute-done.5.refs_6_), channel_id=1, source_target_pairs={{8,0},{16,8},{24,16},{28,24},{20,28},{12,20},{4,12},{0,4},{9,1},{1... | collective-permute-start | bytes 786440 | tf_op jit(solution)/shard_map/ppermute | solution.py:426
  42.7 2.2 %copy-start.1 = (bf16[1024,2048]{1,0:T(8,128)(2,1)S(1)}, bf16[1024,2048]{1,0:T(8,128)(2,1)}, u32[]{:S(2)}) copy-start(bf16[1024,2048]{1,0:T(8,128)(2,1)} %refs_2_) | copy-start | bytes 12582916
  44.1 4.0 %collective-permute-start.17 = (f32[2,128,1024]{2,1,0:T(8,128)S(1)}, f32[2,128,1024]{2,1,0:T(8,128)S(1)}, u32[]{:S(2)}, u32[]{:S(2)}) collective-permute-start(f32[2,128,1024]{2,1,0:T(8,128)S(1)} %get-tuple-element.45), channel_id=1, source_target_pairs={{0,1},{1,0},{2,3},{3,2},{4,5},{5,4},{6,7},{7,6},{8,9},{9,8},{10,11... | collective-permute-start | bytes 3145736 | tf_op jit(solution)/shard_map/ppermute | solution.py:403
  46.1 1.4 %copy-start.3 = (bf16[256,1024]{1,0:T(8,128)(2,1)S(1)}, bf16[256,1024]{1,0:T(8,128)(2,1)}, u32[]{:S(2)}) copy-start(bf16[256,1024]{1,0:T(8,128)(2,1)} %shard_map.86.refs_0_) | copy-start | bytes 1572868
  47.5 2.7 %collective-permute-start.15 = (f32[2,128,1024]{2,1,0:T(8,128)S(1)}, f32[2,128,1024]{2,1,0:T(8,128)S(1)}, u32[]{:S(2)}, u32[]{:S(2)}) collective-permute-start(f32[2,128,1024]{2,1,0:T(8,128)S(1)} %get-tuple-element.43), channel_id=1, source_target_pairs={{0,1},{1,0},{2,3},{3,2},{4,5},{5,4},{6,7},{7,6},{8,9},{9,8},{10,11... | collective-permute-start | bytes 3145736 | tf_op jit(solution)/shard_map/ppermute | solution.py:403
  47.5 4.4 %collective-permute-start.19 = (bf16[256,1024]{1,0:T(8,128)(2,1)S(1)}, bf16[256,1024]{1,0:T(8,128)(2,1)S(1)}, u32[]{:S(2)}, u32[]{:S(2)}) collective-permute-start(bf16[256,1024]{1,0:T(8,128)(2,1)S(1)} %copy-done.3), channel_id=1, source_target_pairs={{0,1},{1,0},{2,3},{3,2},{4,5},{5,4},{6,7},{7,6},{8,9},{9,8},{10,11... | collective-permute-start | bytes 1572872 | tf_op jit(solution)/shard_map/ppermute | solution.py:403
  48.0 3.9 %collective-permute-start.20 = (bf16[256,1024]{1,0:T(8,128)(2,1)S(1)}, bf16[256,1024]{1,0:T(8,128)(2,1)S(1)}, u32[]{:S(2)}, u32[]{:S(2)}) collective-permute-start(bf16[256,1024]{1,0:T(8,128)(2,1)S(1)} %collective-permute-done.6.refs_1_), channel_id=1, source_target_pairs={{0,1},{1,0},{2,3},{3,2},{4,5},{5,4},{6,7},{7,6},{8,9},{9,8},{10,11... | collective-permute-start | bytes 1572872 | tf_op jit(solution)/shard_map/ppermute | solution.py:403
  48.3 10.7 %collective-permute-start.18 = (s16[128,1024]{1,0:T(8,128)(2,1)S(1)}, s16[128,1024]{1,0:T(8,128)(2,1)S(1)}, u32[]{:S(2)}, u32[]{:S(2)}) collective-permute-start(s16[128,1024]{1,0:T(8,128)(2,1)S(1)} %shard_map.92), channel_id=1, source_target_pairs={{0,2},{1,3},{2,0},{3,1},{4,6},{5,7},{6,4},{7,5},{8,10},{9,11},{10,... | collective-permute-start | bytes 786440 | tf_op jit(solution)/shard_map/ppermute | solution.py:406
  50.4 12.3 %collective-permute-start.16 = (s16[128,1024]{1,0:T(8,128)(2,1)S(1)}, s16[128,1024]{1,0:T(8,128)(2,1)S(1)}, u32[]{:S(2)}, u32[]{:S(2)}) collective-permute-start(s16[128,1024]{1,0:T(8,128)(2,1)S(1)} %shard_map.91), channel_id=1, source_target_pairs={{0,2},{1,3},{2,0},{3,1},{4,6},{5,7},{6,4},{7,5},{8,10},{9,11},{10,... | collective-permute-start | bytes 786440 | tf_op jit(solution)/shard_map/ppermute | solution.py:406
  52.8 6.3 %copy-start.2 = (s32[128,1024]{1,0:T(8,128)S(1)}, s32[128,1024]{1,0:T(8,128)}, u32[]{:S(2)}) copy-start(s32[128,1024]{1,0:T(8,128)} %refs_3_.3) | copy-start | bytes 1572868
